TPU v7x, 32 devices: a whole 2x2x4 slice. The times are simulated.
32 devices in a mesh: dp: 16 (over z, y, x), tensor: 2 (over core).
Axes of the slice: x: 2, y: 2, z: 4, core: 2. Of those that a mesh axis runs over, the one named last changes fastest.
Arguments:
- tokens: bfloat16 [4096, 2048], P(('dp', 'tensor')), may hold values from -6 to 6
- cotangent: bfloat16 [4096, 2048], P(('dp', 'tensor')), may hold values from -6 to 6
- weight_qkv: bfloat16 [2048, 4096], P('dp', 'tensor'), may hold values from -0.125 to 0.125
- weight_out: bfloat16 [2048, 2048], P('tensor', 'dp'), may hold values from -1 to 1
- weight_gate_up: bfloat16 [2048, 12288], P('dp', 'tensor'), may hold values from -0.125 to 0.125
- weight_down: bfloat16 [6144, 2048], P('tensor', 'dp'), may hold values from -0.078125 to 0.078125
- norm_gains: bfloat16 [2, 2048], replicated, may hold values from 0.5 to 1.5
- head_gains: bfloat16 [2, 128], replicated, may hold values from 0.099609375 to 1.8984375
- first_qkv: float32 [2048, 4096], P('dp', 'tensor')
- second_qkv: float32 [2048, 4096], P('dp', 'tensor')
- first_out: float32 [2048, 2048], P('tensor', 'dp')
- second_out: float32 [2048, 2048], P('tensor', 'dp')
- first_gate_up: float32 [2048, 12288], P('dp', 'tensor')
- second_gate_up: float32 [2048, 12288], P('dp', 'tensor')
- first_down: float32 [6144, 2048], P('tensor', 'dp')
- second_down: float32 [6144, 2048], P('tensor', 'dp')
- first_norm: float32 [2, 2048], replicated
- second_norm: float32 [2, 2048], replicated
- first_head: float32 [2, 128], replicated
- second_head: float32 [2, 128], replicated
Outputs:
- output: bfloat16 [4096, 2048], P(('dp', 'tensor'))
- input_grad: float32 [4096, 2048], P(('dp', 'tensor'))
- grad_qkv: float32 [2048, 4096], P('dp', 'tensor')
- moment_one_qkv: float32 [2048, 4096], P('dp', 'tensor')
- moment_two_qkv: float32 [2048, 4096], P('dp', 'tensor')
- update_qkv: float32 [2048, 4096], P('dp', 'tensor')
- grad_out: float32 [2048, 2048], P('tensor', 'dp')
- moment_one_out: float32 [2048, 2048], P('tensor', 'dp')
- moment_two_out: float32 [2048, 2048], P('tensor', 'dp')
- update_out: float32 [2048, 2048], P('tensor', 'dp')
- grad_gate_up: float32 [2048, 12288], P('dp', 'tensor')
- moment_one_gate_up: float32 [2048, 12288], P('dp', 'tensor')
- moment_two_gate_up: float32 [2048, 12288], P('dp', 'tensor')
- update_gate_up: float32 [2048, 12288], P('dp', 'tensor')
- grad_down: float32 [6144, 2048], P('tensor', 'dp')
- moment_one_down: float32 [6144, 2048], P('tensor', 'dp')
- moment_two_down: float32 [6144, 2048], P('tensor', 'dp')
- update_down: float32 [6144, 2048], P('tensor', 'dp')
- grad_norm: float32 [2, 2048], replicated
- moment_one_norm: float32 [2, 2048], replicated
- moment_two_norm: float32 [2, 2048], replicated
- update_norm: float32 [2, 2048], replicated
- grad_head: float32 [2, 128], replicated
- moment_one_head: float32 [2, 128], replicated
- moment_two_head: float32 [2, 128], replicated
- update_head: float32 [2, 128], replicated
All inputs are finite; a program needn't handle non-finite values.
Results may differ from a plain program's by a relative error of at most 0.015.
Values may be sent and summed in bfloat16 or wider, within the bound.
No kernel may reach another device: no remote copies, remote signals or barrier semaphores. Data moves between devices by JAX's collectives and lax.ppermute only.
A program may use at most 256 MiB of HBM per device.

v0:
```python
import math

import jax
import jax.numpy as jnp
from jax import lax
from jax.sharding import PartitionSpec as P

HEAD_SIZE = 128
STEP = 10


norm_eps = 1e-06
rope_base = 1000000.0
beta_one = 0.9
beta_two = 0.95
adam_eps = 1e-08
learn_rate = 0.01
weight_decay = 0.1


def matmul(left, right):
    return jnp.dot(left, right, preferred_element_type=jnp.float32)


def matmul_left(left, right):
    return lax.dot_general(
        left, right, (((0,), (0,)), ((), ())), preferred_element_type=jnp.float32
    )


def matmul_right(left, right):
    return lax.dot_general(
        left, right, (((1,), (1,)), ((), ())), preferred_element_type=jnp.float32
    )


def rms_scale(values):
    return lax.rsqrt(jnp.mean(values * values, axis=-1, keepdims=True) + norm_eps)


def rope_tables(sequence_length, width):
    places = jnp.arange(sequence_length, dtype=jnp.float32)[:, None]
    index = jnp.arange(width // 2, dtype=jnp.float32)[None, :]
    angles = places * jnp.power(rope_base, -2.0 * index / width)
    return (jnp.cos(angles)[:, None, :], jnp.sin(angles)[:, None, :])


def rotary(values, cosine, sine_table):
    half_width = values.shape[-1] // 2
    first_half = values[..., :half_width]
    second_half = values[..., half_width:]
    return jnp.concatenate(
        [
            first_half * cosine - second_half * sine_table,
            second_half * cosine + first_half * sine_table,
        ],
        axis=-1,
    )


def rotary_back(upstream, cosine, sine_table):
    half_width = upstream.shape[-1] // 2
    first_half = upstream[..., :half_width]
    second_half = upstream[..., half_width:]
    return jnp.concatenate(
        [
            first_half * cosine + second_half * sine_table,
            second_half * cosine - first_half * sine_table,
        ],
        axis=-1,
    )


def norm_back(upstream, values, scale, gain):
    weighted = upstream * gain
    normed = values * scale
    grad_values = scale * (weighted - normed * jnp.mean(weighted * normed, axis=-1, keepdims=True))
    grad_gain = jnp.sum((upstream * normed).reshape(-1, values.shape[-1]), axis=0)
    return (grad_values, grad_gain)


def gather_rows(values):
    return lax.all_gather(values, "tensor", axis=0, tiled=True)


def sum_rows(values):
    return lax.psum_scatter(values, "tensor", scatter_dimension=0, tiled=True)


def attention_scores(q_rot, k_rot, causal, inv_root):
    scores = (
        jnp.einsum("qhgd,khd->hgqk", q_rot, k_rot, preferred_element_type=jnp.float32) * inv_root
    )
    return jnp.where(causal, scores, -jnp.inf)


def adamw_step(weight, gradient, old_first, old_second, step_value, decay):
    moment_one = beta_one * old_first + (1.0 - beta_one) * gradient
    moment_two = beta_two * old_second + (1.0 - beta_two) * gradient * gradient
    fix_one = 1.0 - jnp.power(beta_one, step_value)
    fix_two = 1.0 - jnp.power(beta_two, step_value)
    update = -learn_rate * (
        moment_one / fix_one / (jnp.sqrt(moment_two / fix_two) + adam_eps) + decay * weight
    )
    return (gradient, moment_one, moment_two, update)


def shards(
    tokens,
    cotangent,
    weight_qkv,
    weight_out,
    weight_gate_up,
    weight_down,
    norm_gains,
    head_gains,
    first_qkv,
    second_qkv,
    first_out,
    second_out,
    first_gate_up,
    second_gate_up,
    first_down,
    second_down,
    first_norm,
    second_norm,
    first_head,
    second_head,
):
    heads_q = weight_out.shape[0] // HEAD_SIZE
    heads_kv = (weight_qkv.shape[1] // HEAD_SIZE - heads_q) // 2
    query_group_width = heads_q // heads_kv
    hidden = weight_down.shape[0]
    query_columns = heads_q * HEAD_SIZE
    key_value_columns = heads_kv * HEAD_SIZE
    inv_root = 1.0 / math.sqrt(HEAD_SIZE)
    gain_rows = norm_gains.astype(jnp.float32)
    head_rows = head_gains.astype(jnp.float32)
    gathered_qkv, gathered_out = (
        lax.all_gather(weight_qkv, "dp", axis=0, tiled=True),
        lax.all_gather(weight_out, "dp", axis=1, tiled=True),
    )
    inputs = tokens.astype(jnp.float32)
    scale_one = rms_scale(inputs)
    normed_one = gather_rows((inputs * scale_one * gain_rows[0]).astype(jnp.bfloat16))
    sequence_length = normed_one.shape[0]
    projected_rows = matmul(normed_one, gathered_qkv)
    queries = projected_rows[:, :query_columns].reshape(sequence_length, heads_q, HEAD_SIZE)
    unrotated_keys = projected_rows[:, query_columns : query_columns + key_value_columns].reshape(
        sequence_length, heads_kv, HEAD_SIZE
    )
    values = (
        projected_rows[:, query_columns + key_value_columns :]
        .astype(jnp.bfloat16)
        .reshape(sequence_length, heads_kv, HEAD_SIZE)
    )
    cosine, sine_table = rope_tables(sequence_length, HEAD_SIZE)
    q_scale = rms_scale(queries)
    k_scale = rms_scale(unrotated_keys)
    q_rot = (
        rotary(queries * q_scale * head_rows[0], cosine, sine_table)
        .astype(jnp.bfloat16)
        .reshape(sequence_length, heads_kv, query_group_width, HEAD_SIZE)
    )
    k_rot = rotary(unrotated_keys * k_scale * head_rows[1], cosine, sine_table).astype(jnp.bfloat16)
    causal = jnp.arange(sequence_length)[:, None] >= jnp.arange(sequence_length)[None, :]
    scores = attention_scores(q_rot, k_rot, causal, inv_root)
    row_max = jnp.max(scores, axis=-1, keepdims=True)
    exp_terms = jnp.exp(scores - row_max)
    row_total = jnp.sum(exp_terms, axis=-1, keepdims=True)
    attn_probs = exp_terms / row_total
    log_total = row_max + jnp.log(row_total)
    attended = (
        jnp.einsum(
            "hgqk,khd->qhgd",
            attn_probs.astype(jnp.bfloat16),
            values,
            preferred_element_type=jnp.float32,
        )
        .reshape(sequence_length, query_columns)
        .astype(jnp.bfloat16)
    )
    middle = inputs + sum_rows(matmul(attended, gathered_out))
    gathered_gu, gathered_down = (
        lax.all_gather(weight_gate_up, "dp", axis=0, tiled=True),
        lax.all_gather(weight_down, "dp", axis=1, tiled=True),
    )
    scale_two = rms_scale(middle)
    normed_two = gather_rows((middle * scale_two * gain_rows[1]).astype(jnp.bfloat16))
    gate_up = matmul(normed_two, gathered_gu)
    gate_part = gate_up[:, :hidden]
    up_part = gate_up[:, hidden:]
    sigmoid_gate = jax.nn.sigmoid(gate_part)
    activation = (gate_part * sigmoid_gate * up_part).astype(jnp.bfloat16)
    output = (middle + sum_rows(matmul(activation, gathered_down))).astype(jnp.bfloat16)
    gathered_gu, gathered_down = (
        lax.all_gather(weight_gate_up, "dp", axis=0, tiled=True),
        lax.all_gather(weight_down, "dp", axis=1, tiled=True),
    )
    cotangent_all = gather_rows(cotangent)
    grad_down = matmul_left(activation, cotangent_all)
    grad_act = matmul_right(cotangent_all, gathered_down)
    grad_gate = grad_act * up_part * sigmoid_gate * (1.0 + gate_part * (1.0 - sigmoid_gate))
    grad_up = grad_act * gate_part * sigmoid_gate
    d_gate_up = jnp.concatenate([grad_gate, grad_up], axis=1).astype(jnp.bfloat16)
    grad_gate_up = matmul_left(normed_two, d_gate_up)
    grad_two = sum_rows(matmul_right(d_gate_up, gathered_gu))
    middle_part, gain_two_grad = norm_back(grad_two, middle, scale_two, gain_rows[1])
    grad_middle = cotangent.astype(jnp.float32) + middle_part
    gathered_qkv, gathered_out = (
        lax.all_gather(weight_qkv, "dp", axis=0, tiled=True),
        lax.all_gather(weight_out, "dp", axis=1, tiled=True),
    )
    d_branch = gather_rows(grad_middle.astype(jnp.bfloat16))
    grad_wout = matmul_left(attended, d_branch)
    d_attended = (
        matmul_right(d_branch, gathered_out)
        .astype(jnp.bfloat16)
        .reshape(sequence_length, heads_kv, query_group_width, HEAD_SIZE)
    )
    scores = attention_scores(q_rot, k_rot, causal, inv_root)
    attn_probs = jnp.where(causal, jnp.exp(scores - log_total), 0.0)
    grad_probs = jnp.einsum(
        "qhgd,khd->hgqk", d_attended, values, preferred_element_type=jnp.float32
    )
    row_delta = jnp.sum(attn_probs * grad_probs, axis=-1, keepdims=True)
    d_scores = (attn_probs * (grad_probs - row_delta) * inv_root).astype(jnp.bfloat16)
    grad_values = jnp.einsum(
        "hgqk,qhgd->khd",
        attn_probs.astype(jnp.bfloat16),
        d_attended,
        preferred_element_type=jnp.float32,
    )
    grad_queries = jnp.einsum(
        "hgqk,khd->qhgd", d_scores, k_rot, preferred_element_type=jnp.float32
    ).reshape(sequence_length, heads_q, HEAD_SIZE)
    grad_keys = jnp.einsum("hgqk,qhgd->khd", d_scores, q_rot, preferred_element_type=jnp.float32)
    raw_queries, q_gain_grad = norm_back(
        rotary_back(grad_queries, cosine, sine_table), queries, q_scale, head_rows[0]
    )
    raw_keys, k_gain_grad = norm_back(
        rotary_back(grad_keys, cosine, sine_table), unrotated_keys, k_scale, head_rows[1]
    )
    d_projected = jnp.concatenate(
        [
            raw_queries.reshape(sequence_length, query_columns),
            raw_keys.reshape(sequence_length, key_value_columns),
            grad_values.reshape(sequence_length, key_value_columns),
        ],
        axis=1,
    ).astype(jnp.bfloat16)
    grad_wqkv = matmul_left(normed_one, d_projected)
    grad_one = sum_rows(matmul_right(d_projected, gathered_qkv))
    input_part, gain_one_grad = norm_back(grad_one, inputs, scale_one, gain_rows[0])
    input_grad = grad_middle + input_part
    shard_qkv, shard_out, shard_gate_up, shard_down = (
        lax.psum_scatter(grad_wqkv, "dp", scatter_dimension=0, tiled=True),
        lax.psum_scatter(grad_wout, "dp", scatter_dimension=1, tiled=True),
        lax.psum_scatter(grad_gate_up, "dp", scatter_dimension=0, tiled=True),
        lax.psum_scatter(grad_down, "dp", scatter_dimension=1, tiled=True),
    )
    grad_norm, grad_head = lax.psum(
        (jnp.stack([gain_one_grad, gain_two_grad]), jnp.stack([q_gain_grad, k_gain_grad])),
        ("dp", "tensor"),
    )
    step_value = jnp.float32(STEP)
    qkv_new = adamw_step(
        weight_qkv.astype(jnp.float32), shard_qkv, first_qkv, second_qkv, step_value, weight_decay
    )
    out_new = adamw_step(
        weight_out.astype(jnp.float32), shard_out, first_out, second_out, step_value, weight_decay
    )
    gate_new = adamw_step(
        weight_gate_up.astype(jnp.float32),
        shard_gate_up,
        first_gate_up,
        second_gate_up,
        step_value,
        weight_decay,
    )
    down_new = adamw_step(
        weight_down.astype(jnp.float32),
        shard_down,
        first_down,
        second_down,
        step_value,
        weight_decay,
    )
    norm_new = adamw_step(gain_rows, grad_norm, first_norm, second_norm, step_value, 0.0)
    head_new = adamw_step(head_rows, grad_head, first_head, second_head, step_value, 0.0)
    return (
        output,
        input_grad,
        qkv_new[0],
        qkv_new[1],
        qkv_new[2],
        qkv_new[3],
        out_new[0],
        out_new[1],
        out_new[2],
        out_new[3],
        gate_new[0],
        gate_new[1],
        gate_new[2],
        gate_new[3],
        down_new[0],
        down_new[1],
        down_new[2],
        down_new[3],
        norm_new[0],
        norm_new[1],
        norm_new[2],
        norm_new[3],
        head_new[0],
        head_new[1],
        head_new[2],
        head_new[3],
    )


def solution(mesh):
    placed = (
        P(("dp", "tensor"), None),
        P(("dp", "tensor"), None),
        P("dp", "tensor"),
        P("tensor", "dp"),
        P("dp", "tensor"),
        P("tensor", "dp"),
        P(),
        P(),
        P("dp", "tensor"),
        P("dp", "tensor"),
        P("tensor", "dp"),
        P("tensor", "dp"),
        P("dp", "tensor"),
        P("dp", "tensor"),
        P("tensor", "dp"),
        P("tensor", "dp"),
        P(),
        P(),
        P(),
        P(),
    )
    return jax.shard_map(
        shards,
        mesh=mesh,
        in_specs=placed,
        out_specs=(
            P(("dp", "tensor"), None),
            P(("dp", "tensor"), None),
            P("dp", "tensor"),
            P("dp", "tensor"),
            P("dp", "tensor"),
            P("dp", "tensor"),
            P("tensor", "dp"),
            P("tensor", "dp"),
            P("tensor", "dp"),
            P("tensor", "dp"),
            P("dp", "tensor"),
            P("dp", "tensor"),
            P("dp", "tensor"),
            P("dp", "tensor"),
            P("tensor", "dp"),
            P("tensor", "dp"),
            P("tensor", "dp"),
            P("tensor", "dp"),
            P(),
            P(),
            P(),
            P(),
            P(),
            P(),
            P(),
            P(),
        ),
        check_vma=False,
    )
```

profile of v0, /device:TPU:0, one launch (start us, length us, event | category | flops | bytes accessed | tf_op | source)
XLA Modules:
  0.0 2490.9 jit_solution(1186766396436216296)
XLA Ops:
  9.3 2.0 fusion.20
  14.1 9.2 all-gather.9.cloned.1.call-done
  23.3 116.8 %all-gather.11.cloned.1.call-done = bf16[2048,2048]{1,0:T(8,128)(2,1)} async-done(((bf16[128,2048]{1,0:T(8,128)(2,1)}), bf16[2048,2048]{1,0:T(8,128)(2,1)}) %all-gather.11.cloned.1.call-update) | async-done | bytes 8388624 | tf_op jit(solution)/shard_map/all_gather | solution.py:140
  140.0 6.0 fusion.91
  152.9 1.7 reshape.221
  155.8 2.0 fusion.90
  159.7 70.5 %all-gather.13.cloned.1.call-done = bf16[1024,2048]{1,0:T(8,128)(2,1)} async-done(((bf16[1024,128]{1,0:T(8,128)(2,1)}), bf16[1024,2048]{1,0:T(8,128)(2,1)}) %all-gather.13.cloned.1.call-update) | async-done | bytes 4194320 | tf_op jit(solution)/shard_map/all_gather | solution.py:141
  230.2 4.8 fusion.92
  235.0 7.9 reduce-scatter.9.cloned.1.call-done
  248.5 7.8 all-gather.15.cloned.1.call-done
  256.3 275.4 %all-gather.17.cloned.1.call-done = bf16[2048,6144]{1,0:T(8,128)(2,1)} async-done(((bf16[128,6144]{1,0:T(8,128)(2,1)}), bf16[2048,6144]{1,0:T(8,128)(2,1)}) %all-gather.17.cloned.1.call-update) | async-done | bytes 25165840 | tf_op jit(solution)/shard_map/all_gather | solution.py:185
  531.8 14.0 fusion.93
  545.8 195.1 %all-gather.19.cloned.1.call-done = bf16[3072,2048]{1,0:T(8,128)(2,1)} async-done(((bf16[3072,128]{1,0:T(8,128)(2,1)}), bf16[3072,2048]{1,0:T(8,128)(2,1)}) %all-gather.19.cloned.1.call-update) | async-done | bytes 12582928 | tf_op jit(solution)/shard_map/all_gather | solution.py:186
  740.9 13.4 multiply_convert_fusion.1
  754.3 13.5 fusion.6
  767.8 7.9 reduce-scatter.13.cloned.1.call-done
  775.7 2.3 multiply_reduce_fusion
  782.5 1.5 copy.180
  785.2 4.9 all-gather.23.cloned.1.call-done
  790.1 4.6 convolution_convert_fusion.1
  794.7 2.1 copy.181
  796.8 3.0 fusion.58
  801.0 6.0 fusion.17
  807.0 6.0 fusion.16
  813.1 1.8 copy.177
  814.9 1.5 multiply_add_fusion.6
  818.4 2.3 fusion.88
  820.6 2.4 copy.179
  823.0 2.4 copy.178
  825.4 1.8 multiply_add_fusion.3
  831.6 7.3 fusion.56
  838.9 9.8 fusion.94
  848.8 6.1 fusion.95
  854.9 10.2 fusion.55
  866.4 11.9 fusion.96
  879.5 21.5 fusion.5
  902.1 2.4 reshape.227
  907.1 1.6 fusion.25
  908.8 43.9 %all-reduce = (f32[2,2048]{1,0:T(2,128)S(1)}, f32[2,128]{1,0:T(2,128)S(1)}) all-reduce(f32[2,2048]{1,0:T(2,128)S(1)} %pad_maximum_fusion.11, f32[2,128]{1,0:T(2,128)S(1)} %pad_maximum_fusion.12), channel_id=1, replica_groups=mesh['dp'=16,'tensor'=2] {'dp','tensor'}, use_global_device_ids=true, to_apply=%region_21.22 | all-reduce | flops 4352 | bytes 34816 | tf_op jit(solution)/shard_map/psum | solution.py:262
  954.0 3.2 fusion.24
  957.2 89.5 %reduce-scatter.19.cloned.1.call-done = f32[1024,128]{1,0:T(8,128)} async-done(((f32[1024,2048]{1,0:T(8,128)}), f32[1024,128]{1,0:T(8,128)}) %reduce-scatter.19.cloned.1.call-update) | async-done | bytes 524304 | tf_op jit(solution)/shard_map/reduce_scatter | solution.py:258
  1046.7 2.7 add_multiply_fusion.3
  1049.4 348.8 %reduce-scatter.17.cloned.1.call-done = f32[128,2048]{1,0:T(8,128)} async-done(((f32[2048,2048]{1,0:T(8,128)}), f32[128,2048]{1,0:T(8,128)}) %reduce-scatter.17.cloned.1.call-update) | async-done | bytes 1048592 | tf_op jit(solution)/shard_map/reduce_scatter | solution.py:257
  1398.2 3.8 add_multiply_fusion.2
  1402.0 369.9 %reduce-scatter.23.cloned.1.call-done = f32[3072,128]{1,0:T(8,128)} async-done(((f32[3072,2048]{1,0:T(8,128)}), f32[3072,128]{1,0:T(8,128)}) %reduce-scatter.23.cloned.1.call-update) | async-done | bytes 1572880 | tf_op jit(solution)/shard_map/reduce_scatter | solution.py:260
  1771.9 5.2 add_multiply_fusion.1
  1777.2 699.9 %reduce-scatter.21.cloned.1.call-done = f32[128,6144]{1,0:T(8,128)} async-done(((f32[2048,6144]{1,0:T(8,128)}), f32[128,6144]{1,0:T(8,128)}) %reduce-scatter.21.cloned.1.call-update) | async-done | bytes 3145744 | tf_op jit(solution)/shard_map/reduce_scatter | solution.py:259
  2477.1 6.9 add_multiply_fusion
  (231 shorter events, 40.8 us)
Async XLA Ops:
  7.2 5.7 copy-start.67
  7.2 16.0 all-gather.9.cloned.1.call-start
  8.1 138.0 %copy-start.40 = (f32[1,2048]{1,0:T(1,128)}, f32[1,2048]{1,0:T(1,128)S(1)}, u32[]{:S(2)}) copy-start(f32[1,2048]{1,0:T(1,128)S(1)} %get-tuple-element.76) | copy-start | bytes 24580
  9.3 136.8 %copy-start.60 = (f32[128]{0:T(128)}, f32[128]{0:T(128)S(1)}, u32[]{:S(2)}) copy-start(f32[128]{0:T(128)S(1)} %add_rsqrt_fusion.3) | copy-start | bytes 1540
  11.4 128.7 %all-gather.11.cloned.1.call-start = ((), (), s32[]{:S(2)}) async-start(), calls=%async_computation.9 | async-start | bytes 8912896 | tf_op jit(solution)/shard_map/all_gather | solution.py:140
  12.1 218.1 %all-gather.13.cloned.1.call-start = ((), (), s32[]{:S(2)}) async-start(), calls=%async_computation.10 | async-start | bytes 4456448 | tf_op jit(solution)/shard_map/all_gather | solution.py:141
  12.8 230.1 %reduce-scatter.9.cloned.1.call-start = ((), (), s32[]{:S(2)}) async-start(), calls=%async_computation.11 | async-start | bytes 3145728 | tf_op jit(solution)/shard_map/reduce_scatter | solution.py:87
  13.6 135.2 %copy-start.51 = (f32[128]{0:T(128)}, f32[128]{0:T(128)S(1)}, u32[]{:S(2)}) copy-start(f32[128]{0:T(128)S(1)} %get-tuple-element.78) | copy-start | bytes 1540
  13.6 141.1 %copy-start.53 = (f32[128]{0:T(128)}, f32[128]{0:T(128)S(1)}, u32[]{:S(2)}) copy-start(f32[128]{0:T(128)S(1)} %get-tuple-element.77) | copy-start | bytes 1540
  146.1 4.5 copy-start.10
  149.6 6.1 copy-start.22
  150.7 5.0 copy-start.12
  155.8 3.4 copy-start.34
  159.7 75.3 %copy-start.36 = (bf16[4,128,2,256]{3,1,2,0:T(8,128)(2,1)}, bf16[4,128,2,256]{3,1,2,0:T(8,128)(2,1)S(1)}, u32[]{:S(2)}) copy-start(bf16[4,128,2,256]{3,1,2,0:T(8,128)(2,1)S(1)} %convolution_convert_fusion) | copy-start | bytes 1572868
  234.9 8.0 copy-start
  235.0 21.3 all-gather.15.cloned.1.call-start
  245.9 285.8 %all-gather.17.cloned.1.call-start = ((), (), s32[]{:S(2)}) async-start(), calls=%async_computation.13 | async-start | bytes 26738688 | tf_op jit(solution)/shard_map/all_gather | solution.py:185
  246.5 299.3 %all-gather.21.cloned.1.call-start = ((), (), s32[]{:S(2)}) async-start(), calls=%async_computation.16 | async-start | bytes 1572864 | tf_op jit(solution)/shard_map/all_gather | solution.py:83
  247.3 493.6 %all-gather.19.cloned.1.call-start = ((), (), s32[]{:S(2)}) async-start(), calls=%async_computation.14 | async-start | bytes 13369344 | tf_op jit(solution)/shard_map/all_gather | solution.py:186
  248.0 527.7 %reduce-scatter.13.cloned.1.call-start = ((), (), s32[]{:S(2)}) async-start(), calls=%async_computation.17 | async-start | bytes 3145728 | tf_op jit(solution)/shard_map/reduce_scatter | solution.py:87
  767.8 22.4 all-gather.23.cloned.1.call-start
  779.7 127.4 %reduce-scatter.15.cloned.1.call-start = ((), (), s32[]{:S(2)}) async-start(), calls=%async_computation.19 | async-start | bytes 3145728 | tf_op jit(solution)/shard_map/reduce_scatter | solution.py:87
  794.7 5.1 copy-start.55
  813.1 3.3 copy-start.54
  838.8 115.2 %reduce-scatter.11.cloned.1.call-start = ((), (), s32[]{:S(2)}) async-start(), calls=%async_computation.15 | async-start | bytes 3145728 | tf_op jit(solution)/shard_map/reduce_scatter | solution.py:87
  848.7 198.0 %reduce-scatter.19.cloned.1.call-start = ((), (), s32[]{:S(2)}) async-start(), calls=%async_computation.21 | async-start | bytes 8912896 | tf_op jit(solution)/shard_map/reduce_scatter | solution.py:258
  854.9 543.4 %reduce-scatter.17.cloned.1.call-start = ((), (), s32[]{:S(2)}) async-start(), calls=%async_computation.20 | async-start | bytes 17825792 | tf_op jit(solution)/shard_map/reduce_scatter | solution.py:257
  865.2 906.8 %reduce-scatter.23.cloned.1.call-start = ((), (), s32[]{:S(2)}) async-start(), calls=%async_computation.23 | async-start | bytes 26738688 | tf_op jit(solution)/shard_map/reduce_scatter | solution.py:260
  878.3 1598.8 %reduce-scatter.21.cloned.1.call-start = ((), (), s32[]{:S(2)}) async-start(), calls=%async_computation.22 | async-start | bytes 53477376 | tf_op jit(solution)/shard_map/reduce_scatter | solution.py:259
  901.0 3.5 copy-start.19
  901.0 3.9 copy-start.17
  906.4 46.3 %copy-start.64 = (f32[2,128]{1,0:T(2,128)S(1)}, f32[2,128]{1,0:T(2,128)}, u32[]{:S(2)}) copy-start(f32[2,128]{1,0:T(2,128)} %param.39) | copy-start | bytes 3076
  906.4 46.3 %copy-start.65 = (f32[2,128]{1,0:T(2,128)S(1)}, f32[2,128]{1,0:T(2,128)}, u32[]{:S(2)}) copy-start(f32[2,128]{1,0:T(2,128)} %param.38) | copy-start | bytes 3076
  906.4 46.3 %copy-start.68 = (bf16[2,128]{1,0:T(2,128)(2,1)S(1)}, bf16[2,128]{1,0:T(2,128)(2,1)}, u32[]{:S(2)}) copy-start(bf16[2,128]{1,0:T(2,128)(2,1)} %param.27) | copy-start | bytes 1540
  906.4 46.9 %copy-start.42 = (bf16[2,2048]{1,0:T(2,128)(2,1)S(1)}, bf16[2,2048]{1,0:T(2,128)(2,1)}, u32[]{:S(2)}) copy-start(bf16[2,2048]{1,0:T(2,128)(2,1)} %param.26) | copy-start | bytes 24580
  906.4 46.9 %copy-start.47 = (f32[2,2048]{1,0:T(2,128)S(1)}, f32[2,2048]{1,0:T(2,128)}, u32[]{:S(2)}) copy-start(f32[2,2048]{1,0:T(2,128)} %param.37) | copy-start | bytes 49156
  906.4 46.9 %copy-start.48 = (f32[2,2048]{1,0:T(2,128)S(1)}, f32[2,2048]{1,0:T(2,128)}, u32[]{:S(2)}) copy-start(f32[2,2048]{1,0:T(2,128)} %param.36) | copy-start | bytes 49156
  906.4 47.6 %copy-start.6 = (f32[128,2048]{1,0:T(8,128)S(1)}, f32[128,2048]{1,0:T(8,128)}, u32[]{:S(2)}) copy-start(f32[128,2048]{1,0:T(8,128)} %reduce-scatter.13.cloned.1.call-done) | copy-start | bytes 3145732
  906.4 47.6 %copy-start.15 = (bf16[128,2048]{1,0:T(8,128)(2,1)S(1)}, bf16[128,2048]{1,0:T(8,128)(2,1)}, u32[]{:S(2)}) copy-start(bf16[128,2048]{1,0:T(8,128)(2,1)} %param.21) | copy-start | bytes 1572868
  906.4 47.6 %copy-start.59 = (f32[128]{0:T(128)S(1)}, f32[128]{0:T(128)}, u32[]{:S(2)}) copy-start(f32[128]{0:T(128)} %copy-done.57) | copy-start | bytes 1540
  906.4 47.6 %copy-start.63 = (f32[128]{0:T(128)S(1)}, f32[128]{0:T(128)}, u32[]{:S(2)}) copy-start(f32[128]{0:T(128)} %copy-done.62) | copy-start | bytes 1540
  952.7 4.5 copy-start.49
  952.7 4.5 copy-start.66
  954.0 92.7 %copy-start.33 = (bf16[1024,128]{1,0:T(8,128)(2,1)S(1)}, bf16[1024,128]{1,0:T(8,128)(2,1)}, u32[]{:S(2)}) copy-start(bf16[1024,128]{1,0:T(8,128)(2,1)} %param.23) | copy-start | bytes 786436
  957.2 441.0 %copy-start.26 = (bf16[128,2048]{1,0:T(8,128)(2,1)S(1)}, bf16[128,2048]{1,0:T(8,128)(2,1)}, u32[]{:S(2)}) copy-start(bf16[128,2048]{1,0:T(8,128)(2,1)} %param.22) | copy-start | bytes 1572868
  957.2 441.0 %copy-start.32 = (f32[128,2048]{1,0:T(8,128)S(1)}, f32[128,2048]{1,0:T(8,128)}, u32[]{:S(2)}) copy-start(f32[128,2048]{1,0:T(8,128)} %param.29) | copy-start | bytes 3145732
  1049.4 722.5 %copy-start.21 = (bf16[3072,128]{1,0:T(8,128)(2,1)S(1)}, bf16[3072,128]{1,0:T(8,128)(2,1)}, u32[]{:S(2)}) copy-start(bf16[3072,128]{1,0:T(8,128)(2,1)} %param.25) | copy-start | bytes 2359300
  1402.0 1075.0 %copy-start.9 = (bf16[128,6144]{1,0:T(8,128)(2,1)S(1)}, bf16[128,6144]{1,0:T(8,128)(2,1)}, u32[]{:S(2)}) copy-start(bf16[128,6144]{1,0:T(8,128)(2,1)} %param.24) | copy-start | bytes 4718596
  (37 other events, 67.4 us)
Sparse Core Ops, SparseCore 0:
  11.5 11.7 all-gather.8
  26.0 113.9 all-gather.10
  142.8 87.3 all-gather.12
  235.1 7.7 reduce-scatter.8
  246.1 10.2 all-gather.14
  259.3 272.3 all-gather.16
  533.4 7.2 all-gather.20
  543.7 197.1 all-gather.18
  767.9 7.7 reduce-scatter.12
  779.9 10.2 all-gather.22
  839.0 10.7 reduce-scatter.14
  852.5 10.8 reduce-scatter.10
  866.2 180.3 reduce-scatter.18
  1049.4 348.7 reduce-scatter.16
  1404.4 367.5 reduce-scatter.22
  1778.4 698.6 reduce-scatter.20
where the time goes:
time: 2500 us; the launch traced here: 2490 us
  waiting for transfers between devices  2210 us (88%)
  matrix products  142 us (6%)
  other arithmetic  46.6 us (2%)
  blocking collectives  43.9 us (2%)
  local copies, waits for them, and re-layouts  34.9 us (1%)
    reduce_scatter x1, waiting for transfers between devices, shards(): lax.psum_scatter(grad_gate_up, 'dp', scatter_dimension=0, tiled=True)  700 us
    reduce_scatter x1, waiting for transfers between devices, shards(): lax.psum_scatter(grad_down, 'dp', scatter_dimension=1, tiled=True)  370 us
    reduce_scatter x1, waiting for transfers between devices, shards(): lax.psum_scatter(grad_wqkv, 'dp', scatter_dimension=0, tiled=True)  349 us
    all_gather x1, waiting for transfers between devices, shards(): lax.all_gather(weight_gate_up, 'dp', axis=0, tiled=True)  275 us
    all_gather x1, waiting for transfers between devices, shards(): lax.all_gather(weight_down, 'dp', axis=1, tiled=True)  195 us
    all_gather x1, waiting for transfers between devices, shards(): lax.all_gather(weight_qkv, 'dp', axis=0, tiled=True)  117 us
    reduce_scatter x1, waiting for transfers between devices, shards(): lax.psum_scatter(grad_wout, 'dp', scatter_dimension=1, tiled=True)  89.5 us
    all_gather x1, waiting for transfers between devices, shards(): lax.all_gather(weight_out, 'dp', axis=1, tiled=True)  70.5 us
  transfers between devices with their start and end apart: 16, of which 13 were waited for; matrix products, arithmetic and copies ran while one was open for 5% of the time, Pallas kernels for 0%

commit v1 on v0

v1 whole, which is shorter than its diff:
```python
import functools
import math

import jax
import jax.numpy as jnp
from jax import lax
from jax.experimental import pallas as pl
from jax.experimental.pallas import tpu as pltpu
from jax.sharding import Mesh
from jax.sharding import PartitionSpec as P

HEAD_SIZE = 128
STEP = 10

norm_eps = 1e-06
rope_base = 1000000.0
beta_one = 0.9
beta_two = 0.95
adam_eps = 1e-08
learn_rate = 0.01
weight_decay = 0.1

bf16 = jnp.bfloat16
f32 = jnp.float32

SWAP = [(0, 1), (1, 0)]


def dot(left, right):
    return jnp.dot(left, right, preferred_element_type=f32)


def dot_tn(left, right):
    return lax.dot_general(left, right, (((0,), (0,)), ((), ())), preferred_element_type=f32)


def dot_nt(left, right):
    return lax.dot_general(left, right, (((1,), (1,)), ((), ())), preferred_element_type=f32)


def swap(value, axis):
    return lax.ppermute(value, axis, SWAP)


def rms_scale(values):
    return lax.rsqrt(jnp.mean(values * values, axis=-1, keepdims=True) + norm_eps)


def norm_back(upstream, values, scale, gain):
    weighted = upstream * gain
    normed = values * scale
    grad_values = scale * (weighted - normed * jnp.mean(weighted * normed, axis=-1, keepdims=True))
    grad_gain = jnp.sum((upstream * normed).reshape(-1, values.shape[-1]), axis=0)
    return (grad_values, grad_gain)


def adamw_step(weight, gradient, old_first, old_second, step_value, decay):
    moment_one = beta_one * old_first + (1.0 - beta_one) * gradient
    moment_two = beta_two * old_second + (1.0 - beta_two) * gradient * gradient
    fix_one = 1.0 - jnp.power(beta_one, step_value)
    fix_two = 1.0 - jnp.power(beta_two, step_value)
    update = -learn_rate * (
        moment_one / fix_one / (jnp.sqrt(moment_two / fix_two) + adam_eps) + decay * weight
    )
    return (gradient, moment_one, moment_two, update)


def vmem_call(kernel, out_shape, *args, name, flops=0):
    size = sum(math.prod(a.shape) * a.dtype.itemsize for a in (*args, *jax.tree.leaves(out_shape)))
    return pl.pallas_call(
        kernel,
        in_specs=[pl.BlockSpec(memory_space=pltpu.SMEM)] + [pl.BlockSpec(memory_space=pltpu.VMEM)] * (len(args) - 1),
        out_specs=jax.tree.map(lambda _: pl.BlockSpec(memory_space=pltpu.VMEM), out_shape),
        out_shape=out_shape,
        cost_estimate=pl.CostEstimate(flops=flops, bytes_accessed=size, transcendentals=0),
        compiler_params=pltpu.CompilerParams(vmem_limit_bytes=40 * 1024 * 1024),
        name=name,
    )(*args)


def shape(rows, columns, dtype):
    return jax.ShapeDtypeStruct((rows, columns), dtype)


def moves(place_ref, width):
    block = width // 16
    zh, x = place_ref[0], place_ref[1]
    for i in range(16):
        xr, zr, j = i // 8, (i // 4) % 2, i % 4
        natural = ((zr + zh - 2 * zr * zh) * 4 + j) * 2 + (xr + x - 2 * xr * x)
        yield pl.ds(i * block, block), pl.ds(pl.multiple_of(natural * block, block), block)


def start_kernel(place, tokens, cotangent, gains, own_tokens, normed, own_cotangent, own_gains):
    values = tokens[...].astype(f32)
    scale = rms_scale(values)
    for own, natural in moves(place, tokens.shape[1]):
        part = tokens[:, natural]
        gain = gains[:, natural]
        own_tokens[:, own] = part
        own_gains[:, own] = gain
        normed[:, own] = (part.astype(f32) * scale * gain[0:1]).astype(bf16)
        own_cotangent[:, own] = cotangent[:, natural]


def middle_kernel(place, base, near, far, tokens, gains, middle, normed):
    value = tokens[...].astype(f32) + (base[...] + near[...].astype(f32) + far[...].astype(f32))
    middle[...] = value
    normed[...] = (value * rms_scale(value) * gains[1:2]).astype(bf16)


def output_kernel(place, base, near, far, middle, output):
    for own, natural in moves(place, middle.shape[1]):
        added = base[:, own] + near[:, own].astype(f32) + far[:, own].astype(f32)
        output[:, natural] = (middle[:, own] + added).astype(bf16)


def back_two_kernel(place, base, near, far, middle, cotangent, gains, grad_middle, branch, dgain):
    upstream = base[...] + near[...].astype(f32) + far[...].astype(f32)
    value = middle[...]
    part, gain_part = norm_back(upstream, value, rms_scale(value), gains[1:2])
    grad = cotangent[...].astype(f32) + part
    grad_middle[...] = grad
    branch[...] = grad.astype(bf16)
    dgain[...] = gain_part[None]


def back_one_kernel(place, base, near, far, tokens, grad_middle, gains, dgain_two, input_grad, dgain):
    value = tokens[...].astype(f32)
    scale = rms_scale(value)
    upstream = base[...] + near[...].astype(f32) + far[...].astype(f32)
    normed = value * scale
    weighted = upstream * gains[0:1]
    mean = jnp.mean(weighted * normed, axis=-1, keepdims=True)
    for own, natural in moves(place, tokens.shape[1]):
        raised = base[:, own] + near[:, own].astype(f32) + far[:, own].astype(f32)
        unit = tokens[:, own].astype(f32) * scale
        grad = scale * (raised * gains[0:1, own] - unit * mean)
        input_grad[:, natural] = grad_middle[:, own] + grad
        dgain[0:1, natural] = jnp.sum(raised * unit, axis=0, keepdims=True)
        dgain[1:2, natural] = dgain_two[:, own]


def join_kernel(count, *refs):
    parts, out, done = refs[:count], refs[count], refs[count + 1]
    copies, at = [], 0
    for i, part in enumerate(parts):
        rows = part.shape[0]
        copies.append(pltpu.make_async_copy(part, out.at[pl.ds(at, rows)], done.at[i]))
        at += rows
    for copy in copies:
        copy.start()
    for copy in copies:
        copy.wait()


def join(*parts):
    total = shape(sum(p.shape[0] for p in parts), parts[0].shape[1], parts[0].dtype)
    size = 2 * total.shape[0] * total.shape[1] * total.dtype.itemsize
    return pl.pallas_call(
        functools.partial(join_kernel, len(parts)),
        in_specs=[pl.BlockSpec(memory_space=pl.ANY)] * len(parts),
        out_specs=pl.BlockSpec(memory_space=pltpu.VMEM),
        out_shape=total,
        scratch_shapes=[pltpu.SemaphoreType.DMA((len(parts),))],
        cost_estimate=pl.CostEstimate(flops=0, bytes_accessed=size, transcendentals=0),
        compiler_params=pltpu.CompilerParams(vmem_limit_bytes=16 * 1024 * 1024),
        name="join",
    )(*parts)


def gather_rows(value):
    over_zl = swap(value, "zl")
    over_y = swap(value, "y")
    over_both = swap(over_zl, "y")
    half = join(value, over_y, over_zl, over_both)
    return join(half, swap(half, "c"))


def sum_rows(left, right_t):
    half = left.shape[0] // 2
    rows = half // 4
    other = dot_nt(left[half:], right_t).astype(bf16)
    mine = dot_nt(left[:half], right_t) + swap(other, "c").astype(f32)
    block = lambda i: mine[i * rows : (i + 1) * rows]
    both = swap(block(3).astype(bf16), "y")
    near = swap(block(1).astype(bf16), "y")
    far = swap((block(2) + both.astype(f32)).astype(bf16), "zl")
    return block(0), near, far


def pack_attention_kernel(wide_q, wide_kv, qkv, out, packed):
    for j in range(4):
        packed[j, :, :wide_q] = qkv[:, j * wide_q : (j + 1) * wide_q]
        for part in range(2):
            at = 4 * (wide_q + part * wide_kv) + j * wide_kv
            to = wide_q + part * wide_kv
            packed[j, :, to : to + wide_kv] = qkv[:, at : at + wide_kv]
        turned = out[j * wide_q : (j + 1) * wide_q, :].astype(f32).T
        packed[j, :, wide_q + 2 * wide_kv :] = turned.astype(bf16)


def pack_attention(qkv, out, wide_q, wide_kv):
    depth = qkv.shape[0]
    packed = jax.ShapeDtypeStruct((4, depth, 2 * wide_q + 2 * wide_kv), bf16)
    return pl.pallas_call(
        functools.partial(pack_attention_kernel, wide_q, wide_kv),
        out_shape=packed,
        compiler_params=pltpu.CompilerParams(vmem_limit_bytes=40 * 1024 * 1024),
        name="pack_attention",
    )(qkv, out)


def pack_columns_kernel(first, second, packed):
    wide = first.shape[1]
    packed[0, :, :wide] = first[...]
    packed[0, :, wide:] = second[...]


def pack_columns(array, wide):
    depth = array.shape[0]
    return pl.pallas_call(
        pack_columns_kernel,
        grid=(4,),
        in_specs=[
            pl.BlockSpec((depth, wide), lambda j: (0, j)),
            pl.BlockSpec((depth, wide), lambda j: (0, j + 4)),
        ],
        out_specs=pl.BlockSpec((1, depth, 2 * wide), lambda j: (j, 0, 0)),
        out_shape=jax.ShapeDtypeStruct((4, depth, 2 * wide), bf16),
        compiler_params=pltpu.CompilerParams(vmem_limit_bytes=40 * 1024 * 1024),
        name="pack_columns",
    )(array, array)


def pack_turned_kernel(array, packed):
    packed[0] = array[...].astype(f32).T.astype(bf16)


def pack_turned(array, wide):
    depth = array.shape[1]
    return pl.pallas_call(
        pack_turned_kernel,
        grid=(4,),
        in_specs=[pl.BlockSpec((wide, depth), lambda j: (j, 0))],
        out_specs=pl.BlockSpec((1, depth, wide), lambda j: (j, 0, 0)),
        out_shape=jax.ShapeDtypeStruct((4, depth, wide), bf16),
        compiler_params=pltpu.CompilerParams(vmem_limit_bytes=40 * 1024 * 1024),
        name="pack_turned",
    )(array)


def exchange(pieces):
    return lax.all_to_all(pieces, ("zl", "y"), 0, 0, tiled=True)


def gather_weight(pieces, rest):
    mine = exchange(pieces)
    if rest > 1:
        mine = lax.all_gather(mine, "r", axis=1, tiled=True)
    mine = mine.reshape(-1, mine.shape[-1])
    far = swap(mine, "zh")
    return jnp.concatenate([mine, far, swap(mine, "x"), swap(far, "x")], axis=0)


def scatter_grad(left, right, rest):
    width = left.shape[1]
    over_x = swap(dot_tn(left[:, width // 2 :], right).astype(bf16), "x")
    near = dot_tn(left[:, : width // 2], right) + over_x.astype(f32)
    far = swap(near[width // 4 :].astype(bf16), "zh")
    mine = (near[: width // 4] + far.astype(f32)).astype(bf16)
    mine = mine.reshape(4, width // 16, -1)
    if rest > 1:
        mine = lax.psum_scatter(mine, "r", scatter_dimension=1, tiled=True)
    return exchange(mine)


fix_one = 1.0 - beta_one**STEP
fix_two = 1.0 - beta_two**STEP


def adam_store(refs, at, gradient):
    weight, first, second, grad_out, one_out, two_out, update_out = refs
    moment_one = beta_one * first[at] + (1.0 - beta_one) * gradient
    moment_two = beta_two * second[at] + (1.0 - beta_two) * gradient * gradient
    ratio = moment_one * (1.0 / fix_one) / (jnp.sqrt(moment_two * (1.0 / fix_two)) + adam_eps)
    grad_out[at] = gradient
    one_out[at] = moment_one
    two_out[at] = moment_two
    update_out[at] = -learn_rate * (ratio + weight_decay * weight[at].astype(f32))


def adam_qkv_kernel(wide_q, wide_kv, got, *refs):
    for j in range(4):
        at, to = 0, 0
        for wide in (wide_q, wide_kv, wide_kv):
            part = got[j, :, at : at + wide].astype(f32)
            adam_store(refs, (slice(None), slice(to + j * wide, to + (j + 1) * wide)), part)
            at += wide
            to += 4 * wide


def adam_columns_kernel(got, *refs):
    adam_store(refs, (slice(None), slice(None)), got[0].astype(f32))


def adam_turned_kernel(got, *refs):
    adam_store(refs, (slice(None), slice(None)), got[0].astype(f32).T)


def adam(kernel, grid, got, got_spec, spec, weight, first, second, name):
    out = jax.ShapeDtypeStruct(weight.shape, f32)
    size = math.prod(weight.shape) * 28
    return pl.pallas_call(
        kernel,
        grid=grid,
        in_specs=[got_spec, spec, spec, spec],
        out_specs=[spec] * 4,
        out_shape=[out] * 4,
        cost_estimate=pl.CostEstimate(flops=size // 2, bytes_accessed=size, transcendentals=0),
        compiler_params=pltpu.CompilerParams(vmem_limit_bytes=40 * 1024 * 1024),
        name=name,
    )(got, weight, first, second)


def adam_qkv(got, weight, first, second, wide_q, wide_kv):
    kernel = functools.partial(adam_qkv_kernel, wide_q, wide_kv)
    whole = lambda array: pl.BlockSpec(array.shape, lambda i: (0,) * array.ndim)
    return adam(kernel, (1,), got, whole(got), whole(weight), weight, first, second, "adam_qkv")


def adam_columns(got, weight, first, second, wide):
    depth, columns = weight.shape
    got_spec = pl.BlockSpec((1, depth, wide), lambda b: (b % 4, 0, b // 4))
    spec = pl.BlockSpec((depth, wide), lambda b: (0, b))
    grid = (columns // wide,)
    return adam(adam_columns_kernel, grid, got, got_spec, spec, weight, first, second, "adam_columns")


def adam_turned(got, weight, first, second, wide):
    depth = weight.shape[1]
    got_spec = pl.BlockSpec((1, depth, wide), lambda j: (j, 0, 0))
    spec = pl.BlockSpec((wide, depth), lambda j: (j, 0))
    return adam(adam_turned_kernel, (4,), got, got_spec, spec, weight, first, second, "adam_turned")


def rope(v, cosine, sine):
    return v * cosine + pltpu.roll(v, HEAD_SIZE // 2, 1) * sine


def rope_back(v, cosine, sine):
    return v * cosine - pltpu.roll(v, HEAD_SIZE // 2, 1) * sine


def head_norm(v, gain, cosine, sine):
    scale = rms_scale(v)
    return scale, rope(v * scale * gain, cosine, sine).astype(bf16)


def probabilities(q_rot, k_rot, shift):
    length = q_rot.shape[0]
    scores = dot_nt(q_rot, k_rot) * (1.0 / math.sqrt(HEAD_SIZE))
    rows = lax.broadcasted_iota(jnp.int32, (length, length), 0)
    cols = lax.broadcasted_iota(jnp.int32, (length, length), 1)
    place_q = jnp.where(rows >= length - shift, rows + shift - length, rows + shift)
    place_k = jnp.where(cols >= length - shift, cols + shift - length, cols + shift)
    scores = jnp.where(place_q >= place_k, scores, -jnp.inf)
    terms = jnp.exp(scores - jnp.max(scores, axis=-1, keepdims=True))
    return terms / jnp.sum(terms, axis=-1, keepdims=True)


def attend_kernel(heads_q, heads_kv, shift_ref, proj_ref, cos_ref, sin_ref, gain_ref, out_ref):
    half, columns = proj_ref.shape[2:]
    cosine, sine = cos_ref[...], sin_ref[...]
    shift = shift_ref[0]
    group = heads_q // heads_kv

    def column(i):
        return proj_ref[:, 0, :, i * HEAD_SIZE : (i + 1) * HEAD_SIZE].reshape(2 * half, HEAD_SIZE)

    for kv in range(heads_kv):
        _, k_rot = head_norm(column(heads_q + kv), gain_ref[1:2, :], cosine, sine)
        values = column(heads_q + heads_kv + kv).astype(bf16)
        for h in range(kv * group, (kv + 1) * group):
            _, q_rot = head_norm(column(h), gain_ref[0:1, :], cosine, sine)
            probs = probabilities(q_rot, k_rot, shift)
            out = dot(probs.astype(bf16), values).astype(bf16)
            out_ref[:, 0, :, h * HEAD_SIZE : (h + 1) * HEAD_SIZE] = out.reshape(2, half, HEAD_SIZE)


def attend_back_kernel(
    heads_q, heads_kv, shift_ref, proj_ref, datt_ref, cos_ref, sin_ref, gain_ref, out_ref, dgain_ref
):
    half, columns = proj_ref.shape[2:]
    cosine, sine = cos_ref[...], sin_ref[...]
    shift = shift_ref[0]
    group = heads_q // heads_kv
    inv_root = 1.0 / math.sqrt(HEAD_SIZE)

    @pl.when(pl.program_id(0) == 0)
    def _():
        dgain_ref[...] = jnp.zeros_like(dgain_ref)

    def column(ref, i):
        return ref[:, 0, :, i * HEAD_SIZE : (i + 1) * HEAD_SIZE].reshape(2 * half, HEAD_SIZE)

    def store(i, value):
        value = value.astype(bf16).reshape(2, half, HEAD_SIZE)
        out_ref[:, 0, :, i * HEAD_SIZE : (i + 1) * HEAD_SIZE] = value

    q_gain, k_gain = gain_ref[0:1, :], gain_ref[1:2, :]
    dgain_q = jnp.zeros((1, HEAD_SIZE), f32)
    dgain_k = jnp.zeros((1, HEAD_SIZE), f32)
    for kv in range(heads_kv):
        key = column(proj_ref, heads_q + kv)
        k_scale, k_rot = head_norm(key, k_gain, cosine, sine)
        values = column(proj_ref, heads_q + heads_kv + kv).astype(bf16)
        grad_values = jnp.zeros((2 * half, HEAD_SIZE), f32)
        grad_keys = jnp.zeros((2 * half, HEAD_SIZE), f32)
        for h in range(kv * group, (kv + 1) * group):
            query = column(proj_ref, h)
            d_att = column(datt_ref, h)
            q_scale, q_rot = head_norm(query, q_gain, cosine, sine)
            probs = probabilities(q_rot, k_rot, shift)
            grad_probs = dot_nt(d_att, values)
            row_delta = jnp.sum(probs * grad_probs, axis=-1, keepdims=True)
            d_scores = (probs * (grad_probs - row_delta) * inv_root).astype(bf16)
            grad_values += dot_tn(probs.astype(bf16), d_att)
            grad_keys += dot_tn(d_scores, q_rot)
            upstream = rope_back(dot(d_scores, k_rot), cosine, sine)
            raw, gain_part = norm_back(upstream, query, q_scale, q_gain)
            dgain_q += gain_part[None]
            store(h, raw)
        raw, gain_part = norm_back(rope_back(grad_keys, cosine, sine), key, k_scale, k_gain)
        dgain_k += gain_part[None]
        store(heads_q + kv, raw)
        store(heads_q + heads_kv + kv, grad_values)
    dgain_ref[0:1, :] += dgain_q
    dgain_ref[1:2, :] += dgain_k


def block_spec(half, columns):
    return pl.BlockSpec((2, 1, half, columns), lambda s: (0, s, 0, 0))


def whole_spec(array):
    return pl.BlockSpec(array.shape, lambda s: (0,) * array.ndim)


def attend(proj, shift, cosine, sine, gains, heads_q, heads_kv):
    _, seqs, half, columns = proj.shape
    return pl.pallas_call(
        functools.partial(attend_kernel, heads_q, heads_kv),
        grid=(seqs,),
        in_specs=[
            pl.BlockSpec(memory_space=pltpu.SMEM),
            block_spec(half, columns),
            whole_spec(cosine),
            whole_spec(sine),
            whole_spec(gains),
        ],
        out_specs=block_spec(half, heads_q * HEAD_SIZE),
        out_shape=jax.ShapeDtypeStruct((2, seqs, half, heads_q * HEAD_SIZE), bf16),
        compiler_params=pltpu.CompilerParams(vmem_limit_bytes=32 * 1024 * 1024),
        name="attend",
    )(shift, proj, cosine, sine, gains)


def attend_back(proj, d_att, shift, cosine, sine, gains, heads_q, heads_kv):
    _, seqs, half, columns = proj.shape
    return pl.pallas_call(
        functools.partial(attend_back_kernel, heads_q, heads_kv),
        grid=(seqs,),
        in_specs=[
            pl.BlockSpec(memory_space=pltpu.SMEM),
            block_spec(half, columns),
            block_spec(half, heads_q * HEAD_SIZE),
            whole_spec(cosine),
            whole_spec(sine),
            whole_spec(gains),
        ],
        out_specs=[block_spec(half, columns), pl.BlockSpec((2, HEAD_SIZE), lambda s: (0, 0))],
        out_shape=[
            jax.ShapeDtypeStruct((2, seqs, half, columns), bf16),
            jax.ShapeDtypeStruct((2, HEAD_SIZE), f32),
        ],
        compiler_params=pltpu.CompilerParams(vmem_limit_bytes=32 * 1024 * 1024),
        name="attend_back",
    )(shift, proj, d_att, cosine, sine, gains)


def shards(
    rest,
    tokens,
    cotangent,
    weight_qkv,
    weight_out,
    weight_gate_up,
    weight_down,
    norm_gains,
    head_gains,
    first_qkv,
    second_qkv,
    first_out,
    second_out,
    first_gate_up,
    second_gate_up,
    first_down,
    second_down,
    first_norm,
    second_norm,
    first_head,
    second_head,
):
    heads_q = weight_out.shape[0] // HEAD_SIZE // 4
    heads_kv = (weight_qkv.shape[1] // HEAD_SIZE - 4 * heads_q) // 2 // 4
    hidden = weight_down.shape[0] // 4
    wide_q, wide_kv = heads_q * HEAD_SIZE, heads_kv * HEAD_SIZE
    wide_qkv = wide_q + 2 * wide_kv
    half, width = tokens.shape
    head_rows = head_gains.astype(f32)
    place = jnp.stack([lax.axis_index("zh"), lax.axis_index("x")]).astype(jnp.int32)

    inputs, normed_own, own_cotangent, own_gains = vmem_call(
        start_kernel,
        [shape(half, width, bf16)] * 3 + [shape(2, width, f32)],
        place, tokens, cotangent, norm_gains.astype(f32),
        name="start",
    )
    attention = gather_weight(pack_attention(weight_qkv, weight_out, wide_q, wide_kv), rest)
    own_qkv, own_out = attention[:, :wide_qkv], attention[:, wide_qkv:]
    normed_one = gather_rows(normed_own)
    own_gate_up = gather_weight(pack_columns(weight_gate_up, hidden), rest)
    own_down = gather_weight(pack_turned(weight_down, hidden), rest)
    cotangent_all = gather_rows(own_cotangent)

    core = lax.axis_index("c")
    shift = (core * half).astype(jnp.int32)
    places = (jnp.arange(2 * half) + shift) % (2 * half)
    index = jnp.arange(HEAD_SIZE // 2, dtype=f32)[None, :]
    angles = places.astype(f32)[:, None] * jnp.power(rope_base, -2.0 * index / HEAD_SIZE)
    cosine = jnp.concatenate([jnp.cos(angles)] * 2, axis=1)
    sine = jnp.concatenate([-jnp.sin(angles), jnp.sin(angles)], axis=1)
    shift = shift.reshape(1)

    projected = dot(normed_one, own_qkv)
    projected = projected.reshape(2, 4, half, wide_qkv)
    attended = attend(projected, shift, cosine, sine, head_rows, heads_q, heads_kv)
    attended = attended.reshape(-1, wide_q)
    middle, normed_own = vmem_call(
        middle_kernel,
        [shape(half, width, f32), shape(half, width, bf16)],
        place, *sum_rows(attended, own_out), inputs, own_gains,
        name="middle",
    )

    normed_two = gather_rows(normed_own)
    gate_up = dot(normed_two, own_gate_up)
    gate, up = gate_up[:, :hidden], gate_up[:, hidden:]
    sigmoid_gate = jax.nn.sigmoid(gate)
    activation = (gate * sigmoid_gate * up).astype(bf16)
    output = vmem_call(
        output_kernel,
        shape(half, width, bf16),
        place, *sum_rows(activation, own_down), middle,
        name="output",
    )

    grad_act = dot(cotangent_all, own_down)
    grad_gate = grad_act * up * sigmoid_gate * (1.0 + gate * (1.0 - sigmoid_gate))
    grad_up = grad_act * gate * sigmoid_gate
    d_gate_up = jnp.concatenate([grad_gate, grad_up], axis=1).astype(bf16)
    grad_middle, branch_own, gain_two_grad = vmem_call(
        back_two_kernel,
        [shape(half, width, f32), shape(half, width, bf16), shape(1, width, f32)],
        place, *sum_rows(d_gate_up, own_gate_up), middle, own_cotangent, own_gains,
        name="back_two",
    )
    d_branch = gather_rows(branch_own)
    grad_down = scatter_grad(cotangent_all, activation, rest)
    grad_gate_up = scatter_grad(normed_two, d_gate_up, rest)

    d_attended = dot(d_branch, own_out).astype(bf16)
    grad_out = scatter_grad(d_branch, attended, rest)
    d_projected, head_grad = attend_back(
        projected,
        d_attended.reshape(2, 4, half, wide_q),
        shift,
        cosine,
        sine,
        head_rows,
        heads_q,
        heads_kv,
    )
    d_projected = d_projected.reshape(-1, wide_qkv)
    input_grad, gain_grads = vmem_call(
        back_one_kernel,
        [shape(half, width, f32), shape(2, width, f32)],
        place, *sum_rows(d_projected, own_qkv), inputs, grad_middle, own_gains, gain_two_grad,
        name="back_one",
    )
    grad_qkv = scatter_grad(normed_one, d_projected, rest)

    sums = jnp.concatenate([gain_grads, head_grad], axis=1)
    for axis in ("c", "x", "y", "zl", "zh"):
        sums = sums + swap(sums, axis)
    if rest > 1:
        sums = lax.psum(sums, "r")
    grad_norm, grad_head = sums[:, :-HEAD_SIZE], sums[:, -HEAD_SIZE:]

    step_value = f32(STEP)

    def step(weight, gradient, first, second):
        return adamw_step(weight.astype(f32), gradient, first, second, step_value, 0.0)

    return (
        output,
        input_grad,
        *adam_qkv(grad_qkv, weight_qkv, first_qkv, second_qkv, wide_q, wide_kv),
        *adam_turned(grad_out, weight_out, first_out, second_out, wide_q),
        *adam_columns(grad_gate_up, weight_gate_up, first_gate_up, second_gate_up, hidden),
        *adam_turned(grad_down, weight_down, first_down, second_down, hidden),
        *step(norm_gains, grad_norm, first_norm, second_norm),
        *step(head_gains, grad_head, first_head, second_head),
    )


def solution(mesh):
    rest = mesh.shape["dp"] // 16
    names = ("zh", "zl", "y", "x", "r", "c")
    cut = Mesh(mesh.devices.reshape(2, 2, 2, 2, rest, 2), names)
    dp = names[:-1]
    rows, tall, wide, copied = P(names, None), P(dp, "c"), P("c", dp), P()
    placed = (rows, rows, tall, wide, tall, wide, copied, copied)
    placed += (tall, tall, wide, wide, tall, tall, wide, wide) + (copied,) * 4
    given = (rows, rows) + (tall,) * 4 + (wide,) * 4 + (tall,) * 4 + (wide,) * 4 + (copied,) * 8
    return jax.shard_map(
        functools.partial(shards, rest),
        mesh=cut,
        in_specs=placed,
        out_specs=given,
        check_vma=False,
    )
```

time: 2500 us -> 678 us (0.27)
  waiting for transfers between devices: 2210 us -> 389 us
  starting transfers between devices: 1.54 us -> 93 us
  Pallas kernels: 0 us -> 64.3 us
  matrix products: 142 us -> 89.6 us
  blocking collectives: 43.9 us -> 0 us
  other arithmetic: 46.6 us -> 15.1 us
    reduce_scatter x8 -> x0, waiting for transfers between devices: 1520 us -> none  [the longest x1 700 us: shards(): lax.psum_scatter(grad_gate_up, 'dp', scatter_dimension=0, tiled=True)]
    all_gather x8 -> x0, waiting for transfers between devices: 680 us -> none  [the longest x1 275 us: shards(): lax.all_gather(weight_gate_up, 'dp', axis=0, tiled=True)]
    ppermute x0 -> x54, waiting for transfers between devices: none -> 374 us  [swap(): return lax.ppermute(value, axis, SWAP)]
    pallas_call x0 -> x22, Pallas kernels: none -> 64.3 us  [the longest x8 18.3 us: join(): pl.pallas_call(functools.partial(join_kernel, len(parts)), in_specs=[pl.B...]
    ppermute x0 -> x54, starting transfers between devices: none -> 63.5 us  [swap(): return lax.ppermute(value, axis, SWAP)]
    dot_general x18 -> x20, matrix products: 142 us -> 89.6 us  [the longest x8 39.4 us: dot_nt(): lax.dot_general(left, right, (((1,), (1,)), ((), ())), preferred_element_...]
    psum x1 -> x0, blocking collectives: 43.9 us -> none  [shards(): lax.psum((jnp.stack([gain_one_grad, gain_two_grad]), jnp.stack([q_gain_gr...]
    all_to_all x0 -> x7, starting transfers between devices: none -> 29.5 us  [exchange(): return lax.all_to_all(pieces, ('zl', 'y'), 0, 0, tiled=True)]
  transfers between devices with their start and end apart: 16 -> 61, of which waited for: 13 -> 34; matrix products, arithmetic and copies ran while one was open for 5% -> 13% of each run, Pallas kernels for 0% -> 8%
where the time goes in v1:
time: 678 us; the launch traced here: 670 us
  waiting for transfers between devices  389 us (57%)
  starting transfers between devices  93 us (14%)
  matrix products  89.6 us (13%)
  Pallas kernels  64.3 us (9%)
  local copies, waits for them, and re-layouts  16.2 us (2%)
  other arithmetic  15.1 us (2%)
    ppermute x54, waiting for transfers between devices, swap(): return lax.ppermute(value, axis, SWAP)  374 us
    ppermute x54, starting transfers between devices, swap(): return lax.ppermute(value, axis, SWAP)  63.5 us
    dot_general x8, matrix products, dot_nt(): lax.dot_general(left, right, (((1,), (1,)), ((), ())), preferred_element_...  39.4 us
    all_to_all x7, starting transfers between devices, exchange(): return lax.all_to_all(pieces, ('zl', 'y'), 0, 0, tiled=True)  29.5 us
    dot_general x8, matrix products, dot_tn(): lax.dot_general(left, right, (((0,), (0,)), ((), ())), preferred_element_...  28 us
    dot_general x4, matrix products, dot(): return jnp.dot(left, right, preferred_element_type=f32)  22.3 us
    pallas_call x8, Pallas kernels, join(): pl.pallas_call(functools.partial(join_kernel, len(parts)), in_specs=[pl.B...  18.3 us
    all_to_all x7, waiting for transfers between devices, exchange(): return lax.all_to_all(pieces, ('zl', 'y'), 0, 0, tiled=True)  15.4 us
  transfers between devices with their start and end apart: 61, of which 34 were waited for; matrix products, arithmetic and copies ran while one was open for 13% of the time, Pallas kernels for 8%

profile of v1, /device:TPU:0, one launch (start us, length us, event | category | flops | bytes accessed | tf_op | source)
XLA Modules:
  0.0 669.7 jit_solution(15089999254415486864)
XLA Ops:
  3.7 5.4 all-to-all-start
  15.2 16.4 %collective-permute-done.1.refs_2_ = bf16[128,2048]{1,0:T(8,128)(2,1)S(1)} collective-permute-done((bf16[128,2048]{1,0:T(8,128)(2,1)S(1)}, bf16[128,2048]{1,0:T(8,128)(2,1)S(1)}, u32[]{:S(2)}, u32[]{:S(2)}) %collective-permute-start.1) | collective-permute-done | bytes 524320 | tf_op jit(solution)/shard_map/ppermute | solution.py:42
  35.8 8.8 %collective-permute-done.2.refs_3_ = bf16[128,2048]{1,0:T(8,128)(2,1)S(1)} collective-permute-done((bf16[128,2048]{1,0:T(8,128)(2,1)S(1)}, bf16[128,2048]{1,0:T(8,128)(2,1)S(1)}, u32[]{:S(2)}, u32[]{:S(2)}) %collective-permute-start.2) | collective-permute-done | bytes 524320 | tf_op jit(solution)/shard_map/ppermute | solution.py:42
  47.7 21.5 %collective-permute-done.4 = bf16[512,768]{1,0:T(8,128)(2,1)S(1)} collective-permute-done((bf16[512,768]{1,0:T(8,128)(2,1)}, bf16[512,768]{1,0:T(8,128)(2,1)S(1)}, u32[]{:S(2)}, u32[]{:S(2)}) %collective-permute-start.4) | collective-permute-done | bytes 786464 | tf_op jit(solution)/shard_map/ppermute | solution.py:42
  71.5 17.3 %collective-permute-done.6 = bf16[512,768]{1,0:T(8,128)(2,1)} collective-permute-done((bf16[512,768]{1,0:T(8,128)(2,1)S(1)}, bf16[512,768]{1,0:T(8,128)(2,1)}, u32[]{:S(2)}, u32[]{:S(2)}) %collective-permute-start.6) | collective-permute-done | bytes 786464 | tf_op jit(solution)/shard_map/ppermute | solution.py:42
  97.9 6.0 attend.1
  108.7 4.4 all-to-all-start.1
  117.7 27.1 %collective-permute-done.9 = bf16[128,2048]{1,0:T(8,128)(2,1)S(1)} collective-permute-done((bf16[128,2048]{1,0:T(8,128)(2,1)S(1)}, bf16[128,2048]{1,0:T(8,128)(2,1)S(1)}, u32[]{:S(2)}, u32[]{:S(2)}) %collective-permute-start.9) | collective-permute-done | bytes 524320 | tf_op jit(solution)/shard_map/ppermute | solution.py:42
  147.0 8.6 %collective-permute-done.8.near = bf16[128,2048]{1,0:T(8,128)(2,1)S(1)} collective-permute-done((bf16[128,2048]{1,0:T(8,128)(2,1)S(1)}, bf16[128,2048]{1,0:T(8,128)(2,1)S(1)}, u32[]{:S(2)}, u32[]{:S(2)}) %collective-permute-start.8) | collective-permute-done | bytes 524320 | tf_op jit(solution)/shard_map/ppermute | solution.py:42
  155.6 4.3 collective-permute-done.10.far
  163.0 23.6 %collective-permute-done.26.refs_2_ = bf16[128,2048]{1,0:T(8,128)(2,1)} collective-permute-done((bf16[128,2048]{1,0:T(8,128)(2,1)}, bf16[128,2048]{1,0:T(8,128)(2,1)}, u32[]{:S(2)}, u32[]{:S(2)}) %collective-permute-start.26) | collective-permute-done | bytes 524320 | tf_op jit(solution)/shard_map/ppermute | solution.py:42
  188.7 7.6 %collective-permute-done.12.refs_2_ = bf16[128,2048]{1,0:T(8,128)(2,1)} collective-permute-done((bf16[128,2048]{1,0:T(8,128)(2,1)}, bf16[128,2048]{1,0:T(8,128)(2,1)}, u32[]{:S(2)}, u32[]{:S(2)}) %collective-permute-start.12) | collective-permute-done | bytes 524320 | tf_op jit(solution)/shard_map/ppermute | solution.py:42
  196.8 4.9 collective-permute-done.27.refs_3_
  204.4 8.6 %collective-permute-done.11.refs_1_ = bf16[128,2048]{1,0:T(8,128)(2,1)S(1)} collective-permute-done((bf16[128,2048]{1,0:T(8,128)(2,1)}, bf16[128,2048]{1,0:T(8,128)(2,1)S(1)}, u32[]{:S(2)}, u32[]{:S(2)}) %collective-permute-start.11) | collective-permute-done | bytes 524320 | tf_op jit(solution)/shard_map/ppermute | solution.py:42
  213.0 7.0 %collective-permute-done.13.refs_3_ = bf16[128,2048]{1,0:T(8,128)(2,1)S(1)} collective-permute-done((bf16[128,2048]{1,0:T(8,128)(2,1)}, bf16[128,2048]{1,0:T(8,128)(2,1)S(1)}, u32[]{:S(2)}, u32[]{:S(2)}) %collective-permute-start.13) | collective-permute-done | bytes 524320 | tf_op jit(solution)/shard_map/ppermute | solution.py:42
  224.5 4.7 all-to-all-start.2
  233.5 7.4 %all-to-all-done.2 = bf16[4,128,768]{2,1,0:T(8,128)(2,1)} async-done(((bf16[4,128,768]{2,1,0:T(8,128)(2,1)}), bf16[4,128,768]{2,1,0:T(8,128)(2,1)}, u32[]{:S(2)}, u32[]{:S(2)}) %all-to-all-start.2) | async-done | bytes 786464 | tf_op jit(solution)/shard_map/all_to_all | solution.py:254
  240.9 4.7 collective-permute-start.18
  245.7 34.7 %collective-permute-done.18 = bf16[512,768]{1,0:T(8,128)(2,1)S(1)} collective-permute-done((bf16[512,768]{1,0:T(8,128)(2,1)}, bf16[512,768]{1,0:T(8,128)(2,1)S(1)}, u32[]{:S(2)}, u32[]{:S(2)}) %collective-permute-start.18) | collective-permute-done | bytes 786464 | tf_op jit(solution)/shard_map/ppermute | solution.py:42
  286.9 13.5 %collective-permute-done.17 = bf16[512,1536]{1,0:T(8,128)(2,1)} collective-permute-done((bf16[512,1536]{1,0:T(8,128)(2,1)}, bf16[512,1536]{1,0:T(8,128)(2,1)}, u32[]{:S(2)}, u32[]{:S(2)}) %collective-permute-start.17) | collective-permute-done | bytes 1572896 | tf_op jit(solution)/shard_map/ppermute | solution.py:42
  300.4 10.5 %fusion.58 = f32[1024,1536]{1,0:T(8,128)} fusion(bf16[1024,2048]{1,0:T(8,128)(2,1)S(1)} %join.11, bf16[512,1536]{1,0:T(8,128)(2,1)} %collective-permute-done.17, bf16[512,1536]{1,0:T(8,128)(2,1)} %collective-permute-done.16, bf16[512,1536]{1,0:T(8,128)(2,1)} %collective-permute-done.15, bf16[512,1536]{1,0:T(8,128)(2,1)} %bitcast.7), kind=kOutput, calls=%fused_computation.99 | convolution fusion | flops 6467616768 | bytes 16777216 | tf_op jit(solution)/shard_map/dot_general | solution.py:30
  310.9 6.3 collective-permute-done.19
  317.2 16.4 %collective-permute-done.20 = bf16[512,768]{1,0:T(8,128)(2,1)S(1)} collective-permute-done((bf16[512,768]{1,0:T(8,128)(2,1)S(1)}, bf16[512,768]{1,0:T(8,128)(2,1)S(1)}, u32[]{:S(2)}, u32[]{:S(2)}) %collective-permute-start.20) | collective-permute-done | bytes 786464 | tf_op jit(solution)/shard_map/ppermute | solution.py:42
  333.6 8.2 %multiply_convert_fusion = (bf16[1024,768]{1,0:T(8,128)(2,1)S(1)}, bf16[1024,768]{1,0:T(8,128)(2,1)S(1)}, bf16[1024,768]{1,0:T(8,128)(2,1)S(1)}) fusion(f32[1024,1536]{1,0:T(8,128)} %fusion.58, bf16[1024,2048]{1,0:T(8,128)(2,1)S(1)} %join.13, bf16[512,768]{1,0:T(8,128)(2,1)S(1)} %collective-permute-done.20, ...), kind=kOutput, calls=%fused_computation.18 | convolution fusion | flops 3246391296 | bytes 18350080 | tf_op jit(solution)/shard_map/dot_general | solution.py:30
  341.9 8.9 %convolution_convert_fusion.3 = bf16[512,2048]{1,0:T(8,128)(2,1)} fusion(bf16[1024,768]{1,0:T(8,128)(2,1)S(1)} %get-tuple-element.93, bf16[1024,768]{1,0:T(8,128)(2,1)S(1)} %get-tuple-element.92, bf16[512,1536]{1,0:T(8,128)(2,1)} %collective-permute-done.17, bf16[512,1536]{1,0:T(8,128)(2,1)} %collective-permute-done.16, ...), kind=kOutput, calls=%fused_computation.24 | convolution fusion | flops 3250585600 | bytes 11534336 | tf_op jit(solution)/shard_map/dot_general | solution.py:38
  355.4 9.8 %fusion.69 = (bf16[512,2048]{1,0:T(8,128)(2,1)}, f32[512,2048]{1,0:T(8,128)}) fusion(bf16[512,2048]{1,0:T(8,128)(2,1)} %collective-permute-done.29, bf16[512,1536]{1,0:T(8,128)(2,1)} %collective-permute-done.17, bf16[512,1536]{1,0:T(8,128)(2,1)} %collective-permute-done.16, bf16[512,1536]{1,0:T(8,128)(2,1)} %collective-permute-done.15, ...), kind=kOutput, calls=%fused_computation.108 | convolution fusion | flops 3252682752 | bytes 17825792 | tf_op jit(solution)/shard_map/dot_general | solution.py:38
  368.3 5.4 convolution_convert_fusion
  375.5 5.8 collective-permute-done.31
  386.3 5.5 collective-permute-done.30.near
  399.4 8.7 %collective-permute-done.34.refs_2_ = bf16[128,2048]{1,0:T(8,128)(2,1)S(1)} collective-permute-done((bf16[128,2048]{1,0:T(8,128)(2,1)S(1)}, bf16[128,2048]{1,0:T(8,128)(2,1)S(1)}, u32[]{:S(2)}, u32[]{:S(2)}) %collective-permute-start.34) | collective-permute-done | bytes 524320 | tf_op jit(solution)/shard_map/ppermute | solution.py:42
  411.1 9.7 %collective-permute-done.35.refs_3_ = bf16[128,2048]{1,0:T(8,128)(2,1)S(1)} collective-permute-done((bf16[128,2048]{1,0:T(8,128)(2,1)S(1)}, bf16[128,2048]{1,0:T(8,128)(2,1)S(1)}, u32[]{:S(2)}, u32[]{:S(2)}) %collective-permute-start.35) | collective-permute-done | bytes 524320 | tf_op jit(solution)/shard_map/ppermute | solution.py:42
  425.9 4.8 collective-permute-start.48
  430.7 5.7 fusion.68
  436.4 29.4 %collective-permute-done.48 = bf16[512,768]{1,0:T(8,128)(2,1)S(1)} collective-permute-done((bf16[512,768]{1,0:T(8,128)(2,1)S(1)}, bf16[512,768]{1,0:T(8,128)(2,1)S(1)}, u32[]{:S(2)}, u32[]{:S(2)}) %collective-permute-start.48) | collective-permute-done | bytes 786464 | tf_op jit(solution)/shard_map/ppermute | solution.py:42
  466.8 3.7 all-to-all-start.6
  470.5 7.1 %convert_add_fusion = f32[1024,1536]{1,0:T(8,128)S(1)} fusion(bf16[1024,1536]{1,0:T(8,128)(2,1)} %collective-permute-done.45, bf16[1024,2048]{1,0:T(8,128)(2,1)} %copy-done.1, bf16[1024,768]{1,0:T(8,128)(2,1)} %copy-done.45, bf16[1024,768]{1,0:T(8,128)(2,1)} %copy-done.46), kind=kOutput, calls=%fused_computation.1 | convolution fusion | flops 3230662656 | bytes 14680064 | tf_op jit(solution)/shard_map/dot_general | solution.py:34
  484.4 8.8 %attend_back.1 = (bf16[2,4,128,512]{3,2,1,0:T(8,128)(2,1)S(1)}, f32[2,128]{1,0:T(2,128)S(1)}) custom-call(s32[1]{0:T(128)} %bitcast.2.shift_ref, f32[2,4,128,512]{3,2,1,0:T(8,128)S(1)} %bitcast.36, bf16[2,4,128,256]{3,2,1,0:T(8,128)(2,1)S(1)} %bitcast.41, f32[256,128]{1,0:T(8,128)S(1)} %get-tuple-element.126.cos_ref, ...), custom_call_target="tpu_custom_call" | custom-call | tf_op jit(solution)/shard_map/attend_back/pallas_call | solution.py:471
  502.6 46.2 %collective-permute-done.46 = bf16[512,1536]{1,0:T(8,128)(2,1)S(1)} collective-permute-done((bf16[512,1536]{1,0:T(8,128)(2,1)S(1)}, bf16[512,1536]{1,0:T(8,128)(2,1)S(1)}, u32[]{:S(2)}, u32[]{:S(2)}) %collective-permute-start.46) | collective-permute-done | bytes 1572896 | tf_op jit(solution)/shard_map/ppermute | solution.py:42
  551.3 3.8 all-to-all-start.5
  568.0 5.0 fusion.70
  579.8 18.4 %collective-permute-done.42 = bf16[512,512]{1,0:T(8,128)(2,1)S(1)} collective-permute-done((bf16[512,512]{1,0:T(8,128)(2,1)S(1)}, bf16[512,512]{1,0:T(8,128)(2,1)S(1)}, u32[]{:S(2)}, u32[]{:S(2)}) %collective-permute-start.42) | collective-permute-done | bytes 524320 | tf_op jit(solution)/shard_map/ppermute | solution.py:42
  604.3 6.0 collective-permute-done.39
  613.7 8.0 %all-to-all-done.4.got = bf16[4,128,256]{2,1,0:T(8,128)(2,1)S(1)} async-done(((bf16[4,128,256]{2,1,0:T(8,128)(2,1)}), bf16[4,128,256]{2,1,0:T(8,128)(2,1)S(1)}, u32[]{:S(2)}, u32[]{:S(2)}) %all-to-all-start.4) | async-done | bytes 262176 | tf_op jit(solution)/shard_map/all_to_all | solution.py:254
  621.7 4.1 all-to-all-start.3
  630.0 3.5 back_one.1
  642.7 3.4 collective-permute-done.52
  649.1 3.5 adam_turned.3
  652.7 6.2 adam_columns.1
  (280 shorter events, 168.4 us)
Async XLA Ops:
  3.7 29.4 %all-to-all-start = ((bf16[4,128,768]{2,1,0:T(8,128)(2,1)}), bf16[4,128,768]{2,1,0:T(8,128)(2,1)}, u32[]{:S(2)}, u32[]{:S(2)}) async-start(bf16[4,128,768]{2,1,0:T(8,128)(2,1)} %pack_attention.1), calls=%async_computation | async-start | bytes 1572864 | tf_op jit(solution)/shard_map/all_to_all | solution.py:254
  11.7 19.9 %collective-permute-start.1 = (bf16[128,2048]{1,0:T(8,128)(2,1)S(1)}, bf16[128,2048]{1,0:T(8,128)(2,1)S(1)}, u32[]{:S(2)}, u32[]{:S(2)}) collective-permute-start(bf16[128,2048]{1,0:T(8,128)(2,1)S(1)} %get-tuple-element.55.refs_0_), channel_id=1, source_target_pairs={{0,8},{8,0},{1,9},{9,1},{2,10},{10,2},{3,11},{11,3},{4,12},{12,4},... | collective-permute-start | bytes 1572872 | tf_op jit(solution)/shard_map/ppermute | solution.py:42
  13.8 22.1 %collective-permute-start = (bf16[128,2048]{1,0:T(8,128)(2,1)S(1)}, bf16[128,2048]{1,0:T(8,128)(2,1)S(1)}, u32[]{:S(2)}, u32[]{:S(2)}) collective-permute-start(bf16[128,2048]{1,0:T(8,128)(2,1)S(1)} %get-tuple-element.55.refs_0_), channel_id=1, source_target_pairs={{0,4},{4,0},{1,5},{5,1},{2,6},{6,2},{3,7},{7,3},{8,12},{12,8},{9,1... | collective-permute-start | bytes 1572872 | tf_op jit(solution)/shard_map/ppermute | solution.py:42
  33.1 36.2 %collective-permute-start.4 = (bf16[512,768]{1,0:T(8,128)(2,1)}, bf16[512,768]{1,0:T(8,128)(2,1)S(1)}, u32[]{:S(2)}, u32[]{:S(2)}) collective-permute-start(bf16[512,768]{1,0:T(8,128)(2,1)} %bitcast.3), channel_id=1, source_target_pairs={{0,16},{16,0},{1,17},{17,1},{2,18},{18,2},{3,19},{19,3},{4,20},{20... | collective-permute-start | bytes 2359304 | tf_op jit(solution)/shard_map/ppermute | solution.py:42
  46.2 46.0 %collective-permute-start.3 = (bf16[512,2048]{1,0:T(8,128)(2,1)}, bf16[512,2048]{1,0:T(8,128)(2,1)}, u32[]{:S(2)}, u32[]{:S(2)}) collective-permute-start(bf16[512,2048]{1,0:T(8,128)(2,1)} %join.8.refs_0_), channel_id=1, source_target_pairs={{0,1},{1,0},{2,3},{3,2},{4,5},{5,4},{6,7},{7,6},{8,9},{9,8},{10,11... | collective-permute-start | bytes 6291464 | tf_op jit(solution)/shard_map/ppermute | solution.py:42
  46.2 25.3 %collective-permute-start.5 = (bf16[512,768]{1,0:T(8,128)(2,1)}, bf16[512,768]{1,0:T(8,128)(2,1)S(1)}, u32[]{:S(2)}, u32[]{:S(2)}) collective-permute-start(bf16[512,768]{1,0:T(8,128)(2,1)} %bitcast.3), channel_id=1, source_target_pairs={{0,2},{2,0},{1,3},{3,1},{4,6},{6,4},{5,7},{7,5},{8,10},{10,8},{9,1... | collective-permute-start | bytes 2359304 | tf_op jit(solution)/shard_map/ppermute | solution.py:42
  69.3 19.6 %collective-permute-start.6 = (bf16[512,768]{1,0:T(8,128)(2,1)S(1)}, bf16[512,768]{1,0:T(8,128)(2,1)}, u32[]{:S(2)}, u32[]{:S(2)}) collective-permute-start(bf16[512,768]{1,0:T(8,128)(2,1)S(1)} %collective-permute-done.4), channel_id=1, source_target_pairs={{0,2},{2,0},{1,3},{3,1},{4,6},{6,4},{5,7},{7,5},{8,10},{10,8},{9,1... | collective-permute-start | bytes 2359304 | tf_op jit(solution)/shard_map/ppermute | solution.py:42
  108.7 54.1 %all-to-all-start.1 = ((bf16[4,128,1536]{2,1,0:T(8,128)(2,1)}), bf16[4,128,1536]{2,1,0:T(8,128)(2,1)}, u32[]{:S(2)}, u32[]{:S(2)}) async-start(bf16[4,128,1536]{2,1,0:T(8,128)(2,1)} %pack_columns.1), calls=%async_computation.1 | async-start | bytes 3145728 | tf_op jit(solution)/shard_map/all_to_all | solution.py:254
  115.6 29.2 %collective-permute-start.9 = (bf16[128,2048]{1,0:T(8,128)(2,1)S(1)}, bf16[128,2048]{1,0:T(8,128)(2,1)S(1)}, u32[]{:S(2)}, u32[]{:S(2)}) collective-permute-start(bf16[128,2048]{1,0:T(8,128)(2,1)S(1)} %get-tuple-element.109), channel_id=1, source_target_pairs={{0,4},{4,0},{1,5},{5,1},{2,6},{6,2},{3,7},{7,3},{8,12},{12,8},{9,1... | collective-permute-start | bytes 1572872 | tf_op jit(solution)/shard_map/ppermute | solution.py:42
  117.6 38.0 %collective-permute-start.8 = (bf16[128,2048]{1,0:T(8,128)(2,1)S(1)}, bf16[128,2048]{1,0:T(8,128)(2,1)S(1)}, u32[]{:S(2)}, u32[]{:S(2)}) collective-permute-start(bf16[128,2048]{1,0:T(8,128)(2,1)S(1)} %get-tuple-element.110), channel_id=1, source_target_pairs={{0,4},{4,0},{1,5},{5,1},{2,6},{6,2},{3,7},{7,3},{8,12},{12,8},{9,1... | collective-permute-start | bytes 1572872 | tf_op jit(solution)/shard_map/ppermute | solution.py:42
  146.1 40.6 %collective-permute-start.26 = (bf16[128,2048]{1,0:T(8,128)(2,1)}, bf16[128,2048]{1,0:T(8,128)(2,1)}, u32[]{:S(2)}, u32[]{:S(2)}) collective-permute-start(bf16[128,2048]{1,0:T(8,128)(2,1)} %get-tuple-element.60.refs_0_.cotangent), channel_id=1, source_target_pairs={{0,8},{8,0},{1,9},{9,1},{2,10},{10,2},{3,11},{11,3},{4,12},{12,4},... | collective-permute-start | bytes 1572872 | tf_op jit(solution)/shard_map/ppermute | solution.py:42
  161.7 34.6 %collective-permute-start.12 = (bf16[128,2048]{1,0:T(8,128)(2,1)}, bf16[128,2048]{1,0:T(8,128)(2,1)}, u32[]{:S(2)}, u32[]{:S(2)}) collective-permute-start(bf16[128,2048]{1,0:T(8,128)(2,1)} %get-tuple-element.58.refs_0_), channel_id=1, source_target_pairs={{0,8},{8,0},{1,9},{9,1},{2,10},{10,2},{3,11},{11,3},{4,12},{12,4},... | collective-permute-start | bytes 1572872 | tf_op jit(solution)/shard_map/ppermute | solution.py:42
  162.7 69.3 %collective-permute-start.15 = (bf16[512,1536]{1,0:T(8,128)(2,1)}, bf16[512,1536]{1,0:T(8,128)(2,1)}, u32[]{:S(2)}, u32[]{:S(2)}) collective-permute-start(bf16[512,1536]{1,0:T(8,128)(2,1)} %bitcast.7), channel_id=1, source_target_pairs={{0,16},{16,0},{1,17},{17,1},{2,18},{18,2},{3,19},{19,3},{4,20},{20... | collective-permute-start | bytes 4718600 | tf_op jit(solution)/shard_map/ppermute | solution.py:42
  162.7 34.1 %collective-permute-start.25 = (bf16[128,2048]{1,0:T(8,128)(2,1)}, bf16[128,2048]{1,0:T(8,128)(2,1)S(1)}, u32[]{:S(2)}, u32[]{:S(2)}) collective-permute-start(bf16[128,2048]{1,0:T(8,128)(2,1)} %get-tuple-element.60.refs_0_.cotangent), channel_id=1, source_target_pairs={{0,4},{4,0},{1,5},{5,1},{2,6},{6,2},{3,7},{7,3},{8,12},{12,8},{9,1... | collective-permute-start | bytes 1572872 | tf_op jit(solution)/shard_map/ppermute | solution.py:42
  186.7 15.1 %collective-permute-start.27 = (bf16[128,2048]{1,0:T(8,128)(2,1)}, bf16[128,2048]{1,0:T(8,128)(2,1)S(1)}, u32[]{:S(2)}, u32[]{:S(2)}) collective-permute-start(bf16[128,2048]{1,0:T(8,128)(2,1)} %collective-permute-done.26.refs_2_), channel_id=1, source_target_pairs={{0,4},{4,0},{1,5},{5,1},{2,6},{6,2},{3,7},{7,3},{8,12},{12,8},{9,1... | collective-permute-start | bytes 1572872 | tf_op jit(solution)/shard_map/ppermute | solution.py:42
  186.8 26.1 %collective-permute-start.11 = (bf16[128,2048]{1,0:T(8,128)(2,1)}, bf16[128,2048]{1,0:T(8,128)(2,1)S(1)}, u32[]{:S(2)}, u32[]{:S(2)}) collective-permute-start(bf16[128,2048]{1,0:T(8,128)(2,1)} %get-tuple-element.58.refs_0_), channel_id=1, source_target_pairs={{0,4},{4,0},{1,5},{5,1},{2,6},{6,2},{3,7},{7,3},{8,12},{12,8},{9,1... | collective-permute-start | bytes 1572872 | tf_op jit(solution)/shard_map/ppermute | solution.py:42
  196.3 23.7 %collective-permute-start.13 = (bf16[128,2048]{1,0:T(8,128)(2,1)}, bf16[128,2048]{1,0:T(8,128)(2,1)S(1)}, u32[]{:S(2)}, u32[]{:S(2)}) collective-permute-start(bf16[128,2048]{1,0:T(8,128)(2,1)} %collective-permute-done.12.refs_2_), channel_id=1, source_target_pairs={{0,4},{4,0},{1,5},{5,1},{2,6},{6,2},{3,7},{7,3},{8,12},{12,8},{9,1... | collective-permute-start | bytes 1572872 | tf_op jit(solution)/shard_map/ppermute | solution.py:42
  204.3 77.6 %collective-permute-start.28 = (bf16[512,2048]{1,0:T(8,128)(2,1)}, bf16[512,2048]{1,0:T(8,128)(2,1)}, u32[]{:S(2)}, u32[]{:S(2)}) collective-permute-start(bf16[512,2048]{1,0:T(8,128)(2,1)} %join.12.refs_0_), channel_id=1, source_target_pairs={{0,1},{1,0},{2,3},{3,2},{4,5},{5,4},{6,7},{7,6},{8,9},{9,8},{10,11... | collective-permute-start | bytes 6291464 | tf_op jit(solution)/shard_map/ppermute | solution.py:42
  222.6 62.0 %collective-permute-start.14 = (bf16[512,2048]{1,0:T(8,128)(2,1)}, bf16[512,2048]{1,0:T(8,128)(2,1)}, u32[]{:S(2)}, u32[]{:S(2)}) collective-permute-start(bf16[512,2048]{1,0:T(8,128)(2,1)} %join.10.refs_0_), channel_id=1, source_target_pairs={{0,1},{1,0},{2,3},{3,2},{4,5},{5,4},{6,7},{7,6},{8,9},{9,8},{10,11... | collective-permute-start | bytes 6291464 | tf_op jit(solution)/shard_map/ppermute | solution.py:42
  224.5 16.5 %all-to-all-start.2 = ((bf16[4,128,768]{2,1,0:T(8,128)(2,1)}), bf16[4,128,768]{2,1,0:T(8,128)(2,1)}, u32[]{:S(2)}, u32[]{:S(2)}) async-start(bf16[4,128,768]{2,1,0:T(8,128)(2,1)} %pack_turned.1), calls=%async_computation.2 | async-start | bytes 1572864 | tf_op jit(solution)/shard_map/all_to_all | solution.py:254
  229.2 57.7 %collective-permute-start.16 = (bf16[512,1536]{1,0:T(8,128)(2,1)}, bf16[512,1536]{1,0:T(8,128)(2,1)}, u32[]{:S(2)}, u32[]{:S(2)}) collective-permute-start(bf16[512,1536]{1,0:T(8,128)(2,1)} %bitcast.7), channel_id=1, source_target_pairs={{0,2},{2,0},{1,3},{3,1},{4,6},{6,4},{5,7},{7,5},{8,10},{10,8},{9,1... | collective-permute-start | bytes 4718600 | tf_op jit(solution)/shard_map/ppermute | solution.py:42
  232.0 68.5 %collective-permute-start.17 = (bf16[512,1536]{1,0:T(8,128)(2,1)}, bf16[512,1536]{1,0:T(8,128)(2,1)}, u32[]{:S(2)}, u32[]{:S(2)}) collective-permute-start(bf16[512,1536]{1,0:T(8,128)(2,1)} %collective-permute-done.15), channel_id=1, source_target_pairs={{0,2},{2,0},{1,3},{3,1},{4,6},{6,4},{5,7},{7,5},{8,10},{10,8},{9,1... | collective-permute-start | bytes 4718600 | tf_op jit(solution)/shard_map/ppermute | solution.py:42
  240.9 39.4 %collective-permute-start.18 = (bf16[512,768]{1,0:T(8,128)(2,1)}, bf16[512,768]{1,0:T(8,128)(2,1)S(1)}, u32[]{:S(2)}, u32[]{:S(2)}) collective-permute-start(bf16[512,768]{1,0:T(8,128)(2,1)} %bitcast.8), channel_id=1, source_target_pairs={{0,16},{16,0},{1,17},{17,1},{2,18},{18,2},{3,19},{19,3},{4,20},{20... | collective-permute-start | bytes 2359304 | tf_op jit(solution)/shard_map/ppermute | solution.py:42
  280.3 36.8 %collective-permute-start.19 = (bf16[512,768]{1,0:T(8,128)(2,1)}, bf16[512,768]{1,0:T(8,128)(2,1)S(1)}, u32[]{:S(2)}, u32[]{:S(2)}) collective-permute-start(bf16[512,768]{1,0:T(8,128)(2,1)} %bitcast.8), channel_id=1, source_target_pairs={{0,2},{2,0},{1,3},{3,1},{4,6},{6,4},{5,7},{7,5},{8,10},{10,8},{9,1... | collective-permute-start | bytes 2359304 | tf_op jit(solution)/shard_map/ppermute | solution.py:42
  281.9 51.7 %collective-permute-start.20 = (bf16[512,768]{1,0:T(8,128)(2,1)S(1)}, bf16[512,768]{1,0:T(8,128)(2,1)S(1)}, u32[]{:S(2)}, u32[]{:S(2)}) collective-permute-start(bf16[512,768]{1,0:T(8,128)(2,1)S(1)} %collective-permute-done.18), channel_id=1, source_target_pairs={{0,2},{2,0},{1,3},{3,1},{4,6},{6,4},{5,7},{7,5},{8,10},{10,8},{9,1... | collective-permute-start | bytes 2359304 | tf_op jit(solution)/shard_map/ppermute | solution.py:42
  353.9 68.5 %collective-permute-start.47 = (bf16[1024,768]{1,0:T(8,128)(2,1)}, bf16[1024,768]{1,0:T(8,128)(2,1)}, u32[]{:S(2)}, u32[]{:S(2)}) collective-permute-start(bf16[1024,768]{1,0:T(8,128)(2,1)} %fusion.17), channel_id=1, source_target_pairs={{0,2},{2,0},{1,3},{3,1},{4,6},{6,4},{5,7},{7,5},{8,10},{10,8},{9,1... | collective-permute-start | bytes 4718600 | tf_op jit(solution)/shard_map/ppermute | solution.py:42
  373.7 96.9 %collective-permute-start.45 = (bf16[1024,1536]{1,0:T(8,128)(2,1)}, bf16[1024,1536]{1,0:T(8,128)(2,1)}, u32[]{:S(2)}, u32[]{:S(2)}) collective-permute-start(bf16[1024,1536]{1,0:T(8,128)(2,1)} %convolution_convert_fusion), channel_id=1, source_target_pairs={{0,2},{2,0},{1,3},{3,1},{4,6},{6,4},{5,7},{7,5},{8,10},{10,8},{9,1... | collective-permute-start | bytes 9437192 | tf_op jit(solution)/shard_map/ppermute | solution.py:42
  375.2 16.7 %collective-permute-start.30 = (bf16[128,2048]{1,0:T(8,128)(2,1)S(1)}, bf16[128,2048]{1,0:T(8,128)(2,1)S(1)}, u32[]{:S(2)}, u32[]{:S(2)}) collective-permute-start(bf16[128,2048]{1,0:T(8,128)(2,1)S(1)} %get-tuple-element.106), channel_id=1, source_target_pairs={{0,4},{4,0},{1,5},{5,1},{2,6},{6,2},{3,7},{7,3},{8,12},{12,8},{9,1... | collective-permute-start | bytes 1572872 | tf_op jit(solution)/shard_map/ppermute | solution.py:42
  386.2 44.5 %collective-permute-start.21 = (bf16[512,2048]{1,0:T(8,128)(2,1)S(1)}, bf16[512,2048]{1,0:T(8,128)(2,1)S(1)}, u32[]{:S(2)}, u32[]{:S(2)}) collective-permute-start(bf16[512,2048]{1,0:T(8,128)(2,1)S(1)} %convolution_convert_fusion.4), channel_id=1, source_target_pairs={{0,1},{1,0},{2,3},{3,2},{4,5},{5,4},{6,7},{7,6},{8,9},{9,8},{10,11... | collective-permute-start | bytes 6291464 | tf_op jit(solution)/shard_map/ppermute | solution.py:42
  422.3 56.7 %collective-permute-start.36 = (bf16[512,2048]{1,0:T(8,128)(2,1)}, bf16[512,2048]{1,0:T(8,128)(2,1)}, u32[]{:S(2)}, u32[]{:S(2)}) collective-permute-start(bf16[512,2048]{1,0:T(8,128)(2,1)} %join.14.refs_0_), channel_id=1, source_target_pairs={{0,1},{1,0},{2,3},{3,2},{4,5},{5,4},{6,7},{7,6},{8,9},{9,8},{10,11... | collective-permute-start | bytes 6291464 | tf_op jit(solution)/shard_map/ppermute | solution.py:42
  425.9 39.9 %collective-permute-start.48 = (bf16[512,768]{1,0:T(8,128)(2,1)S(1)}, bf16[512,768]{1,0:T(8,128)(2,1)S(1)}, u32[]{:S(2)}, u32[]{:S(2)}) collective-permute-start(bf16[512,768]{1,0:T(8,128)(2,1)S(1)} %slice.345), channel_id=1, source_target_pairs={{0,16},{16,0},{1,17},{17,1},{2,18},{18,2},{3,19},{19,3},{4,20},{20... | collective-permute-start | bytes 2359304 | tf_op jit(solution)/shard_map/ppermute | solution.py:42
  466.8 83.7 %all-to-all-start.6 = ((bf16[4,128,768]{2,1,0:T(8,128)(2,1)}), bf16[4,128,768]{2,1,0:T(8,128)(2,1)S(1)}, u32[]{:S(2)}, u32[]{:S(2)}) async-start(bf16[4,128,768]{2,1,0:T(8,128)(2,1)} %bitcast.43), calls=%async_computation.6 | async-start | bytes 1572864 | tf_op jit(solution)/shard_map/all_to_all | solution.py:254
  477.8 71.0 %collective-permute-start.46 = (bf16[512,1536]{1,0:T(8,128)(2,1)S(1)}, bf16[512,1536]{1,0:T(8,128)(2,1)S(1)}, u32[]{:S(2)}, u32[]{:S(2)}) collective-permute-start(bf16[512,1536]{1,0:T(8,128)(2,1)S(1)} %slice.344), channel_id=1, source_target_pairs={{0,16},{16,0},{1,17},{17,1},{2,18},{18,2},{3,19},{19,3},{4,20},{20... | collective-permute-start | bytes 4718600 | tf_op jit(solution)/shard_map/ppermute | solution.py:42
  494.8 64.7 %collective-permute-start.43 = (bf16[1024,256]{1,0:T(8,128)(2,1)}, bf16[1024,256]{1,0:T(8,128)(2,1)}, u32[]{:S(2)}, u32[]{:S(2)}) collective-permute-start(bf16[1024,256]{1,0:T(8,128)(2,1)} %fusion.37), channel_id=1, source_target_pairs={{0,2},{2,0},{1,3},{3,1},{4,6},{6,4},{5,7},{7,5},{8,10},{10,8},{9,1... | collective-permute-start | bytes 1572872 | tf_op jit(solution)/shard_map/ppermute | solution.py:42
  499.3 68.7 %collective-permute-start.37 = (bf16[512,2048]{1,0:T(8,128)(2,1)}, bf16[512,2048]{1,0:T(8,128)(2,1)}, u32[]{:S(2)}, u32[]{:S(2)}) collective-permute-start(bf16[512,2048]{1,0:T(8,128)(2,1)} %convolution_convert_fusion.2), channel_id=1, source_target_pairs={{0,1},{1,0},{2,3},{3,2},{4,5},{5,4},{6,7},{7,6},{8,9},{9,8},{10,11... | collective-permute-start | bytes 6291464 | tf_op jit(solution)/shard_map/ppermute | solution.py:42
  501.5 61.7 %collective-permute-start.41 = (bf16[1024,512]{1,0:T(8,128)(2,1)}, bf16[1024,512]{1,0:T(8,128)(2,1)}, u32[]{:S(2)}, u32[]{:S(2)}) collective-permute-start(bf16[1024,512]{1,0:T(8,128)(2,1)} %fusion.31), channel_id=1, source_target_pairs={{0,2},{2,0},{1,3},{3,1},{4,6},{6,4},{5,7},{7,5},{8,10},{10,8},{9,1... | collective-permute-start | bytes 3145736 | tf_op jit(solution)/shard_map/ppermute | solution.py:42
  551.3 49.5 %all-to-all-start.5 = ((bf16[4,128,1536]{2,1,0:T(8,128)(2,1)}), bf16[4,128,1536]{2,1,0:T(8,128)(2,1)S(1)}, u32[]{:S(2)}, u32[]{:S(2)}) async-start(bf16[4,128,1536]{2,1,0:T(8,128)(2,1)} %bitcast.42), calls=%async_computation.5 | async-start | bytes 3145728 | tf_op jit(solution)/shard_map/all_to_all | solution.py:254
  557.4 68.4 %collective-permute-start.23 = (bf16[128,2048]{1,0:T(8,128)(2,1)}, bf16[128,2048]{1,0:T(8,128)(2,1)}, u32[]{:S(2)}, u32[]{:S(2)}) collective-permute-start(bf16[128,2048]{1,0:T(8,128)(2,1)} %get-tuple-element.107), channel_id=1, source_target_pairs={{0,4},{4,0},{1,5},{5,1},{2,6},{6,2},{3,7},{7,3},{8,12},{12,8},{9,1... | collective-permute-start | bytes 1572872 | tf_op jit(solution)/shard_map/ppermute | solution.py:42
  559.4 87.3 %collective-permute-start.22 = (bf16[128,2048]{1,0:T(8,128)(2,1)}, bf16[128,2048]{1,0:T(8,128)(2,1)}, u32[]{:S(2)}, u32[]{:S(2)}) collective-permute-start(bf16[128,2048]{1,0:T(8,128)(2,1)} %get-tuple-element.108), channel_id=1, source_target_pairs={{0,4},{4,0},{1,5},{5,1},{2,6},{6,2},{3,7},{7,3},{8,12},{12,8},{9,1... | collective-permute-start | bytes 1572872 | tf_op jit(solution)/shard_map/ppermute | solution.py:42
  562.3 16.8 %collective-permute-start.44 = (bf16[512,256]{1,0:T(8,128)(2,1)S(1)}, bf16[512,256]{1,0:T(8,128)(2,1)S(1)}, u32[]{:S(2)}, u32[]{:S(2)}) collective-permute-start(bf16[512,256]{1,0:T(8,128)(2,1)S(1)} %slice.347), channel_id=1, source_target_pairs={{0,16},{16,0},{1,17},{17,1},{2,18},{18,2},{3,19},{19,3},{4,20},{20... | collective-permute-start | bytes 786440 | tf_op jit(solution)/shard_map/ppermute | solution.py:42
  565.9 32.3 %collective-permute-start.42 = (bf16[512,512]{1,0:T(8,128)(2,1)S(1)}, bf16[512,512]{1,0:T(8,128)(2,1)S(1)}, u32[]{:S(2)}, u32[]{:S(2)}) collective-permute-start(bf16[512,512]{1,0:T(8,128)(2,1)S(1)} %slice.346), channel_id=1, source_target_pairs={{0,16},{16,0},{1,17},{17,1},{2,18},{18,2},{3,19},{19,3},{4,20},{20... | collective-permute-start | bytes 1572872 | tf_op jit(solution)/shard_map/ppermute | solution.py:42
  574.0 36.2 %collective-permute-start.39 = (bf16[128,2048]{1,0:T(8,128)(2,1)}, bf16[128,2048]{1,0:T(8,128)(2,1)}, u32[]{:S(2)}, u32[]{:S(2)}) collective-permute-start(bf16[128,2048]{1,0:T(8,128)(2,1)} %get-tuple-element.103), channel_id=1, source_target_pairs={{0,4},{4,0},{1,5},{5,1},{2,6},{6,2},{3,7},{7,3},{8,12},{12,8},{9,1... | collective-permute-start | bytes 1572872 | tf_op jit(solution)/shard_map/ppermute | solution.py:42
  599.2 30.7 %collective-permute-start.38 = (bf16[128,2048]{1,0:T(8,128)(2,1)}, bf16[128,2048]{1,0:T(8,128)(2,1)}, u32[]{:S(2)}, u32[]{:S(2)}) collective-permute-start(bf16[128,2048]{1,0:T(8,128)(2,1)} %get-tuple-element.104), channel_id=1, source_target_pairs={{0,4},{4,0},{1,5},{5,1},{2,6},{6,2},{3,7},{7,3},{8,12},{12,8},{9,1... | collective-permute-start | bytes 1572872 | tf_op jit(solution)/shard_map/ppermute | solution.py:42
  600.8 20.9 %all-to-all-start.4 = ((bf16[4,128,256]{2,1,0:T(8,128)(2,1)}), bf16[4,128,256]{2,1,0:T(8,128)(2,1)S(1)}, u32[]{:S(2)}, u32[]{:S(2)}) async-start(bf16[4,128,256]{2,1,0:T(8,128)(2,1)} %bitcast.47), calls=%async_computation.4 | async-start | bytes 524288 | tf_op jit(solution)/shard_map/all_to_all | solution.py:254
  613.2 16.7 %collective-permute-start.40 = (bf16[128,2048]{1,0:T(8,128)(2,1)}, bf16[128,2048]{1,0:T(8,128)(2,1)}, u32[]{:S(2)}, u32[]{:S(2)}) collective-permute-start(bf16[128,2048]{1,0:T(8,128)(2,1)} %get-tuple-element.95), channel_id=1, source_target_pairs={{0,8},{8,0},{1,9},{9,1},{2,10},{10,2},{3,11},{11,3},{4,12},{12,4},... | collective-permute-start | bytes 1572872 | tf_op jit(solution)/shard_map/ppermute | solution.py:42
  621.7 39.4 %all-to-all-start.3 = ((bf16[4,128,512]{2,1,0:T(8,128)(2,1)}), bf16[4,128,512]{2,1,0:T(8,128)(2,1)}, u32[]{:S(2)}, u32[]{:S(2)}) async-start(bf16[4,128,512]{2,1,0:T(8,128)(2,1)} %bitcast.44), calls=%async_computation.3 | async-start | bytes 1048576 | tf_op jit(solution)/shard_map/all_to_all | solution.py:254
  627.9 18.9 %collective-permute-start.24 = (bf16[128,2048]{1,0:T(8,128)(2,1)S(1)}, bf16[128,2048]{1,0:T(8,128)(2,1)S(1)}, u32[]{:S(2)}, u32[]{:S(2)}) collective-permute-start(bf16[128,2048]{1,0:T(8,128)(2,1)S(1)} %get-tuple-element.99), channel_id=1, source_target_pairs={{0,8},{8,0},{1,9},{9,1},{2,10},{10,2},{3,11},{11,3},{4,12},{12,4},... | collective-permute-start | bytes 1572872 | tf_op jit(solution)/shard_map/ppermute | solution.py:42
  646.2 21.8 %collective-permute-start.53 = (f32[2,2176]{1,0:T(2,128)S(1)}, f32[2,2176]{1,0:T(2,128)S(1)}, u32[]{:S(2)}, u32[]{:S(2)}) collective-permute-start(f32[2,2176]{1,0:T(2,128)S(1)} %add.143), channel_id=1, source_target_pairs={{0,16},{16,0},{1,17},{17,1},{2,18},{18,2},{3,19},{19,3},{4,20},{20... | collective-permute-start | bytes 52232 | tf_op jit(solution)/shard_map/ppermute | solution.py:42
  (77 other events, 1500.6 us)

commit v2 on v1

--- a/solution.py
+++ b/solution.py
@@ -25,6 +25,8 @@
 
 SWAP = [(0, 1), (1, 0)]
 
+FREE = pl.CostEstimate(flops=0, bytes_accessed=0, transcendentals=0)
+
 
 def dot(left, right):
     return jnp.dot(left, right, preferred_element_type=f32)
@@ -72,7 +74,7 @@
         in_specs=[pl.BlockSpec(memory_space=pltpu.SMEM)] + [pl.BlockSpec(memory_space=pltpu.VMEM)] * (len(args) - 1),
         out_specs=jax.tree.map(lambda _: pl.BlockSpec(memory_space=pltpu.VMEM), out_shape),
         out_shape=out_shape,
-        cost_estimate=pl.CostEstimate(flops=flops, bytes_accessed=size, transcendentals=0),
+        cost_estimate=FREE,
         compiler_params=pltpu.CompilerParams(vmem_limit_bytes=40 * 1024 * 1024),
         name=name,
     )(*args)
@@ -163,30 +165,38 @@
         out_specs=pl.BlockSpec(memory_space=pltpu.VMEM),
         out_shape=total,
         scratch_shapes=[pltpu.SemaphoreType.DMA((len(parts),))],
-        cost_estimate=pl.CostEstimate(flops=0, bytes_accessed=size, transcendentals=0),
+        cost_estimate=FREE,
         compiler_params=pltpu.CompilerParams(vmem_limit_bytes=16 * 1024 * 1024),
         name="join",
     )(*parts)
 
 
-def gather_rows(value):
+def after(value, *others):
+    return lax.optimization_barrier((value, *others))[0]
+
+
+def rows_of(value, count):
+    step = value.shape[0] // count
+    return [value[i * step : (i + 1) * step] for i in range(count)]
+
+
+def gather_rows(value, at_send=(), at_half=(), at_whole=()):
     over_zl = swap(value, "zl")
     over_y = swap(value, "y")
-    over_both = swap(over_zl, "y")
-    half = join(value, over_y, over_zl, over_both)
-    return join(half, swap(half, "c"))
-
-
-def sum_rows(left, right_t):
+    over_both = swap(after(over_zl, *at_send), "y")
+    half = join(after(value, *at_half), over_y, over_zl, over_both)
+    return join(after(half, *at_whole), swap(half, "c"))
+
+
+def sum_rows(left, right_t, at_mine=(), at_far=()):
     half = left.shape[0] // 2
-    rows = half // 4
-    other = dot_nt(left[half:], right_t).astype(bf16)
-    mine = dot_nt(left[:half], right_t) + swap(other, "c").astype(f32)
-    block = lambda i: mine[i * rows : (i + 1) * rows]
-    both = swap(block(3).astype(bf16), "y")
-    near = swap(block(1).astype(bf16), "y")
-    far = swap((block(2) + both.astype(f32)).astype(bf16), "zl")
-    return block(0), near, far
+    other = swap(dot_nt(left[half:], right_t).astype(bf16), "c")
+    mine = dot_nt(left[:half], right_t) + after(other, *at_mine).astype(f32)
+    block = rows_of(mine, 4)
+    both = swap(block[3].astype(bf16), "y")
+    near = swap(block[1].astype(bf16), "y")
+    far = swap((block[2] + after(both, *at_far).astype(f32)).astype(bf16), "zl")
+    return block[0], near, far
 
 
 def pack_attention_kernel(wide_q, wide_kv, qkv, out, packed):
@@ -206,6 +216,7 @@
     return pl.pallas_call(
         functools.partial(pack_attention_kernel, wide_q, wide_kv),
         out_shape=packed,
+        cost_estimate=FREE,
         compiler_params=pltpu.CompilerParams(vmem_limit_bytes=40 * 1024 * 1024),
         name="pack_attention",
     )(qkv, out)
@@ -228,6 +239,7 @@
         ],
         out_specs=pl.BlockSpec((1, depth, 2 * wide), lambda j: (j, 0, 0)),
         out_shape=jax.ShapeDtypeStruct((4, depth, 2 * wide), bf16),
+        cost_estimate=FREE,
         compiler_params=pltpu.CompilerParams(vmem_limit_bytes=40 * 1024 * 1024),
         name="pack_columns",
     )(array, array)
@@ -245,6 +257,7 @@
         in_specs=[pl.BlockSpec((wide, depth), lambda j: (j, 0))],
         out_specs=pl.BlockSpec((1, depth, wide), lambda j: (j, 0, 0)),
         out_shape=jax.ShapeDtypeStruct((4, depth, wide), bf16),
+        cost_estimate=FREE,
         compiler_params=pltpu.CompilerParams(vmem_limit_bytes=40 * 1024 * 1024),
         name="pack_turned",
     )(array)
@@ -254,25 +267,32 @@
     return lax.all_to_all(pieces, ("zl", "y"), 0, 0, tiled=True)
 
 
-def gather_weight(pieces, rest):
+def own_block(pieces, rest):
     mine = exchange(pieces)
     if rest > 1:
         mine = lax.all_gather(mine, "r", axis=1, tiled=True)
-    mine = mine.reshape(-1, mine.shape[-1])
-    far = swap(mine, "zh")
-    return jnp.concatenate([mine, far, swap(mine, "x"), swap(far, "x")], axis=0)
-
-
-def scatter_grad(left, right, rest):
+    return mine.reshape(-1, mine.shape[-1])
+
+
+def send_parts(left, right):
     width = left.shape[1]
-    over_x = swap(dot_tn(left[:, width // 2 :], right).astype(bf16), "x")
-    near = dot_tn(left[:, : width // 2], right) + over_x.astype(f32)
-    far = swap(near[width // 4 :].astype(bf16), "zh")
-    mine = (near[: width // 4] + far.astype(f32)).astype(bf16)
-    mine = mine.reshape(4, width // 16, -1)
+    part = lambda a, b: dot_tn(left[:, a * width // 4 : b * width // 4], right).astype(bf16)
+    return part(3, 4), part(2, 3)
+
+
+def far_part(left, right, got):
+    width = left.shape[1]
+    return (dot_tn(left[:, width // 4 : width // 2], right) + got.astype(f32)).astype(bf16)
+
+
+def own_part(left, right, got, far, rest):
+    width = left.shape[1]
+    far = jnp.concatenate(far, axis=0).astype(f32)
+    mine = dot_tn(left[:, : width // 4], right) + got.astype(f32) + far
+    mine = mine.astype(bf16).reshape(4, width // 16, -1)
     if rest > 1:
         mine = lax.psum_scatter(mine, "r", scatter_dimension=1, tiled=True)
-    return exchange(mine)
+    return mine
 
 
 fix_one = 1.0 - beta_one**STEP
@@ -311,13 +331,14 @@
 def adam(kernel, grid, got, got_spec, spec, weight, first, second, name):
     out = jax.ShapeDtypeStruct(weight.shape, f32)
     size = math.prod(weight.shape) * 28
+    cost = pl.CostEstimate(flops=size // 2, bytes_accessed=size, transcendentals=0)
     return pl.pallas_call(
         kernel,
         grid=grid,
         in_specs=[got_spec, spec, spec, spec],
         out_specs=[spec] * 4,
         out_shape=[out] * 4,
-        cost_estimate=pl.CostEstimate(flops=size // 2, bytes_accessed=size, transcendentals=0),
+        cost_estimate=cost,
         compiler_params=pltpu.CompilerParams(vmem_limit_bytes=40 * 1024 * 1024),
         name=name,
     )(got, weight, first, second)
@@ -461,6 +482,7 @@
         ],
         out_specs=block_spec(half, heads_q * HEAD_SIZE),
         out_shape=jax.ShapeDtypeStruct((2, seqs, half, heads_q * HEAD_SIZE), bf16),
+        cost_estimate=FREE,
         compiler_params=pltpu.CompilerParams(vmem_limit_bytes=32 * 1024 * 1024),
         name="attend",
     )(shift, proj, cosine, sine, gains)
@@ -484,6 +506,7 @@
             jax.ShapeDtypeStruct((2, seqs, half, columns), bf16),
             jax.ShapeDtypeStruct((2, HEAD_SIZE), f32),
         ],
+        cost_estimate=FREE,
         compiler_params=pltpu.CompilerParams(vmem_limit_bytes=32 * 1024 * 1024),
         name="attend_back",
     )(shift, proj, d_att, cosine, sine, gains)
@@ -527,12 +550,42 @@
         place, tokens, cotangent, norm_gains.astype(f32),
         name="start",
     )
-    attention = gather_weight(pack_attention(weight_qkv, weight_out, wide_q, wide_kv), rest)
-    own_qkv, own_out = attention[:, :wide_qkv], attention[:, wide_qkv:]
-    normed_one = gather_rows(normed_own)
-    own_gate_up = gather_weight(pack_columns(weight_gate_up, hidden), rest)
-    own_down = gather_weight(pack_turned(weight_down, hidden), rest)
-    cotangent_all = gather_rows(own_cotangent)
+    together = lax.optimization_barrier
+    side = lambda value: swap(value, "x")
+    block = own_block(pack_attention(weight_qkv, weight_out, wide_q, wide_kv), rest)
+    own, over_zl, over_y = normed_own, swap(normed_own, "zl"), swap(normed_own, "y")
+    own, over_zl, over_y, block, packed = together(
+        (own, over_zl, over_y, block, pack_columns(weight_gate_up, hidden))
+    )
+    block_qkv, block_out = block[:, :wide_qkv], block[:, wide_qkv:]
+    block_gu = own_block(packed, rest)
+    far_qkv, side_qkv, over_both = swap(block_qkv, "zh"), side(block_qkv), swap(over_zl, "y")
+    far_qkv, side_qkv, over_both, block_out, packed = together(
+        (far_qkv, side_qkv, over_both, block_out, pack_turned(weight_down, hidden))
+    )
+    both_qkv, far_out, side_out = side(far_qkv), swap(block_out, "zh"), side(block_out)
+    half_one = join(own, over_y, over_zl, over_both)
+    half_two = swap(half_one, "c")
+    both_qkv, far_out, side_out, half_one, half_two, block_gu, packed, own_cotangent = together(
+        (both_qkv, far_out, side_out, half_one, half_two, block_gu, packed, own_cotangent)
+    )
+    normed_one = join(half_one, half_two)
+    both_out = side(far_out)
+    cotangent_zl, cotangent_y = swap(own_cotangent, "zl"), swap(own_cotangent, "y")
+    block_down = own_block(packed, rest)
+    side_gu, side_down = side(block_gu), side(block_down)
+    far_gu = [swap(part, "zh") for part in rows_of(block_gu, 2)]
+    far_down = [swap(block_down, "zh")]
+    both_gu = [side(part) for part in far_gu]
+    both_down = [side(part) for part in far_down]
+    own_qkv = jnp.concatenate([block_qkv, far_qkv, side_qkv, both_qkv], axis=0)
+    own_out = jnp.concatenate([block_out, far_out, side_out, both_out], axis=0)
+    own_gate_up = jnp.concatenate([block_gu, *far_gu, side_gu, *both_gu], axis=0)
+    own_down = jnp.concatenate([block_down, *far_down, side_down, *both_down], axis=0)
+
+    cotangent_both = swap(cotangent_zl, "y")
+    cotangent_half = join(own_cotangent, cotangent_y, cotangent_zl, cotangent_both)
+    cotangent_all = join(cotangent_half, swap(cotangent_half, "c"))
 
     core = lax.axis_index("c")
     shift = (core * half).astype(jnp.int32)
@@ -546,42 +599,54 @@
     projected = dot(normed_one, own_qkv)
     projected = projected.reshape(2, 4, half, wide_qkv)
     attended = attend(projected, shift, cosine, sine, head_rows, heads_q, heads_kv)
-    attended = attended.reshape(-1, wide_q)
+    attended = after(attended.reshape(-1, wide_q), far_gu[0], cotangent_zl, cotangent_y, block_down)
     middle, normed_own = vmem_call(
         middle_kernel,
         [shape(half, width, f32), shape(half, width, bf16)],
-        place, *sum_rows(attended, own_out), inputs, own_gains,
+        place,
+        *sum_rows(attended, own_out, (cotangent_both,), (far_gu[1], side_gu)),
+        inputs, after(own_gains, both_gu[0], cotangent_all),
         name="middle",
     )
 
-    normed_two = gather_rows(normed_own)
+    normed_two = gather_rows(
+        normed_own, at_send=(*far_down, side_down), at_half=(both_gu[1],)
+    )
     gate_up = dot(normed_two, own_gate_up)
     gate, up = gate_up[:, :hidden], gate_up[:, hidden:]
     sigmoid_gate = jax.nn.sigmoid(gate)
     activation = (gate * sigmoid_gate * up).astype(bf16)
-    output = vmem_call(
-        output_kernel,
-        shape(half, width, bf16),
-        place, *sum_rows(activation, own_down), middle,
-        name="output",
-    )
-
-    grad_act = dot(cotangent_all, own_down)
+    parts = send_parts(cotangent_all, activation)
+    grad_act = dot(after(cotangent_all, parts[0]), own_down)
     grad_gate = grad_act * up * sigmoid_gate * (1.0 + gate * (1.0 - sigmoid_gate))
     grad_up = grad_act * gate * sigmoid_gate
     d_gate_up = jnp.concatenate([grad_gate, grad_up], axis=1).astype(bf16)
+
+    side_far, side_near = map(side, parts)
+    far = far_part(cotangent_all, activation, side_far)
+    far_down = [swap(far, "zh")]
+    side_far_gu, side_near_gu = map(side, send_parts(normed_two, d_gate_up))
+    far = far_part(normed_two, d_gate_up, side_far_gu)
+    far_rows = far
+    far_gu = [swap(part, "zh") for part in rows_of(far, 2)]
+
     grad_middle, branch_own, gain_two_grad = vmem_call(
         back_two_kernel,
         [shape(half, width, f32), shape(half, width, bf16), shape(1, width, f32)],
-        place, *sum_rows(d_gate_up, own_gate_up), middle, own_cotangent, own_gains,
+        place,
+        *sum_rows(d_gate_up, own_gate_up, (side_far,), (far_down[0],)),
+        middle, own_cotangent, after(own_gains, side_far_gu),
         name="back_two",
     )
-    d_branch = gather_rows(branch_own)
-    grad_down = scatter_grad(cotangent_all, activation, rest)
-    grad_gate_up = scatter_grad(normed_two, d_gate_up, rest)
-
-    d_attended = dot(d_branch, own_out).astype(bf16)
-    grad_out = scatter_grad(d_branch, attended, rest)
+    base, near, far = sum_rows(activation, own_down)
+    output = vmem_call(
+        output_kernel, shape(half, width, bf16), place, base, near, far, middle, name="output"
+    )
+    d_branch = gather_rows(branch_own, at_send=(far_rows,), at_half=(side_near, far_gu[0]))
+    grad_down = exchange(own_part(cotangent_all, activation, side_near, far_down, rest))
+    new_down = adam_turned(grad_down, weight_down, first_down, second_down, hidden)
+
+    d_attended = after(dot(d_branch, own_out).astype(bf16), output, grad_down)
     d_projected, head_grad = attend_back(
         projected,
         d_attended.reshape(2, 4, half, wide_q),
@@ -592,17 +657,34 @@
         heads_q,
         heads_kv,
     )
-    d_projected = d_projected.reshape(-1, wide_qkv)
+    d_projected = after(d_projected.reshape(-1, wide_qkv), far_gu[1])
+    side_far_out, side_near_out = map(side, send_parts(d_branch, attended))
+    far_out = swap(far_part(d_branch, attended, side_far_out), "zh")
+    side_far_qkv, side_near_qkv = map(side, send_parts(normed_one, d_projected))
+    far_qkv = swap(far_part(normed_one, d_projected, side_far_qkv), "zh")
+
+    grad_gate_up = own_part(normed_two, d_gate_up, side_near_gu, far_gu, rest)
+    terms = sum_rows(
+        d_projected, own_qkv, at_far=(grad_gate_up, side_far_qkv, side_far_out)
+    )
+    grad_gate_up = exchange(grad_gate_up)
+    new_gate_up = adam_columns(grad_gate_up, weight_gate_up, first_gate_up, second_gate_up, hidden)
+    grad_out = exchange(own_part(d_branch, attended, side_near_out, [far_out], rest))
+    new_out = adam_turned(grad_out, weight_out, first_out, second_out, wide_q)
+    grad_qkv = exchange(own_part(normed_one, d_projected, side_near_qkv, [far_qkv], rest))
+    new_qkv = adam_qkv(grad_qkv, weight_qkv, first_qkv, second_qkv, wide_q, wide_kv)
     input_grad, gain_grads = vmem_call(
         back_one_kernel,
         [shape(half, width, f32), shape(2, width, f32)],
-        place, *sum_rows(d_projected, own_qkv), inputs, grad_middle, own_gains, gain_two_grad,
+        place, *terms, inputs, grad_middle, after(own_gains, far_out, new_down[3]), gain_two_grad,
         name="back_one",
     )
-    grad_qkv = scatter_grad(normed_one, d_projected, rest)
 
     sums = jnp.concatenate([gain_grads, head_grad], axis=1)
-    for axis in ("c", "x", "y", "zl", "zh"):
+    sums = sums + swap(sums, "c")
+    sums = sums + swap(after(sums, new_gate_up[3]), "x")
+    sums = sums + swap(after(sums, new_out[3]), "y")
+    for axis in ("zl", "zh"):
         sums = sums + swap(sums, axis)
     if rest > 1:
         sums = lax.psum(sums, "r")
@@ -616,10 +698,10 @@
     return (
         output,
         input_grad,
-        *adam_qkv(grad_qkv, weight_qkv, first_qkv, second_qkv, wide_q, wide_kv),
-        *adam_turned(grad_out, weight_out, first_out, second_out, wide_q),
-        *adam_columns(grad_gate_up, weight_gate_up, first_gate_up, second_gate_up, hidden),
-        *adam_turned(grad_down, weight_down, first_down, second_down, hidden),
+        *new_qkv,
+        *new_out,
+        *new_gate_up,
+        *new_down,
         *step(norm_gains, grad_norm, first_norm, second_norm),
         *step(head_gains, grad_head, first_head, second_head),
     )

time: 678 us -> 572 us (0.84)
  waiting for transfers between devices: 389 us -> 259 us
  local copies, waits for them, and re-layouts: 16.2 us -> 39.9 us
  starting transfers between devices: 93 us -> 106 us
  Pallas kernels: 64.3 us -> 54.3 us
    ppermute x54 -> x64, waiting for transfers between devices: 374 us -> 259 us  [swap(): return lax.ppermute(value, axis, SWAP)]
    unnamed x129 -> x181, local copies, waits for them, and re-layouts: 9.41 us -> 31.5 us
    all_to_all x7, waiting for transfers between devices: 15.4 us -> 0.02 us  [exchange(): return lax.all_to_all(pieces, ('zl', 'y'), 0, 0, tiled=True)]
    ppermute x54 -> x64, starting transfers between devices: 63.5 us -> 75.9 us  [swap(): return lax.ppermute(value, axis, SWAP)]
    dot_general x8 -> x16, matrix products: 28 us -> 37.6 us  [dot_tn(): lax.dot_general(left, right, (((0,), (0,)), ((), ())), preferred_element_...]
    pallas_call x8, Pallas kernels: 18.3 us -> 11.3 us  [join(): pl.pallas_call(functools.partial(join_kernel, len(parts)), in_specs=[pl.B...]
  transfers between devices with their start and end apart: 61 -> 71, of which waited for: 34 -> 28; matrix products, arithmetic and copies ran while one was open for 13% -> 17% of each run, Pallas kernels for 8% -> 9%
where the time goes in v2:
time: 572 us; the launch traced here: 562 us
  waiting for transfers between devices  259 us (45%)
  starting transfers between devices  106 us (19%)
  matrix products  92.1 us (16%)
  Pallas kernels  54.3 us (9%)
  local copies, waits for them, and re-layouts  39.9 us (7%)
  other arithmetic  9.27 us (2%)
    ppermute x64, waiting for transfers between devices, swap(): return lax.ppermute(value, axis, SWAP)  259 us
    ppermute x64, starting transfers between devices, swap(): return lax.ppermute(value, axis, SWAP)  75.9 us
    dot_general x16, matrix products, dot_tn(): lax.dot_general(left, right, (((0,), (0,)), ((), ())), preferred_element_...  37.6 us
    dot_general x8, matrix products, dot_nt(): lax.dot_general(left, right, (((1,), (1,)), ((), ())), preferred_element_...  34.2 us
    unnamed x181, local copies, waits for them, and re-layouts  31.5 us
    all_to_all x7, starting transfers between devices, exchange(): return lax.all_to_all(pieces, ('zl', 'y'), 0, 0, tiled=True)  29.8 us
    dot_general x4, matrix products, dot(): return jnp.dot(left, right, preferred_element_type=f32)  20.3 us
    pallas_call x4, Pallas kernels, adam(): pl.pallas_call(kernel, grid=grid, in_specs=[got_spec, spec, spec, spec],...  15.2 us
  transfers between devices with their start and end apart: 71, of which 28 were waited for; matrix products, arithmetic and copies ran while one was open for 17% of the time, Pallas kernels for 9%

profile of v2, /device:TPU:0, one launch (start us, length us, event | category | flops | bytes accessed | tf_op | source)
XLA Modules:
  0.0 562.3 jit_solution(7630089068937923464)
XLA Ops:
  3.8 5.2 all-to-all-start
  17.1 14.7 %collective-permute-done.refs_2_ = bf16[128,2048]{1,0:T(8,128)(2,1)} collective-permute-done((bf16[128,2048]{1,0:T(8,128)(2,1)S(1)}, bf16[128,2048]{1,0:T(8,128)(2,1)}, u32[]{:S(2)}, u32[]{:S(2)}) %collective-permute-start) | collective-permute-done | bytes 524320 | tf_op jit(solution)/shard_map/ppermute | solution.py:44
  40.1 4.4 all-to-all-start.1
  47.3 12.6 %collective-permute-done.2 = bf16[512,512]{1,0:T(8,128)(2,1)} collective-permute-done((bf16[512,512]{1,0:T(8,128)(2,1)}, bf16[512,512]{1,0:T(8,128)(2,1)}, u32[]{:S(2)}, u32[]{:S(2)}) %collective-permute-start.2) | collective-permute-done | bytes 524320 | tf_op jit(solution)/shard_map/ppermute | solution.py:44
  70.9 10.5 %collective-permute-done.6 = bf16[512,256]{1,0:T(8,128)(2,1)} collective-permute-done((bf16[512,256]{1,0:T(8,128)(2,1)S(1)}, bf16[512,256]{1,0:T(8,128)(2,1)}, u32[]{:S(2)}, u32[]{:S(2)}) %collective-permute-start.6) | collective-permute-done | bytes 262176 | tf_op jit(solution)/shard_map/ppermute | solution.py:44
  81.4 3.6 collective-permute-done.7
  85.7 3.6 collective-permute-start.10
  90.0 4.2 all-to-all-start.2
  101.4 5.4 fusion.47
  106.8 6.0 %attend.1 = bf16[2,4,128,256]{3,2,1,0:T(8,128)(2,1)S(1)} custom-call(s32[1]{0:T(128)} %bitcast.2.shift_ref, f32[2,4,128,512]{3,2,1,0:T(8,128)S(1)} %bitcast.36, f32[256,128]{1,0:T(8,128)S(1)} %get-tuple-element.197.cos_ref, f32[256,128]{1,0:T(8,128)S(1)} %get-tuple-element.198.sin_ref, f32[2,128]{1,0:T(2,128)S(1)} %convert_element_type.164.gain_ref), custom_call_target="tpu_custom_call" | custom-call | tf_op jit(solution)/shard_map/attend/pallas_call | solution.py:473
  116.3 16.7 %collective-permute-done.9 = bf16[256,1536]{1,0:T(8,128)(2,1)} collective-permute-done((bf16[256,1536]{1,0:T(8,128)(2,1)S(1)}, bf16[256,1536]{1,0:T(8,128)(2,1)}, u32[]{:S(2)}, u32[]{:S(2)}) %collective-permute-start.9) | collective-permute-done | bytes 786464 | tf_op jit(solution)/shard_map/ppermute | solution.py:44
  137.6 12.2 %collective-permute-done.14.refs_3_ = bf16[128,2048]{1,0:T(8,128)(2,1)S(1)} collective-permute-done((bf16[128,2048]{1,0:T(8,128)(2,1)}, bf16[128,2048]{1,0:T(8,128)(2,1)S(1)}, u32[]{:S(2)}, u32[]{:S(2)}) %collective-permute-start.14) | collective-permute-done | bytes 524320 | tf_op jit(solution)/shard_map/ppermute | solution.py:44
  155.3 19.4 %collective-permute-done.17 = bf16[256,1536]{1,0:T(8,128)(2,1)S(1)} collective-permute-done((bf16[256,1536]{1,0:T(8,128)(2,1)S(1)}, bf16[256,1536]{1,0:T(8,128)(2,1)S(1)}, u32[]{:S(2)}, u32[]{:S(2)}) %collective-permute-start.17) | collective-permute-done | bytes 786464 | tf_op jit(solution)/shard_map/ppermute | solution.py:44
  179.1 12.3 %collective-permute-done.20 = bf16[256,1536]{1,0:T(8,128)(2,1)S(1)} collective-permute-done((bf16[256,1536]{1,0:T(8,128)(2,1)}, bf16[256,1536]{1,0:T(8,128)(2,1)S(1)}, u32[]{:S(2)}, u32[]{:S(2)}) %collective-permute-start.20) | collective-permute-done | bytes 786464 | tf_op jit(solution)/shard_map/ppermute | solution.py:44
  191.4 7.1 %collective-permute-done.19.far = bf16[128,2048]{1,0:T(8,128)(2,1)S(1)} collective-permute-done((bf16[128,2048]{1,0:T(8,128)(2,1)S(1)}, bf16[128,2048]{1,0:T(8,128)(2,1)S(1)}, u32[]{:S(2)}, u32[]{:S(2)}) %collective-permute-start.19) | collective-permute-done | bytes 524320 | tf_op jit(solution)/shard_map/ppermute | solution.py:44
  202.8 9.7 %collective-permute-done.25 = bf16[512,768]{1,0:T(8,128)(2,1)} collective-permute-done((bf16[512,768]{1,0:T(8,128)(2,1)}, bf16[512,768]{1,0:T(8,128)(2,1)}, u32[]{:S(2)}, u32[]{:S(2)}) %collective-permute-start.25) | collective-permute-done | bytes 786464 | tf_op jit(solution)/shard_map/ppermute | solution.py:44
  212.5 6.7 %collective-permute-done.24.refs_2_ = bf16[128,2048]{1,0:T(8,128)(2,1)S(1)} collective-permute-done((bf16[128,2048]{1,0:T(8,128)(2,1)S(1)}, bf16[128,2048]{1,0:T(8,128)(2,1)S(1)}, u32[]{:S(2)}, u32[]{:S(2)}) %collective-permute-start.24) | collective-permute-done | bytes 524320 | tf_op jit(solution)/shard_map/ppermute | solution.py:44
  220.9 3.3 collective-permute-done.22
  224.3 6.7 %collective-permute-done.27.refs_3_ = bf16[128,2048]{1,0:T(8,128)(2,1)S(1)} collective-permute-done((bf16[128,2048]{1,0:T(8,128)(2,1)S(1)}, bf16[128,2048]{1,0:T(8,128)(2,1)S(1)}, u32[]{:S(2)}, u32[]{:S(2)}) %collective-permute-start.27) | collective-permute-done | bytes 524320 | tf_op jit(solution)/shard_map/ppermute | solution.py:44
  236.9 6.6 %fusion.61 = f32[1024,1536]{1,0:T(8,128)S(1)} fusion(bf16[1024,2048]{1,0:T(8,128)(2,1)S(1)} %join.13, bf16[2048,1536]{1,0:T(8,128)(2,1)S(1)} %constant_dynamic-update-slice_fusion.4), kind=kOutput, calls=%fused_computation.124 | convolution fusion | flops 6442450944 | bytes 16777216 | tf_op jit(solution)/shard_map/dot_general | solution.py:32
  245.4 9.0 %collective-permute-done.29 = bf16[512,768]{1,0:T(8,128)(2,1)S(1)} collective-permute-done((bf16[512,768]{1,0:T(8,128)(2,1)}, bf16[512,768]{1,0:T(8,128)(2,1)S(1)}, u32[]{:S(2)}, u32[]{:S(2)}) %collective-permute-start.29) | collective-permute-done | bytes 786464 | tf_op jit(solution)/shard_map/ppermute | solution.py:44
  254.5 7.0 %multiply_convert_fusion = (bf16[1024,768]{1,0:T(8,128)(2,1)S(1)}, bf16[1024,768]{1,0:T(8,128)(2,1)S(1)}) fusion(f32[1024,1536]{1,0:T(8,128)S(1)} %fusion.61, bf16[1024,2048]{1,0:T(8,128)(2,1)S(1)} %join.11, bf16[512,768]{1,0:T(8,128)(2,1)S(1)} %collective-permute-done.29, bf16[512,768]{1,0:T(8,128)(2,1)S(1)} %copy-done.71, ...), kind=kOutput, calls=%fused_computation.13 | convolution fusion | flops 3244032000 | bytes 16777216 | tf_op jit(solution)/shard_map/dot_general | solution.py:32
  262.7 6.4 %convolution_convert_fusion.4 = bf16[512,2048]{1,0:T(8,128)(2,1)S(1)} fusion(bf16[2048,1536]{1,0:T(8,128)(2,1)} %copy-done.59, bf16[1024,768]{1,0:T(8,128)(2,1)S(1)} %get-tuple-element.167, bf16[1024,768]{1,0:T(8,128)(2,1)S(1)} %get-tuple-element.166), kind=kOutput, calls=%fused_computation.23 | convolution fusion | flops 3225419776 | bytes 11534336 | tf_op jit(solution)/shard_map/dot_general | solution.py:40
  270.7 4.4 convolution_convert_fusion.3
  275.7 13.9 %collective-permute-done.35 = bf16[512,768]{1,0:T(8,128)(2,1)S(1)} collective-permute-done((bf16[512,768]{1,0:T(8,128)(2,1)S(1)}, bf16[512,768]{1,0:T(8,128)(2,1)S(1)}, u32[]{:S(2)}, u32[]{:S(2)}) %collective-permute-start.35) | collective-permute-done | bytes 786464 | tf_op jit(solution)/shard_map/ppermute | solution.py:44
  291.5 6.2 %fusion.59 = (bf16[512,2048]{1,0:T(8,128)(2,1)S(1)}, f32[512,2048]{1,0:T(8,128)S(1)}) fusion(bf16[512,2048]{1,0:T(8,128)(2,1)S(1)} %collective-permute-done.34, bf16[2048,1536]{1,0:T(8,128)(2,1)} %copy-done.59, bf16[1024,768]{1,0:T(8,128)(2,1)} %copy-done.82, bf16[1024,768]{1,0:T(8,128)(2,1)} %copy-done.78), kind=kOutput, calls=%fused_computation.122 | convolution fusion | flops 3227516928 | bytes 17825792 | tf_op jit(solution)/shard_map/dot_general | solution.py:40
  299.7 3.4 convolution_convert_fusion.5
  303.5 23.7 %collective-permute-done.38 = bf16[512,768]{1,0:T(8,128)(2,1)} collective-permute-done((bf16[512,768]{1,0:T(8,128)(2,1)}, bf16[512,768]{1,0:T(8,128)(2,1)}, u32[]{:S(2)}, u32[]{:S(2)}) %collective-permute-start.38) | collective-permute-done | bytes 786464 | tf_op jit(solution)/shard_map/ppermute | solution.py:44
  334.2 7.2 %collective-permute-done.39.far = bf16[128,2048]{1,0:T(8,128)(2,1)S(1)} collective-permute-done((bf16[128,2048]{1,0:T(8,128)(2,1)S(1)}, bf16[128,2048]{1,0:T(8,128)(2,1)S(1)}, u32[]{:S(2)}, u32[]{:S(2)}) %collective-permute-start.39) | collective-permute-done | bytes 524320 | tf_op jit(solution)/shard_map/ppermute | solution.py:44
  348.4 17.5 %collective-permute-done.44.refs_2_ = bf16[128,2048]{1,0:T(8,128)(2,1)S(1)} collective-permute-done((bf16[128,2048]{1,0:T(8,128)(2,1)S(1)}, bf16[128,2048]{1,0:T(8,128)(2,1)S(1)}, u32[]{:S(2)}, u32[]{:S(2)}) %collective-permute-start.44) | collective-permute-done | bytes 524320 | tf_op jit(solution)/shard_map/ppermute | solution.py:44
  367.7 5.2 fusion.58
  372.8 7.9 %collective-permute-done.42 = bf16[256,1536]{1,0:T(8,128)(2,1)S(1)} collective-permute-done((bf16[256,1536]{1,0:T(8,128)(2,1)S(1)}, bf16[256,1536]{1,0:T(8,128)(2,1)S(1)}, u32[]{:S(2)}, u32[]{:S(2)}) %collective-permute-start.42) | collective-permute-done | bytes 786464 | tf_op jit(solution)/shard_map/ppermute | solution.py:44
  389.7 3.3 add_convert_fusion
  393.1 3.7 all-to-all-start.3
  402.3 4.3 collective-permute-start.47
  406.6 12.5 %collective-permute-done.31.near = bf16[128,2048]{1,0:T(8,128)(2,1)S(1)} collective-permute-done((bf16[128,2048]{1,0:T(8,128)(2,1)}, bf16[128,2048]{1,0:T(8,128)(2,1)S(1)}, u32[]{:S(2)}, u32[]{:S(2)}) %collective-permute-start.31) | collective-permute-done | bytes 524320 | tf_op jit(solution)/shard_map/ppermute | solution.py:44
  419.2 13.2 %collective-permute-done.33.far = bf16[128,2048]{1,0:T(8,128)(2,1)S(1)} collective-permute-done((bf16[128,2048]{1,0:T(8,128)(2,1)S(1)}, bf16[128,2048]{1,0:T(8,128)(2,1)S(1)}, u32[]{:S(2)}, u32[]{:S(2)}) %collective-permute-start.33) | collective-permute-done | bytes 524320 | tf_op jit(solution)/shard_map/ppermute | solution.py:44
  441.5 8.8 %attend_back.1 = (bf16[2,4,128,512]{3,2,1,0:T(8,128)(2,1)S(1)}, f32[2,128]{1,0:T(2,128)S(1)}) custom-call(s32[1]{0:T(128)} %bitcast.2.shift_ref, f32[2,4,128,512]{3,2,1,0:T(8,128)S(1)} %bitcast.37, bf16[2,4,128,256]{3,2,1,0:T(8,128)(2,1)S(1)} %bitcast.44, f32[256,128]{1,0:T(8,128)S(1)} %get-tuple-element.197.cos_ref, f32[256,128]{1,0:T(8,128)S(1)} %copy-done.27, ...), custom_call_target="tpu_custom_call" | custom-call | tf_op jit(solution)/shard_map/attend_back/pallas_call | solution.py:493
  450.4 4.5 convolution_convert_fusion.2
  455.0 4.8 fusion.2
  459.8 3.6 all-to-all-start.6
  475.8 5.6 fusion.60
  496.2 4.2 all-to-all-start.5
  505.5 7.5 %collective-permute-done.57 = bf16[512,512]{1,0:T(8,128)(2,1)} collective-permute-done((bf16[512,512]{1,0:T(8,128)(2,1)}, bf16[512,512]{1,0:T(8,128)(2,1)}, u32[]{:S(2)}, u32[]{:S(2)}) %collective-permute-start.57) | collective-permute-done | bytes 524320 | tf_op jit(solution)/shard_map/ppermute | solution.py:44
  516.1 4.5 all-to-all-start.4
  525.7 3.5 adam_turned.2
  535.8 6.2 %adam_columns.1 = (f32[128,6144]{1,0:T(8,128)}, f32[128,6144]{1,0:T(8,128)}, f32[128,6144]{1,0:T(8,128)}, f32[128,6144]{1,0:T(8,128)}) custom-call(bf16[4,128,1536]{2,1,0:T(8,128)(2,1)S(1)} %all-to-all-done.6.got, bf16[128,6144]{1,0:T(8,128)(2,1)S(1)} %copy-done, f32[128,6144]{1,0:T(8,128)S(1)} %copy-done.13, f32[128,6144]{1,0:T(8,128)S(1)} %copy-done.14), custom_call_target="tpu_custom_call" | custom-call | flops 11010048 | bytes 22020096 | tf_op jit(solution)/shard_map/adam_columns/pallas_call | solution.py:335
  557.2 3.4 adam_qkv.1
  (356 shorter events, 183.3 us)
Async XLA Ops:
  3.8 28.7 %all-to-all-start = ((bf16[4,128,768]{2,1,0:T(8,128)(2,1)}), bf16[4,128,768]{2,1,0:T(8,128)(2,1)}, u32[]{:S(2)}, u32[]{:S(2)}) async-start(bf16[4,128,768]{2,1,0:T(8,128)(2,1)} %pack_attention.1), calls=%async_computation | async-start | bytes 1572864 | tf_op jit(solution)/shard_map/all_to_all | solution.py:267
  11.0 20.7 %collective-permute-start = (bf16[128,2048]{1,0:T(8,128)(2,1)S(1)}, bf16[128,2048]{1,0:T(8,128)(2,1)}, u32[]{:S(2)}, u32[]{:S(2)}) collective-permute-start(bf16[128,2048]{1,0:T(8,128)(2,1)S(1)} %get-tuple-element.96.refs_0_), channel_id=1, source_target_pairs={{0,8},{8,0},{1,9},{9,1},{2,10},{10,2},{3,11},{11,3},{4,12},{12,4},... | collective-permute-start | bytes 1572872 | tf_op jit(solution)/shard_map/ppermute | solution.py:44
  34.4 25.6 %collective-permute-start.2 = (bf16[512,512]{1,0:T(8,128)(2,1)}, bf16[512,512]{1,0:T(8,128)(2,1)}, u32[]{:S(2)}, u32[]{:S(2)}) collective-permute-start(bf16[512,512]{1,0:T(8,128)(2,1)} %slice.158), channel_id=1, source_target_pairs={{0,16},{16,0},{1,17},{17,1},{2,18},{18,2},{3,19},{19,3},{4,20},{20... | collective-permute-start | bytes 1572872 | tf_op jit(solution)/shard_map/ppermute | solution.py:44
  37.1 22.9 %collective-permute-start.3 = (bf16[512,512]{1,0:T(8,128)(2,1)}, bf16[512,512]{1,0:T(8,128)(2,1)}, u32[]{:S(2)}, u32[]{:S(2)}) collective-permute-start(bf16[512,512]{1,0:T(8,128)(2,1)} %slice.158), channel_id=1, source_target_pairs={{0,2},{2,0},{1,3},{3,1},{4,6},{6,4},{5,7},{7,5},{8,10},{10,8},{9,1... | collective-permute-start | bytes 1572872 | tf_op jit(solution)/shard_map/ppermute | solution.py:44
  38.6 21.4 %collective-permute-start.4 = (bf16[128,2048]{1,0:T(8,128)(2,1)}, bf16[128,2048]{1,0:T(8,128)(2,1)}, u32[]{:S(2)}, u32[]{:S(2)}) collective-permute-start(bf16[128,2048]{1,0:T(8,128)(2,1)} %collective-permute-done.refs_2_), channel_id=1, source_target_pairs={{0,4},{4,0},{1,5},{5,1},{2,6},{6,2},{3,7},{7,3},{8,12},{12,8},{9,1... | collective-permute-start | bytes 1572872 | tf_op jit(solution)/shard_map/ppermute | solution.py:44
  40.1 45.6 %all-to-all-start.1 = ((bf16[4,128,1536]{2,1,0:T(8,128)(2,1)}), bf16[4,128,1536]{2,1,0:T(8,128)(2,1)}, u32[]{:S(2)}, u32[]{:S(2)}) async-start(bf16[4,128,1536]{2,1,0:T(8,128)(2,1)} %pack_columns.1), calls=%async_computation.1 | async-start | bytes 3145728 | tf_op jit(solution)/shard_map/all_to_all | solution.py:267
  64.7 21.0 %collective-permute-start.8 = (bf16[512,2048]{1,0:T(8,128)(2,1)}, bf16[512,2048]{1,0:T(8,128)(2,1)}, u32[]{:S(2)}, u32[]{:S(2)}) collective-permute-start(bf16[512,2048]{1,0:T(8,128)(2,1)} %join.8.refs_0_), channel_id=1, source_target_pairs={{0,1},{1,0},{2,3},{3,2},{4,5},{5,4},{6,7},{7,6},{8,9},{9,8},{10,11... | collective-permute-start | bytes 6291464 | tf_op jit(solution)/shard_map/ppermute | solution.py:44
  64.8 20.9 %collective-permute-start.5 = (bf16[512,512]{1,0:T(8,128)(2,1)}, bf16[512,512]{1,0:T(8,128)(2,1)}, u32[]{:S(2)}, u32[]{:S(2)}) collective-permute-start(bf16[512,512]{1,0:T(8,128)(2,1)} %collective-permute-done.2), channel_id=1, source_target_pairs={{0,2},{2,0},{1,3},{3,1},{4,6},{6,4},{5,7},{7,5},{8,10},{10,8},{9,1... | collective-permute-start | bytes 1572872 | tf_op jit(solution)/shard_map/ppermute | solution.py:44
  85.7 29.7 %collective-permute-start.10 = (bf16[128,2048]{1,0:T(8,128)(2,1)S(1)}, bf16[128,2048]{1,0:T(8,128)(2,1)}, u32[]{:S(2)}, u32[]{:S(2)}) collective-permute-start(bf16[128,2048]{1,0:T(8,128)(2,1)S(1)} %copy-done.20), channel_id=1, source_target_pairs={{0,8},{8,0},{1,9},{9,1},{2,10},{10,2},{3,11},{11,3},{4,12},{12,4},... | collective-permute-start | bytes 1572872 | tf_op jit(solution)/shard_map/ppermute | solution.py:44
  89.3 26.1 %collective-permute-start.11 = (bf16[128,2048]{1,0:T(8,128)(2,1)S(1)}, bf16[128,2048]{1,0:T(8,128)(2,1)}, u32[]{:S(2)}, u32[]{:S(2)}) collective-permute-start(bf16[128,2048]{1,0:T(8,128)(2,1)S(1)} %copy-done.20), channel_id=1, source_target_pairs={{0,4},{4,0},{1,5},{5,1},{2,6},{6,2},{3,7},{7,3},{8,12},{12,8},{9,1... | collective-permute-start | bytes 1572872 | tf_op jit(solution)/shard_map/ppermute | solution.py:44
  90.0 43.0 %all-to-all-start.2 = ((bf16[4,128,768]{2,1,0:T(8,128)(2,1)}), bf16[4,128,768]{2,1,0:T(8,128)(2,1)}, u32[]{:S(2)}, u32[]{:S(2)}) async-start(bf16[4,128,768]{2,1,0:T(8,128)(2,1)} %pack_turned.1), calls=%async_computation.2 | async-start | bytes 1572864 | tf_op jit(solution)/shard_map/all_to_all | solution.py:267
  96.6 36.5 %collective-permute-start.9 = (bf16[256,1536]{1,0:T(8,128)(2,1)S(1)}, bf16[256,1536]{1,0:T(8,128)(2,1)}, u32[]{:S(2)}, u32[]{:S(2)}) collective-permute-start(bf16[256,1536]{1,0:T(8,128)(2,1)S(1)} %get-tuple-element.187), channel_id=1, source_target_pairs={{0,16},{16,0},{1,17},{17,1},{2,18},{18,2},{3,19},{19,3},{4,20},{20... | collective-permute-start | bytes 2359304 | tf_op jit(solution)/shard_map/ppermute | solution.py:44
  137.1 38.0 %collective-permute-start.18 = (bf16[512,1536]{1,0:T(8,128)(2,1)}, bf16[512,1536]{1,0:T(8,128)(2,1)S(1)}, u32[]{:S(2)}, u32[]{:S(2)}) collective-permute-start(bf16[512,1536]{1,0:T(8,128)(2,1)} %bitcast.4), channel_id=1, source_target_pairs={{0,2},{2,0},{1,3},{3,1},{4,6},{6,4},{5,7},{7,5},{8,10},{10,8},{9,1... | collective-permute-start | bytes 4718600 | tf_op jit(solution)/shard_map/ppermute | solution.py:44
  137.6 37.1 %collective-permute-start.17 = (bf16[256,1536]{1,0:T(8,128)(2,1)S(1)}, bf16[256,1536]{1,0:T(8,128)(2,1)S(1)}, u32[]{:S(2)}, u32[]{:S(2)}) collective-permute-start(bf16[256,1536]{1,0:T(8,128)(2,1)S(1)} %copy-done.58), channel_id=1, source_target_pairs={{0,16},{16,0},{1,17},{17,1},{2,18},{18,2},{3,19},{19,3},{4,20},{20... | collective-permute-start | bytes 2359304 | tf_op jit(solution)/shard_map/ppermute | solution.py:44
  151.1 26.2 %collective-permute-start.21 = (bf16[512,2048]{1,0:T(8,128)(2,1)S(1)}, bf16[512,2048]{1,0:T(8,128)(2,1)S(1)}, u32[]{:S(2)}, u32[]{:S(2)}) collective-permute-start(bf16[512,2048]{1,0:T(8,128)(2,1)S(1)} %join.10.refs_0_), channel_id=1, source_target_pairs={{0,1},{1,0},{2,3},{3,2},{4,5},{5,4},{6,7},{7,6},{8,9},{9,8},{10,11... | collective-permute-start | bytes 6291464 | tf_op jit(solution)/shard_map/ppermute | solution.py:44
  153.0 22.0 %collective-permute-start.16 = (bf16[128,2048]{1,0:T(8,128)(2,1)S(1)}, bf16[128,2048]{1,0:T(8,128)(2,1)S(1)}, u32[]{:S(2)}, u32[]{:S(2)}) collective-permute-start(bf16[128,2048]{1,0:T(8,128)(2,1)S(1)} %get-tuple-element.182), channel_id=1, source_target_pairs={{0,4},{4,0},{1,5},{5,1},{2,6},{6,2},{3,7},{7,3},{8,12},{12,8},{9,1... | collective-permute-start | bytes 1572872 | tf_op jit(solution)/shard_map/ppermute | solution.py:44
  154.7 36.6 %collective-permute-start.20 = (bf16[256,1536]{1,0:T(8,128)(2,1)}, bf16[256,1536]{1,0:T(8,128)(2,1)S(1)}, u32[]{:S(2)}, u32[]{:S(2)}) collective-permute-start(bf16[256,1536]{1,0:T(8,128)(2,1)} %collective-permute-done.9), channel_id=1, source_target_pairs={{0,2},{2,0},{1,3},{3,1},{4,6},{6,4},{5,7},{7,5},{8,10},{10,8},{9,1... | collective-permute-start | bytes 2359304 | tf_op jit(solution)/shard_map/ppermute | solution.py:44
  175.2 23.2 %collective-permute-start.19 = (bf16[128,2048]{1,0:T(8,128)(2,1)S(1)}, bf16[128,2048]{1,0:T(8,128)(2,1)S(1)}, u32[]{:S(2)}, u32[]{:S(2)}) collective-permute-start(bf16[128,2048]{1,0:T(8,128)(2,1)S(1)} %get-tuple-element.174), channel_id=1, source_target_pairs={{0,8},{8,0},{1,9},{9,1},{2,10},{10,2},{3,11},{11,3},{4,12},{12,4},... | collective-permute-start | bytes 1572872 | tf_op jit(solution)/shard_map/ppermute | solution.py:44
  175.3 37.2 %collective-permute-start.25 = (bf16[512,768]{1,0:T(8,128)(2,1)}, bf16[512,768]{1,0:T(8,128)(2,1)}, u32[]{:S(2)}, u32[]{:S(2)}) collective-permute-start(bf16[512,768]{1,0:T(8,128)(2,1)} %bitcast.7), channel_id=1, source_target_pairs={{0,16},{16,0},{1,17},{17,1},{2,18},{18,2},{3,19},{19,3},{4,20},{20... | collective-permute-start | bytes 2359304 | tf_op jit(solution)/shard_map/ppermute | solution.py:44
  177.3 35.2 %collective-permute-start.26 = (bf16[512,768]{1,0:T(8,128)(2,1)}, bf16[512,768]{1,0:T(8,128)(2,1)S(1)}, u32[]{:S(2)}, u32[]{:S(2)}) collective-permute-start(bf16[512,768]{1,0:T(8,128)(2,1)} %bitcast.7), channel_id=1, source_target_pairs={{0,2},{2,0},{1,3},{3,1},{4,6},{6,4},{5,7},{7,5},{8,10},{10,8},{9,1... | collective-permute-start | bytes 2359304 | tf_op jit(solution)/shard_map/ppermute | solution.py:44
  199.5 24.8 %collective-permute-start.22 = (bf16[256,1536]{1,0:T(8,128)(2,1)S(1)}, bf16[256,1536]{1,0:T(8,128)(2,1)S(1)}, u32[]{:S(2)}, u32[]{:S(2)}) collective-permute-start(bf16[256,1536]{1,0:T(8,128)(2,1)S(1)} %collective-permute-done.17), channel_id=1, source_target_pairs={{0,2},{2,0},{1,3},{3,1},{4,6},{6,4},{5,7},{7,5},{8,10},{10,8},{9,1... | collective-permute-start | bytes 2359304 | tf_op jit(solution)/shard_map/ppermute | solution.py:44
  201.1 23.2 %collective-permute-start.23 = (bf16[128,2048]{1,0:T(8,128)(2,1)S(1)}, bf16[128,2048]{1,0:T(8,128)(2,1)S(1)}, u32[]{:S(2)}, u32[]{:S(2)}) collective-permute-start(bf16[128,2048]{1,0:T(8,128)(2,1)S(1)} %get-tuple-element.118.refs_0_), channel_id=1, source_target_pairs={{0,4},{4,0},{1,5},{5,1},{2,6},{6,2},{3,7},{7,3},{8,12},{12,8},{9,1... | collective-permute-start | bytes 1572872 | tf_op jit(solution)/shard_map/ppermute | solution.py:44
  234.3 20.2 %collective-permute-start.29 = (bf16[512,768]{1,0:T(8,128)(2,1)}, bf16[512,768]{1,0:T(8,128)(2,1)S(1)}, u32[]{:S(2)}, u32[]{:S(2)}) collective-permute-start(bf16[512,768]{1,0:T(8,128)(2,1)} %collective-permute-done.25), channel_id=1, source_target_pairs={{0,2},{2,0},{1,3},{3,1},{4,6},{6,4},{5,7},{7,5},{8,10},{10,8},{9,1... | collective-permute-start | bytes 2359304 | tf_op jit(solution)/shard_map/ppermute | solution.py:44
  269.1 22.4 %collective-permute-start.34 = (bf16[512,2048]{1,0:T(8,128)(2,1)S(1)}, bf16[512,2048]{1,0:T(8,128)(2,1)S(1)}, u32[]{:S(2)}, u32[]{:S(2)}) collective-permute-start(bf16[512,2048]{1,0:T(8,128)(2,1)S(1)} %convolution_convert_fusion.4), channel_id=1, source_target_pairs={{0,1},{1,0},{2,3},{3,2},{4,5},{5,4},{6,7},{7,6},{8,9},{9,8},{10,11... | collective-permute-start | bytes 6291464 | tf_op jit(solution)/shard_map/ppermute | solution.py:44
  269.2 20.4 %collective-permute-start.35 = (bf16[512,768]{1,0:T(8,128)(2,1)S(1)}, bf16[512,768]{1,0:T(8,128)(2,1)S(1)}, u32[]{:S(2)}, u32[]{:S(2)}) collective-permute-start(bf16[512,768]{1,0:T(8,128)(2,1)S(1)} %convolution_convert_fusion.7), channel_id=1, source_target_pairs={{0,2},{2,0},{1,3},{3,1},{4,6},{6,4},{5,7},{7,5},{8,10},{10,8},{9,1... | collective-permute-start | bytes 2359304 | tf_op jit(solution)/shard_map/ppermute | solution.py:44
  275.1 55.8 %collective-permute-start.40 = (bf16[512,1536]{1,0:T(8,128)(2,1)}, bf16[512,1536]{1,0:T(8,128)(2,1)}, u32[]{:S(2)}, u32[]{:S(2)}) collective-permute-start(bf16[512,1536]{1,0:T(8,128)(2,1)} %convolution_convert_fusion.3), channel_id=1, source_target_pairs={{0,2},{2,0},{1,3},{3,1},{4,6},{6,4},{5,7},{7,5},{8,10},{10,8},{9,1... | collective-permute-start | bytes 4718600 | tf_op jit(solution)/shard_map/ppermute | solution.py:44
  291.5 35.7 %collective-permute-start.38 = (bf16[512,768]{1,0:T(8,128)(2,1)}, bf16[512,768]{1,0:T(8,128)(2,1)}, u32[]{:S(2)}, u32[]{:S(2)}) collective-permute-start(bf16[512,768]{1,0:T(8,128)(2,1)} %add_convert_fusion.1), channel_id=1, source_target_pairs={{0,16},{16,0},{1,17},{17,1},{2,18},{18,2},{3,19},{19,3},{4,20},{20... | collective-permute-start | bytes 2359304 | tf_op jit(solution)/shard_map/ppermute | solution.py:44
  297.9 29.4 %collective-permute-start.37 = (bf16[128,2048]{1,0:T(8,128)(2,1)S(1)}, bf16[128,2048]{1,0:T(8,128)(2,1)S(1)}, u32[]{:S(2)}, u32[]{:S(2)}) collective-permute-start(bf16[128,2048]{1,0:T(8,128)(2,1)S(1)} %get-tuple-element.178), channel_id=1, source_target_pairs={{0,4},{4,0},{1,5},{5,1},{2,6},{6,2},{3,7},{7,3},{8,12},{12,8},{9,1... | collective-permute-start | bytes 1572872 | tf_op jit(solution)/shard_map/ppermute | solution.py:44
  303.1 43.6 %collective-permute-start.30 = (bf16[512,2048]{1,0:T(8,128)(2,1)S(1)}, bf16[512,2048]{1,0:T(8,128)(2,1)S(1)}, u32[]{:S(2)}, u32[]{:S(2)}) collective-permute-start(bf16[512,2048]{1,0:T(8,128)(2,1)S(1)} %convolution_convert_fusion.5), channel_id=1, source_target_pairs={{0,1},{1,0},{2,3},{3,2},{4,5},{5,4},{6,7},{7,6},{8,9},{9,8},{10,11... | collective-permute-start | bytes 6291464 | tf_op jit(solution)/shard_map/ppermute | solution.py:44
  303.2 31.0 %collective-permute-start.36 = (bf16[128,2048]{1,0:T(8,128)(2,1)S(1)}, bf16[128,2048]{1,0:T(8,128)(2,1)S(1)}, u32[]{:S(2)}, u32[]{:S(2)}) collective-permute-start(bf16[128,2048]{1,0:T(8,128)(2,1)S(1)} %get-tuple-element.179), channel_id=1, source_target_pairs={{0,4},{4,0},{1,5},{5,1},{2,6},{6,2},{3,7},{7,3},{8,12},{12,8},{9,1... | collective-permute-start | bytes 1572872 | tf_op jit(solution)/shard_map/ppermute | solution.py:44
  329.4 43.4 %collective-permute-start.41 = (bf16[512,768]{1,0:T(8,128)(2,1)}, bf16[512,768]{1,0:T(8,128)(2,1)}, u32[]{:S(2)}, u32[]{:S(2)}) collective-permute-start(bf16[512,768]{1,0:T(8,128)(2,1)} %convolution_convert_fusion.6), channel_id=1, source_target_pairs={{0,2},{2,0},{1,3},{3,1},{4,6},{6,4},{5,7},{7,5},{8,10},{10,8},{9,1... | collective-permute-start | bytes 2359304 | tf_op jit(solution)/shard_map/ppermute | solution.py:44
  342.9 23.0 %collective-permute-start.44 = (bf16[128,2048]{1,0:T(8,128)(2,1)S(1)}, bf16[128,2048]{1,0:T(8,128)(2,1)S(1)}, u32[]{:S(2)}, u32[]{:S(2)}) collective-permute-start(bf16[128,2048]{1,0:T(8,128)(2,1)S(1)} %get-tuple-element.126.refs_0_), channel_id=1, source_target_pairs={{0,8},{8,0},{1,9},{9,1},{2,10},{10,2},{3,11},{11,3},{4,12},{12,4},... | collective-permute-start | bytes 1572872 | tf_op jit(solution)/shard_map/ppermute | solution.py:44
  344.2 36.6 %collective-permute-start.42 = (bf16[256,1536]{1,0:T(8,128)(2,1)S(1)}, bf16[256,1536]{1,0:T(8,128)(2,1)S(1)}, u32[]{:S(2)}, u32[]{:S(2)}) collective-permute-start(bf16[256,1536]{1,0:T(8,128)(2,1)S(1)} %get-tuple-element.185), channel_id=1, source_target_pairs={{0,16},{16,0},{1,17},{17,1},{2,18},{18,2},{3,19},{19,3},{4,20},{20... | collective-permute-start | bytes 2359304 | tf_op jit(solution)/shard_map/ppermute | solution.py:44
  346.7 34.1 %collective-permute-start.43 = (bf16[128,2048]{1,0:T(8,128)(2,1)S(1)}, bf16[128,2048]{1,0:T(8,128)(2,1)S(1)}, u32[]{:S(2)}, u32[]{:S(2)}) collective-permute-start(bf16[128,2048]{1,0:T(8,128)(2,1)S(1)} %get-tuple-element.126.refs_0_), channel_id=1, source_target_pairs={{0,4},{4,0},{1,5},{5,1},{2,6},{6,2},{3,7},{7,3},{8,12},{12,8},{9,1... | collective-permute-start | bytes 1572872 | tf_op jit(solution)/shard_map/ppermute | solution.py:44
  382.4 51.6 %collective-permute-start.46 = (bf16[512,2048]{1,0:T(8,128)(2,1)}, bf16[512,2048]{1,0:T(8,128)(2,1)}, u32[]{:S(2)}, u32[]{:S(2)}) collective-permute-start(bf16[512,2048]{1,0:T(8,128)(2,1)} %join.14.refs_0_), channel_id=1, source_target_pairs={{0,1},{1,0},{2,3},{3,2},{4,5},{5,4},{6,7},{7,6},{8,9},{9,8},{10,11... | collective-permute-start | bytes 6291464 | tf_op jit(solution)/shard_map/ppermute | solution.py:44
  388.3 66.7 %collective-permute-start.51 = (bf16[512,1536]{1,0:T(8,128)(2,1)}, bf16[512,1536]{1,0:T(8,128)(2,1)}, u32[]{:S(2)}, u32[]{:S(2)}) collective-permute-start(bf16[512,1536]{1,0:T(8,128)(2,1)} %convolution_convert_fusion.1), channel_id=1, source_target_pairs={{0,2},{2,0},{1,3},{3,1},{4,6},{6,4},{5,7},{7,5},{8,10},{10,8},{9,1... | collective-permute-start | bytes 4718600 | tf_op jit(solution)/shard_map/ppermute | solution.py:44
  393.1 46.5 %all-to-all-start.3 = ((bf16[4,128,768]{2,1,0:T(8,128)(2,1)}), bf16[4,128,768]{2,1,0:T(8,128)(2,1)S(1)}, u32[]{:S(2)}, u32[]{:S(2)}) async-start(bf16[4,128,768]{2,1,0:T(8,128)(2,1)} %bitcast.52), calls=%async_computation.3 | async-start | bytes 1572864 | tf_op jit(solution)/shard_map/all_to_all | solution.py:267
  396.8 22.3 %collective-permute-start.31 = (bf16[128,2048]{1,0:T(8,128)(2,1)}, bf16[128,2048]{1,0:T(8,128)(2,1)S(1)}, u32[]{:S(2)}, u32[]{:S(2)}) collective-permute-start(bf16[128,2048]{1,0:T(8,128)(2,1)} %get-tuple-element.181), channel_id=1, source_target_pairs={{0,4},{4,0},{1,5},{5,1},{2,6},{6,2},{3,7},{7,3},{8,12},{12,8},{9,1... | collective-permute-start | bytes 1572872 | tf_op jit(solution)/shard_map/ppermute | solution.py:44
  400.7 31.7 %collective-permute-start.33 = (bf16[128,2048]{1,0:T(8,128)(2,1)S(1)}, bf16[128,2048]{1,0:T(8,128)(2,1)S(1)}, u32[]{:S(2)}, u32[]{:S(2)}) collective-permute-start(bf16[128,2048]{1,0:T(8,128)(2,1)S(1)} %get-tuple-element.172), channel_id=1, source_target_pairs={{0,8},{8,0},{1,9},{9,1},{2,10},{10,2},{3,11},{11,3},{4,12},{12,4},... | collective-permute-start | bytes 1572872 | tf_op jit(solution)/shard_map/ppermute | solution.py:44
  402.3 48.1 %collective-permute-start.47 = (bf16[256,1536]{1,0:T(8,128)(2,1)}, bf16[256,1536]{1,0:T(8,128)(2,1)}, u32[]{:S(2)}, u32[]{:S(2)}) collective-permute-start(bf16[256,1536]{1,0:T(8,128)(2,1)} %get-tuple-element.184), channel_id=1, source_target_pairs={{0,16},{16,0},{1,17},{17,1},{2,18},{18,2},{3,19},{19,3},{4,20},{20... | collective-permute-start | bytes 2359304 | tf_op jit(solution)/shard_map/ppermute | solution.py:44
  454.9 20.9 %collective-permute-start.48 = (bf16[512,2048]{1,0:T(8,128)(2,1)}, bf16[512,2048]{1,0:T(8,128)(2,1)}, u32[]{:S(2)}, u32[]{:S(2)}) collective-permute-start(bf16[512,2048]{1,0:T(8,128)(2,1)} %convolution_convert_fusion.2), channel_id=1, source_target_pairs={{0,1},{1,0},{2,3},{3,2},{4,5},{5,4},{6,7},{7,6},{8,9},{9,8},{10,11... | collective-permute-start | bytes 6291464 | tf_op jit(solution)/shard_map/ppermute | solution.py:44
  459.8 36.4 %all-to-all-start.6 = ((bf16[4,128,1536]{2,1,0:T(8,128)(2,1)}), bf16[4,128,1536]{2,1,0:T(8,128)(2,1)S(1)}, u32[]{:S(2)}, u32[]{:S(2)}) async-start(bf16[4,128,1536]{2,1,0:T(8,128)(2,1)} %bitcast.51), calls=%async_computation.6 | async-start | bytes 3145728 | tf_op jit(solution)/shard_map/all_to_all | solution.py:267
  470.4 21.1 %collective-permute-start.58 = (bf16[512,256]{1,0:T(8,128)(2,1)S(1)}, bf16[512,256]{1,0:T(8,128)(2,1)S(1)}, u32[]{:S(2)}, u32[]{:S(2)}) collective-permute-start(bf16[512,256]{1,0:T(8,128)(2,1)S(1)} %convolution_convert_fusion.11), channel_id=1, source_target_pairs={{0,2},{2,0},{1,3},{3,1},{4,6},{6,4},{5,7},{7,5},{8,10},{10,8},{9,1... | collective-permute-start | bytes 786440 | tf_op jit(solution)/shard_map/ppermute | solution.py:44
  473.4 32.1 %collective-permute-start.56 = (bf16[512,512]{1,0:T(8,128)(2,1)}, bf16[512,512]{1,0:T(8,128)(2,1)}, u32[]{:S(2)}, u32[]{:S(2)}) collective-permute-start(bf16[512,512]{1,0:T(8,128)(2,1)} %convolution_convert_fusion.8), channel_id=1, source_target_pairs={{0,2},{2,0},{1,3},{3,1},{4,6},{6,4},{5,7},{7,5},{8,10},{10,8},{9,1... | collective-permute-start | bytes 1572872 | tf_op jit(solution)/shard_map/ppermute | solution.py:44
  487.4 25.6 %collective-permute-start.57 = (bf16[512,512]{1,0:T(8,128)(2,1)}, bf16[512,512]{1,0:T(8,128)(2,1)}, u32[]{:S(2)}, u32[]{:S(2)}) collective-permute-start(bf16[512,512]{1,0:T(8,128)(2,1)} %fusion.8), channel_id=1, source_target_pairs={{0,16},{16,0},{1,17},{17,1},{2,18},{18,2},{3,19},{19,3},{4,20},{20... | collective-permute-start | bytes 1572872 | tf_op jit(solution)/shard_map/ppermute | solution.py:44
  492.7 36.6 %collective-permute-start.49 = (bf16[128,2048]{1,0:T(8,128)(2,1)}, bf16[128,2048]{1,0:T(8,128)(2,1)}, u32[]{:S(2)}, u32[]{:S(2)}) collective-permute-start(bf16[128,2048]{1,0:T(8,128)(2,1)} %get-tuple-element.177), channel_id=1, source_target_pairs={{0,4},{4,0},{1,5},{5,1},{2,6},{6,2},{3,7},{7,3},{8,12},{12,8},{9,1... | collective-permute-start | bytes 1572872 | tf_op jit(solution)/shard_map/ppermute | solution.py:44
  503.5 25.8 %collective-permute-start.54 = (bf16[128,2048]{1,0:T(8,128)(2,1)}, bf16[128,2048]{1,0:T(8,128)(2,1)}, u32[]{:S(2)}, u32[]{:S(2)}) collective-permute-start(bf16[128,2048]{1,0:T(8,128)(2,1)} %get-tuple-element.168), channel_id=1, source_target_pairs={{0,8},{8,0},{1,9},{9,1},{2,10},{10,2},{3,11},{11,3},{4,12},{12,4},... | collective-permute-start | bytes 1572872 | tf_op jit(solution)/shard_map/ppermute | solution.py:44
  516.1 37.6 %all-to-all-start.4 = ((bf16[4,128,512]{2,1,0:T(8,128)(2,1)}), bf16[4,128,512]{2,1,0:T(8,128)(2,1)}, u32[]{:S(2)}, u32[]{:S(2)}) async-start(bf16[4,128,512]{2,1,0:T(8,128)(2,1)} %bitcast.53), calls=%async_computation.4 | async-start | bytes 1048576 | tf_op jit(solution)/shard_map/all_to_all | solution.py:267
  (109 other events, 1816.9 us)

commit v3 on v2

--- a/solution.py
+++ b/solution.py
@@ -188,15 +188,19 @@
     return join(after(half, *at_whole), swap(half, "c"))
 
 
-def sum_rows(left, right_t, at_mine=(), at_far=()):
+def sum_cores(left, right_t, at_mine=None):
     half = left.shape[0] // 2
     other = swap(dot_nt(left[half:], right_t).astype(bf16), "c")
-    mine = dot_nt(left[:half], right_t) + after(other, *at_mine).astype(f32)
+    if at_mine is not None:
+        other = after(other, *at_mine)
+    return dot_nt(left[:half], right_t) + other.astype(f32)
+
+
+def sum_chips(mine, at_far=None):
     block = rows_of(mine, 4)
-    both = swap(block[3].astype(bf16), "y")
-    near = swap(block[1].astype(bf16), "y")
-    far = swap((block[2] + after(both, *at_far).astype(f32)).astype(bf16), "zl")
-    return block[0], near, far
+    both, near = swap(block[3].astype(bf16), "y"), swap(block[1].astype(bf16), "y")
+    came = both if at_far is None else after(both, *at_far)
+    return block[0], near, swap((block[2] + came.astype(f32)).astype(bf16), "zl"), both
 
 
 def pack_attention_kernel(wide_q, wide_kv, qkv, out, packed):
@@ -599,19 +603,18 @@
     projected = dot(normed_one, own_qkv)
     projected = projected.reshape(2, 4, half, wide_qkv)
     attended = attend(projected, shift, cosine, sine, head_rows, heads_q, heads_kv)
-    attended = after(attended.reshape(-1, wide_q), far_gu[0], cotangent_zl, cotangent_y, block_down)
+    attended = after(
+        attended.reshape(-1, wide_q), block_down, cotangent_zl, cotangent_y, far_gu[0]
+    )
+    mine = sum_cores(attended, own_out, (cotangent_both,))
+    terms = sum_chips(mine, (side_gu, far_gu[1]))[:3]
     middle, normed_own = vmem_call(
         middle_kernel,
         [shape(half, width, f32), shape(half, width, bf16)],
-        place,
-        *sum_rows(attended, own_out, (cotangent_both,), (far_gu[1], side_gu)),
-        inputs, after(own_gains, both_gu[0], cotangent_all),
+        place, *terms, inputs, after(own_gains, cotangent_all),
         name="middle",
     )
-
-    normed_two = gather_rows(
-        normed_own, at_send=(*far_down, side_down), at_half=(both_gu[1],)
-    )
+    normed_two = gather_rows(normed_own, (side_down,), (*both_gu, *far_down))
     gate_up = dot(normed_two, own_gate_up)
     gate, up = gate_up[:, :hidden], gate_up[:, hidden:]
     sigmoid_gate = jax.nn.sigmoid(gate)
@@ -624,29 +627,37 @@
 
     side_far, side_near = map(side, parts)
     far = far_part(cotangent_all, activation, side_far)
-    far_down = [swap(far, "zh")]
+    far_down = [swap(part, "zh") for part in rows_of(far, 2)]
     side_far_gu, side_near_gu = map(side, send_parts(normed_two, d_gate_up))
-    far = far_part(normed_two, d_gate_up, side_far_gu)
-    far_rows = far
-    far_gu = [swap(part, "zh") for part in rows_of(far, 2)]
-
+    far_rows = far_part(normed_two, d_gate_up, side_far_gu)
+    far_gu = [swap(part, "zh") for part in rows_of(far_rows, 2)]
+    grad_down = own_part(cotangent_all, activation, side_near, far_down, rest)
+    got_down = exchange(grad_down)
+    new_down = adam_turned(got_down, weight_down, first_down, second_down, hidden)
+    own_sum_gu = own_part(normed_two, d_gate_up, side_near_gu, far_gu, rest)
+    grad_gate_up = exchange(own_sum_gu)
+    new_gate_up = adam_columns(grad_gate_up, weight_gate_up, first_gate_up, second_gate_up, hidden)
+    mine = sum_cores(activation, own_down)
+    base, near_output, far_output, _ = sum_chips(mine)
+    output = vmem_call(
+        output_kernel, shape(half, width, bf16), place, base, near_output, far_output, middle, name="output"
+    )
+
+    terms = sum_chips(sum_cores(d_gate_up, own_gate_up, (side_far,)), far_down)[:3]
     grad_middle, branch_own, gain_two_grad = vmem_call(
         back_two_kernel,
         [shape(half, width, f32), shape(half, width, bf16), shape(1, width, f32)],
-        place,
-        *sum_rows(d_gate_up, own_gate_up, (side_far,), (far_down[0],)),
-        middle, own_cotangent, after(own_gains, side_far_gu),
+        place, *terms, middle, own_cotangent, after(own_gains, side_far_gu),
         name="back_two",
     )
-    base, near, far = sum_rows(activation, own_down)
-    output = vmem_call(
-        output_kernel, shape(half, width, bf16), place, base, near, far, middle, name="output"
-    )
-    d_branch = gather_rows(branch_own, at_send=(far_rows,), at_half=(side_near, far_gu[0]))
-    grad_down = exchange(own_part(cotangent_all, activation, side_near, far_down, rest))
-    new_down = adam_turned(grad_down, weight_down, first_down, second_down, hidden)
-
-    d_attended = after(dot(d_branch, own_out).astype(bf16), output, grad_down)
+    d_branch = gather_rows(branch_own, (far_rows,), (side_near, far_gu[0]), (near_output,))
+    side_far_out, side_near_out = map(side, send_parts(d_branch, attended))
+    far_out = far_part(d_branch, attended, side_far_out)
+    far_out = swap(far_out, "zh")
+    grad_out = exchange(own_part(d_branch, attended, side_near_out, [far_out], rest))
+    new_out = adam_turned(grad_out, weight_out, first_out, second_out, wide_q)
+
+    d_attended = after(dot(d_branch, own_out).astype(bf16), new_down[3])
     d_projected, head_grad = attend_back(
         projected,
         d_attended.reshape(2, 4, half, wide_q),
@@ -657,34 +668,25 @@
         heads_q,
         heads_kv,
     )
-    d_projected = after(d_projected.reshape(-1, wide_qkv), far_gu[1])
-    side_far_out, side_near_out = map(side, send_parts(d_branch, attended))
-    far_out = swap(far_part(d_branch, attended, side_far_out), "zh")
+    d_projected = after(d_projected.reshape(-1, wide_qkv), got_down, far_output)
     side_far_qkv, side_near_qkv = map(side, send_parts(normed_one, d_projected))
-    far_qkv = swap(far_part(normed_one, d_projected, side_far_qkv), "zh")
-
-    grad_gate_up = own_part(normed_two, d_gate_up, side_near_gu, far_gu, rest)
-    terms = sum_rows(
-        d_projected, own_qkv, at_far=(grad_gate_up, side_far_qkv, side_far_out)
-    )
-    grad_gate_up = exchange(grad_gate_up)
-    new_gate_up = adam_columns(grad_gate_up, weight_gate_up, first_gate_up, second_gate_up, hidden)
-    grad_out = exchange(own_part(d_branch, attended, side_near_out, [far_out], rest))
-    new_out = adam_turned(grad_out, weight_out, first_out, second_out, wide_q)
+    far_qkv = far_part(normed_one, d_projected, side_far_qkv)
+    far_qkv = swap(far_qkv, "zh")
     grad_qkv = exchange(own_part(normed_one, d_projected, side_near_qkv, [far_qkv], rest))
     new_qkv = adam_qkv(grad_qkv, weight_qkv, first_qkv, second_qkv, wide_q, wide_kv)
+    terms = sum_chips(sum_cores(d_projected, own_qkv, ()), (far_gu[1], side_far_qkv))[:3]
+    back_one_gains = after(own_gains, own_sum_gu, side_far_out, side_near_out, far_out)
     input_grad, gain_grads = vmem_call(
         back_one_kernel,
         [shape(half, width, f32), shape(2, width, f32)],
-        place, *terms, inputs, grad_middle, after(own_gains, far_out, new_down[3]), gain_two_grad,
+        place, *terms, inputs, grad_middle, back_one_gains, gain_two_grad,
         name="back_one",
     )
 
     sums = jnp.concatenate([gain_grads, head_grad], axis=1)
-    sums = sums + swap(sums, "c")
-    sums = sums + swap(after(sums, new_gate_up[3]), "x")
-    sums = sums + swap(after(sums, new_out[3]), "y")
-    for axis in ("zl", "zh"):
+    steps = (("c", new_gate_up[3:]), ("x", ()), ("y", ()), ("zl", new_out[3:]), ("zh", ()))
+    for axis, ready in steps:
+        sums = after(sums, *ready)
         sums = sums + swap(sums, axis)
     if rest > 1:
         sums = lax.psum(sums, "r")

time: 572 us -> 551 us (0.963)
  starting transfers between devices: 106 us -> 92 us
  waiting for transfers between devices: 259 us -> 249 us
    ppermute x64 -> x65, starting transfers between devices: 75.9 us -> 63.1 us  [swap(): return lax.ppermute(value, axis, SWAP)]
    ppermute x64 -> x65, waiting for transfers between devices: 259 us -> 249 us  [swap(): return lax.ppermute(value, axis, SWAP)]
    unnamed x181 -> x168, local copies, waits for them, and re-layouts: 31.5 us -> 28 us
  transfers between devices with their start and end apart: 71 -> 72, of which waited for: 28 -> 30; matrix products, arithmetic and copies ran while one was open for 17% -> 19% of each run, Pallas kernels for 9% -> 10%
where the time goes in v3:
time: 551 us; the launch traced here: 541 us
  waiting for transfers between devices  249 us (45%)
  matrix products  93.1 us (17%)
  starting transfers between devices  92 us (17%)
  Pallas kernels  57 us (10%)
  local copies, waits for them, and re-layouts  37.9 us (7%)
  other arithmetic  9.99 us (2%)
    ppermute x65, waiting for transfers between devices, swap(): return lax.ppermute(value, axis, SWAP)  249 us
    ppermute x65, starting transfers between devices, swap(): return lax.ppermute(value, axis, SWAP)  63.1 us
    dot_general x8, matrix products, dot_nt(): lax.dot_general(left, right, (((1,), (1,)), ((), ())), preferred_element_...  35.4 us
    dot_general x16, matrix products, dot_tn(): lax.dot_general(left, right, (((0,), (0,)), ((), ())), preferred_element_...  35.3 us
    all_to_all x7, starting transfers between devices, exchange(): return lax.all_to_all(pieces, ('zl', 'y'), 0, 0, tiled=True)  28.8 us
    unnamed x168, local copies, waits for them, and re-layouts  28 us
    dot_general x4, matrix products, dot(): return jnp.dot(left, right, preferred_element_type=f32)  22.4 us
    pallas_call x4, Pallas kernels, adam(): pl.pallas_call(kernel, grid=grid, in_specs=[got_spec, spec, spec, spec],...  15.2 us
  transfers between devices with their start and end apart: 72, of which 30 were waited for; matrix products, arithmetic and copies ran while one was open for 19% of the time, Pallas kernels for 10%

profile of v3, /device:TPU:0, one launch (start us, length us, event | category | flops | bytes accessed | tf_op | source)
XLA Modules:
  0.0 541.3 jit_solution(5498637854767686706)
XLA Ops:
  3.8 5.2 all-to-all-start
  17.4 14.2 %collective-permute-done.refs_2_ = bf16[128,2048]{1,0:T(8,128)(2,1)S(1)} collective-permute-done((bf16[128,2048]{1,0:T(8,128)(2,1)S(1)}, bf16[128,2048]{1,0:T(8,128)(2,1)S(1)}, u32[]{:S(2)}, u32[]{:S(2)}) %collective-permute-start) | collective-permute-done | bytes 524320 | tf_op jit(solution)/shard_map/ppermute | solution.py:44
  40.8 4.4 all-to-all-start.1
  48.6 12.0 %collective-permute-done.2 = bf16[512,512]{1,0:T(8,128)(2,1)} collective-permute-done((bf16[512,512]{1,0:T(8,128)(2,1)}, bf16[512,512]{1,0:T(8,128)(2,1)}, u32[]{:S(2)}, u32[]{:S(2)}) %collective-permute-start.2) | collective-permute-done | bytes 524320 | tf_op jit(solution)/shard_map/ppermute | solution.py:44
  74.7 8.6 %collective-permute-done.6 = bf16[512,256]{1,0:T(8,128)(2,1)} collective-permute-done((bf16[512,256]{1,0:T(8,128)(2,1)}, bf16[512,256]{1,0:T(8,128)(2,1)}, u32[]{:S(2)}, u32[]{:S(2)}) %collective-permute-start.6) | collective-permute-done | bytes 262176 | tf_op jit(solution)/shard_map/ppermute | solution.py:44
  83.2 3.5 collective-permute-done.7
  91.1 4.2 all-to-all-start.2
  101.6 5.4 fusion.48
  107.0 6.0 %attend.1 = bf16[2,4,128,256]{3,2,1,0:T(8,128)(2,1)S(1)} custom-call(s32[1]{0:T(128)} %bitcast.2.shift_ref, f32[2,4,128,512]{3,2,1,0:T(8,128)S(1)} %bitcast.36, f32[256,128]{1,0:T(8,128)S(1)} %get-tuple-element.201.cos_ref, f32[256,128]{1,0:T(8,128)S(1)} %copy-done.24, f32[2,128]{1,0:T(2,128)S(1)} %copy-done.45), custom_call_target="tpu_custom_call" | custom-call | tf_op jit(solution)/shard_map/attend/pallas_call | solution.py:477
  118.6 15.4 %collective-permute-done.11 = bf16[256,1536]{1,0:T(8,128)(2,1)} collective-permute-done((bf16[256,1536]{1,0:T(8,128)(2,1)S(1)}, bf16[256,1536]{1,0:T(8,128)(2,1)}, u32[]{:S(2)}, u32[]{:S(2)}) %collective-permute-start.11) | collective-permute-done | bytes 786464 | tf_op jit(solution)/shard_map/ppermute | solution.py:44
  138.6 12.2 %collective-permute-done.14.refs_3_ = bf16[128,2048]{1,0:T(8,128)(2,1)S(1)} collective-permute-done((bf16[128,2048]{1,0:T(8,128)(2,1)}, bf16[128,2048]{1,0:T(8,128)(2,1)S(1)}, u32[]{:S(2)}, u32[]{:S(2)}) %collective-permute-start.14) | collective-permute-done | bytes 524320 | tf_op jit(solution)/shard_map/ppermute | solution.py:44
  157.3 17.9 %collective-permute-done.18 = bf16[256,1536]{1,0:T(8,128)(2,1)S(1)} collective-permute-done((bf16[256,1536]{1,0:T(8,128)(2,1)S(1)}, bf16[256,1536]{1,0:T(8,128)(2,1)S(1)}, u32[]{:S(2)}, u32[]{:S(2)}) %collective-permute-start.18) | collective-permute-done | bytes 786464 | tf_op jit(solution)/shard_map/ppermute | solution.py:44
  176.4 4.4 collective-permute-done.15.near
  180.8 8.5 %collective-permute-done.19.far = bf16[128,2048]{1,0:T(8,128)(2,1)S(1)} collective-permute-done((bf16[128,2048]{1,0:T(8,128)(2,1)S(1)}, bf16[128,2048]{1,0:T(8,128)(2,1)S(1)}, u32[]{:S(2)}, u32[]{:S(2)}) %collective-permute-start.19) | collective-permute-done | bytes 524320 | tf_op jit(solution)/shard_map/ppermute | solution.py:44
  196.7 15.3 %collective-permute-done.25.refs_2_ = bf16[128,2048]{1,0:T(8,128)(2,1)S(1)} collective-permute-done((bf16[128,2048]{1,0:T(8,128)(2,1)S(1)}, bf16[128,2048]{1,0:T(8,128)(2,1)S(1)}, u32[]{:S(2)}, u32[]{:S(2)}) %collective-permute-start.25) | collective-permute-done | bytes 524320 | tf_op jit(solution)/shard_map/ppermute | solution.py:44
  213.0 15.9 %collective-permute-done.22 = bf16[256,1536]{1,0:T(8,128)(2,1)S(1)} collective-permute-done((bf16[256,1536]{1,0:T(8,128)(2,1)S(1)}, bf16[256,1536]{1,0:T(8,128)(2,1)S(1)}, u32[]{:S(2)}, u32[]{:S(2)}) %collective-permute-start.22) | collective-permute-done | bytes 786464 | tf_op jit(solution)/shard_map/ppermute | solution.py:44
  234.9 6.6 %fusion.63 = f32[1024,1536]{1,0:T(8,128)S(1)} fusion(bf16[1024,2048]{1,0:T(8,128)(2,1)S(1)} %join.13, bf16[2048,1536]{1,0:T(8,128)(2,1)S(1)} %constant_dynamic-update-slice_fusion.4), kind=kOutput, calls=%fused_computation.125 | convolution fusion | flops 6442450944 | bytes 16777216 | tf_op jit(solution)/shard_map/dot_general | solution.py:32
  243.6 8.7 %collective-permute-done.29 = bf16[512,768]{1,0:T(8,128)(2,1)S(1)} collective-permute-done((bf16[512,768]{1,0:T(8,128)(2,1)S(1)}, bf16[512,768]{1,0:T(8,128)(2,1)S(1)}, u32[]{:S(2)}, u32[]{:S(2)}) %collective-permute-start.29) | collective-permute-done | bytes 786464 | tf_op jit(solution)/shard_map/ppermute | solution.py:44
  252.2 6.9 %multiply_convert_fusion = (bf16[1024,768]{1,0:T(8,128)(2,1)S(1)}, bf16[1024,768]{1,0:T(8,128)(2,1)S(1)}) fusion(f32[1024,1536]{1,0:T(8,128)S(1)} %fusion.63, bf16[1024,2048]{1,0:T(8,128)(2,1)S(1)} %join.11, bf16[512,768]{1,0:T(8,128)(2,1)S(1)} %collective-permute-done.29, bf16[512,768]{1,0:T(8,128)(2,1)S(1)} %copy-done.63, ...), kind=kOutput, calls=%fused_computation.13 | convolution fusion | flops 3244032000 | bytes 16777216 | tf_op jit(solution)/shard_map/dot_general | solution.py:32
  260.3 6.4 %convolution_convert_fusion.4 = bf16[512,2048]{1,0:T(8,128)(2,1)S(1)} fusion(bf16[2048,1536]{1,0:T(8,128)(2,1)} %copy-done.53, bf16[1024,768]{1,0:T(8,128)(2,1)S(1)} %get-tuple-element.169, bf16[1024,768]{1,0:T(8,128)(2,1)S(1)} %get-tuple-element.168), kind=kOutput, calls=%fused_computation.23 | convolution fusion | flops 3225419776 | bytes 11534336 | tf_op jit(solution)/shard_map/dot_general | solution.py:40
  267.5 4.4 convolution_convert_fusion.3
  273.3 13.9 %collective-permute-done.35 = bf16[512,768]{1,0:T(8,128)(2,1)S(1)} collective-permute-done((bf16[512,768]{1,0:T(8,128)(2,1)S(1)}, bf16[512,768]{1,0:T(8,128)(2,1)S(1)}, u32[]{:S(2)}, u32[]{:S(2)}) %collective-permute-start.35) | collective-permute-done | bytes 786464 | tf_op jit(solution)/shard_map/ppermute | solution.py:44
  291.4 6.2 %fusion.61 = (bf16[512,2048]{1,0:T(8,128)(2,1)S(1)}, f32[512,2048]{1,0:T(8,128)S(1)}) fusion(bf16[512,2048]{1,0:T(8,128)(2,1)S(1)} %collective-permute-done.34, bf16[2048,1536]{1,0:T(8,128)(2,1)} %copy-done.53, bf16[1024,768]{1,0:T(8,128)(2,1)} %copy-done.76, bf16[1024,768]{1,0:T(8,128)(2,1)} %copy-done.72), kind=kOutput, calls=%fused_computation.123 | convolution fusion | flops 3227516928 | bytes 17825792 | tf_op jit(solution)/shard_map/dot_general | solution.py:40
  298.3 4.8 convolution_convert_fusion.5
  303.0 14.7 %collective-permute-done.38 = bf16[256,768]{1,0:T(8,128)(2,1)S(1)} collective-permute-done((bf16[256,768]{1,0:T(8,128)(2,1)S(1)}, bf16[256,768]{1,0:T(8,128)(2,1)S(1)}, u32[]{:S(2)}, u32[]{:S(2)}) %collective-permute-start.38) | collective-permute-done | bytes 393248 | tf_op jit(solution)/shard_map/ppermute | solution.py:44
  318.2 6.7 %collective-permute-done.39 = bf16[256,768]{1,0:T(8,128)(2,1)} collective-permute-done((bf16[256,768]{1,0:T(8,128)(2,1)S(1)}, bf16[256,768]{1,0:T(8,128)(2,1)}, u32[]{:S(2)}, u32[]{:S(2)}) %collective-permute-start.39) | collective-permute-done | bytes 393248 | tf_op jit(solution)/shard_map/ppermute | solution.py:44
  330.4 7.5 %collective-permute-done.40.far = bf16[128,2048]{1,0:T(8,128)(2,1)S(1)} collective-permute-done((bf16[128,2048]{1,0:T(8,128)(2,1)S(1)}, bf16[128,2048]{1,0:T(8,128)(2,1)S(1)}, u32[]{:S(2)}, u32[]{:S(2)}) %collective-permute-start.40) | collective-permute-done | bytes 524320 | tf_op jit(solution)/shard_map/ppermute | solution.py:44
  344.0 17.3 %collective-permute-done.45.refs_2_ = bf16[128,2048]{1,0:T(8,128)(2,1)} collective-permute-done((bf16[128,2048]{1,0:T(8,128)(2,1)}, bf16[128,2048]{1,0:T(8,128)(2,1)}, u32[]{:S(2)}, u32[]{:S(2)}) %collective-permute-start.45) | collective-permute-done | bytes 524320 | tf_op jit(solution)/shard_map/ppermute | solution.py:44
  364.7 3.7 all-to-all-start.3
  368.4 8.9 %collective-permute-done.43 = bf16[256,1536]{1,0:T(8,128)(2,1)} collective-permute-done((bf16[256,1536]{1,0:T(8,128)(2,1)}, bf16[256,1536]{1,0:T(8,128)(2,1)}, u32[]{:S(2)}, u32[]{:S(2)}) %collective-permute-start.43) | collective-permute-done | bytes 786464 | tf_op jit(solution)/shard_map/ppermute | solution.py:44
  380.3 3.8 fusion.60
  385.6 4.2 convolution_convert_fusion.1
  392.5 7.4 %collective-permute-done.32 = bf16[128,2048]{1,0:T(8,128)(2,1)S(1)} collective-permute-done((bf16[128,2048]{1,0:T(8,128)(2,1)S(1)}, bf16[128,2048]{1,0:T(8,128)(2,1)S(1)}, u32[]{:S(2)}, u32[]{:S(2)}) %collective-permute-start.32) | collective-permute-done | bytes 524320 | tf_op jit(solution)/shard_map/ppermute | solution.py:44
  406.2 3.5 adam_turned.2
  412.9 3.4 convolution_convert_fusion.10
  416.3 8.8 %attend_back.1 = (bf16[2,4,128,512]{3,2,1,0:T(8,128)(2,1)S(1)}, f32[2,128]{1,0:T(2,128)S(1)}) custom-call(s32[1]{0:T(128)} %bitcast.2.shift_ref, f32[2,4,128,512]{3,2,1,0:T(8,128)S(1)} %bitcast.37, bf16[2,4,128,256]{3,2,1,0:T(8,128)(2,1)S(1)} %bitcast.44, f32[256,128]{1,0:T(8,128)S(1)} %get-tuple-element.201.cos_ref, f32[256,128]{1,0:T(8,128)S(1)} %copy-done.25, ...), custom_call_target="tpu_custom_call" | custom-call | tf_op jit(solution)/shard_map/attend_back/pallas_call | solution.py:497
  425.2 4.5 convolution_convert_fusion.2
  429.8 9.2 %collective-permute-done.51 = bf16[256,1536]{1,0:T(8,128)(2,1)} collective-permute-done((bf16[256,1536]{1,0:T(8,128)(2,1)}, bf16[256,1536]{1,0:T(8,128)(2,1)}, u32[]{:S(2)}, u32[]{:S(2)}) %collective-permute-start.51) | collective-permute-done | bytes 786464 | tf_op jit(solution)/shard_map/ppermute | solution.py:44
  439.0 4.9 fusion.2
  443.9 3.8 all-to-all-start.6
  460.1 5.6 %fusion.62 = (bf16[512,2048]{1,0:T(8,128)(2,1)S(1)}, f32[512,2048]{1,0:T(8,128)}) fusion(bf16[512,2048]{1,0:T(8,128)(2,1)} %collective-permute-done.48, bf16[512,512]{1,0:T(8,128)(2,1)} %collective-permute-done.5, bf16[512,512]{1,0:T(8,128)(2,1)} %collective-permute-done.3, bf16[512,512]{1,0:T(8,128)(2,1)} %collective-permute-done.2, ...), kind=kOutput, calls=%fused_computation.124 | convolution fusion | flops 1085276160 | bytes 11010048 | tf_op jit(solution)/shard_map/dot_general | solution.py:40
  468.5 7.2 %collective-permute-done.52 = bf16[512,512]{1,0:T(8,128)(2,1)S(1)} collective-permute-done((bf16[512,512]{1,0:T(8,128)(2,1)S(1)}, bf16[512,512]{1,0:T(8,128)(2,1)S(1)}, u32[]{:S(2)}, u32[]{:S(2)}) %collective-permute-start.52) | collective-permute-done | bytes 524320 | tf_op jit(solution)/shard_map/ppermute | solution.py:44
  481.1 3.4 all-to-all-start.5
  489.6 8.9 %collective-permute-done.59 = bf16[512,512]{1,0:T(8,128)(2,1)} collective-permute-done((bf16[512,512]{1,0:T(8,128)(2,1)}, bf16[512,512]{1,0:T(8,128)(2,1)}, u32[]{:S(2)}, u32[]{:S(2)}) %collective-permute-start.59) | collective-permute-done | bytes 524320 | tf_op jit(solution)/shard_map/ppermute | solution.py:44
  501.6 4.1 all-to-all-start.4
  509.5 6.2 %adam_columns.1 = (f32[128,6144]{1,0:T(8,128)}, f32[128,6144]{1,0:T(8,128)}, f32[128,6144]{1,0:T(8,128)}, f32[128,6144]{1,0:T(8,128)}) custom-call(bf16[4,128,1536]{2,1,0:T(8,128)(2,1)S(1)} %all-to-all-done.6.got, bf16[128,6144]{1,0:T(8,128)(2,1)S(1)} %copy-done, f32[128,6144]{1,0:T(8,128)S(1)} %copy-done.13, f32[128,6144]{1,0:T(8,128)S(1)} %copy-done.14), custom_call_target="tpu_custom_call" | custom-call | flops 11010048 | bytes 22020096 | tf_op jit(solution)/shard_map/adam_columns/pallas_call | solution.py:339
  515.8 3.5 back_one.1
  536.1 3.4 adam_qkv.1
  (346 shorter events, 173.3 us)
Async XLA Ops:
  3.8 29.4 %all-to-all-start = ((bf16[4,128,768]{2,1,0:T(8,128)(2,1)}), bf16[4,128,768]{2,1,0:T(8,128)(2,1)}, u32[]{:S(2)}, u32[]{:S(2)}) async-start(bf16[4,128,768]{2,1,0:T(8,128)(2,1)} %pack_attention.1), calls=%async_computation | async-start | bytes 1572864 | tf_op jit(solution)/shard_map/all_to_all | solution.py:271
  11.2 20.4 %collective-permute-start = (bf16[128,2048]{1,0:T(8,128)(2,1)S(1)}, bf16[128,2048]{1,0:T(8,128)(2,1)S(1)}, u32[]{:S(2)}, u32[]{:S(2)}) collective-permute-start(bf16[128,2048]{1,0:T(8,128)(2,1)S(1)} %get-tuple-element.97.refs_0_), channel_id=1, source_target_pairs={{0,8},{8,0},{1,9},{9,1},{2,10},{10,2},{3,11},{11,3},{4,12},{12,4},... | collective-permute-start | bytes 1572872 | tf_op jit(solution)/shard_map/ppermute | solution.py:44
  35.1 25.6 %collective-permute-start.2 = (bf16[512,512]{1,0:T(8,128)(2,1)}, bf16[512,512]{1,0:T(8,128)(2,1)}, u32[]{:S(2)}, u32[]{:S(2)}) collective-permute-start(bf16[512,512]{1,0:T(8,128)(2,1)} %slice.164), channel_id=1, source_target_pairs={{0,16},{16,0},{1,17},{17,1},{2,18},{18,2},{3,19},{19,3},{4,20},{20... | collective-permute-start | bytes 1572872 | tf_op jit(solution)/shard_map/ppermute | solution.py:44
  37.8 22.8 %collective-permute-start.3 = (bf16[512,512]{1,0:T(8,128)(2,1)}, bf16[512,512]{1,0:T(8,128)(2,1)}, u32[]{:S(2)}, u32[]{:S(2)}) collective-permute-start(bf16[512,512]{1,0:T(8,128)(2,1)} %slice.164), channel_id=1, source_target_pairs={{0,2},{2,0},{1,3},{3,1},{4,6},{6,4},{5,7},{7,5},{8,10},{10,8},{9,1... | collective-permute-start | bytes 1572872 | tf_op jit(solution)/shard_map/ppermute | solution.py:44
  39.3 21.3 %collective-permute-start.4 = (bf16[128,2048]{1,0:T(8,128)(2,1)}, bf16[128,2048]{1,0:T(8,128)(2,1)}, u32[]{:S(2)}, u32[]{:S(2)}) collective-permute-start(bf16[128,2048]{1,0:T(8,128)(2,1)} %copy-done.38), channel_id=1, source_target_pairs={{0,4},{4,0},{1,5},{5,1},{2,6},{6,2},{3,7},{7,3},{8,12},{12,8},{9,1... | collective-permute-start | bytes 1572872 | tf_op jit(solution)/shard_map/ppermute | solution.py:44
  40.8 45.9 %all-to-all-start.1 = ((bf16[4,128,1536]{2,1,0:T(8,128)(2,1)}), bf16[4,128,1536]{2,1,0:T(8,128)(2,1)}, u32[]{:S(2)}, u32[]{:S(2)}) async-start(bf16[4,128,1536]{2,1,0:T(8,128)(2,1)} %pack_columns.1), calls=%async_computation.1 | async-start | bytes 3145728 | tf_op jit(solution)/shard_map/all_to_all | solution.py:271
  66.3 20.4 %collective-permute-start.8 = (bf16[512,2048]{1,0:T(8,128)(2,1)}, bf16[512,2048]{1,0:T(8,128)(2,1)}, u32[]{:S(2)}, u32[]{:S(2)}) collective-permute-start(bf16[512,2048]{1,0:T(8,128)(2,1)} %join.8.refs_0_), channel_id=1, source_target_pairs={{0,1},{1,0},{2,3},{3,2},{4,5},{5,4},{6,7},{7,6},{8,9},{9,8},{10,11... | collective-permute-start | bytes 6291464 | tf_op jit(solution)/shard_map/ppermute | solution.py:44
  66.4 20.3 %collective-permute-start.5 = (bf16[512,512]{1,0:T(8,128)(2,1)}, bf16[512,512]{1,0:T(8,128)(2,1)}, u32[]{:S(2)}, u32[]{:S(2)}) collective-permute-start(bf16[512,512]{1,0:T(8,128)(2,1)} %collective-permute-done.2), channel_id=1, source_target_pairs={{0,2},{2,0},{1,3},{3,1},{4,6},{6,4},{5,7},{7,5},{8,10},{10,8},{9,1... | collective-permute-start | bytes 1572872 | tf_op jit(solution)/shard_map/ppermute | solution.py:44
  86.7 31.9 %collective-permute-start.9 = (bf16[128,2048]{1,0:T(8,128)(2,1)S(1)}, bf16[128,2048]{1,0:T(8,128)(2,1)}, u32[]{:S(2)}, u32[]{:S(2)}) collective-permute-start(bf16[128,2048]{1,0:T(8,128)(2,1)S(1)} %get-tuple-element.108.refs_0_.cotangent), channel_id=1, source_target_pairs={{0,8},{8,0},{1,9},{9,1},{2,10},{10,2},{3,11},{11,3},{4,12},{12,4},... | collective-permute-start | bytes 1572872 | tf_op jit(solution)/shard_map/ppermute | solution.py:44
  89.7 29.0 %collective-permute-start.10 = (bf16[128,2048]{1,0:T(8,128)(2,1)S(1)}, bf16[128,2048]{1,0:T(8,128)(2,1)}, u32[]{:S(2)}, u32[]{:S(2)}) collective-permute-start(bf16[128,2048]{1,0:T(8,128)(2,1)S(1)} %get-tuple-element.108.refs_0_.cotangent), channel_id=1, source_target_pairs={{0,4},{4,0},{1,5},{5,1},{2,6},{6,2},{3,7},{7,3},{8,12},{12,8},{9,1... | collective-permute-start | bytes 1572872 | tf_op jit(solution)/shard_map/ppermute | solution.py:44
  91.1 43.0 %all-to-all-start.2 = ((bf16[4,128,768]{2,1,0:T(8,128)(2,1)}), bf16[4,128,768]{2,1,0:T(8,128)(2,1)}, u32[]{:S(2)}, u32[]{:S(2)}) async-start(bf16[4,128,768]{2,1,0:T(8,128)(2,1)} %pack_turned.1), calls=%async_computation.2 | async-start | bytes 1572864 | tf_op jit(solution)/shard_map/all_to_all | solution.py:271
  97.6 36.5 %collective-permute-start.11 = (bf16[256,1536]{1,0:T(8,128)(2,1)S(1)}, bf16[256,1536]{1,0:T(8,128)(2,1)}, u32[]{:S(2)}, u32[]{:S(2)}) collective-permute-start(bf16[256,1536]{1,0:T(8,128)(2,1)S(1)} %get-tuple-element.189), channel_id=1, source_target_pairs={{0,16},{16,0},{1,17},{17,1},{2,18},{18,2},{3,19},{19,3},{4,20},{20... | collective-permute-start | bytes 2359304 | tf_op jit(solution)/shard_map/ppermute | solution.py:44
  138.1 37.1 %collective-permute-start.17 = (bf16[512,1536]{1,0:T(8,128)(2,1)}, bf16[512,1536]{1,0:T(8,128)(2,1)S(1)}, u32[]{:S(2)}, u32[]{:S(2)}) collective-permute-start(bf16[512,1536]{1,0:T(8,128)(2,1)} %bitcast.4), channel_id=1, source_target_pairs={{0,2},{2,0},{1,3},{3,1},{4,6},{6,4},{5,7},{7,5},{8,10},{10,8},{9,1... | collective-permute-start | bytes 4718600 | tf_op jit(solution)/shard_map/ppermute | solution.py:44
  138.6 36.6 %collective-permute-start.18 = (bf16[256,1536]{1,0:T(8,128)(2,1)S(1)}, bf16[256,1536]{1,0:T(8,128)(2,1)S(1)}, u32[]{:S(2)}, u32[]{:S(2)}) collective-permute-start(bf16[256,1536]{1,0:T(8,128)(2,1)S(1)} %copy-done.52), channel_id=1, source_target_pairs={{0,16},{16,0},{1,17},{17,1},{2,18},{18,2},{3,19},{19,3},{4,20},{20... | collective-permute-start | bytes 2359304 | tf_op jit(solution)/shard_map/ppermute | solution.py:44
  152.1 24.0 %collective-permute-start.20 = (bf16[512,2048]{1,0:T(8,128)(2,1)S(1)}, bf16[512,2048]{1,0:T(8,128)(2,1)S(1)}, u32[]{:S(2)}, u32[]{:S(2)}) collective-permute-start(bf16[512,2048]{1,0:T(8,128)(2,1)S(1)} %join.10.refs_0_), channel_id=1, source_target_pairs={{0,1},{1,0},{2,3},{3,2},{4,5},{5,4},{6,7},{7,6},{8,9},{9,8},{10,11... | collective-permute-start | bytes 6291464 | tf_op jit(solution)/shard_map/ppermute | solution.py:44
  157.0 23.9 %collective-permute-start.15 = (bf16[128,2048]{1,0:T(8,128)(2,1)S(1)}, bf16[128,2048]{1,0:T(8,128)(2,1)S(1)}, u32[]{:S(2)}, u32[]{:S(2)}) collective-permute-start(bf16[128,2048]{1,0:T(8,128)(2,1)S(1)} %get-tuple-element.185), channel_id=1, source_target_pairs={{0,4},{4,0},{1,5},{5,1},{2,6},{6,2},{3,7},{7,3},{8,12},{12,8},{9,1... | collective-permute-start | bytes 1572872 | tf_op jit(solution)/shard_map/ppermute | solution.py:44
  175.5 20.7 %collective-permute-start.26 = (bf16[512,768]{1,0:T(8,128)(2,1)}, bf16[512,768]{1,0:T(8,128)(2,1)S(1)}, u32[]{:S(2)}, u32[]{:S(2)}) collective-permute-start(bf16[512,768]{1,0:T(8,128)(2,1)} %bitcast.7), channel_id=1, source_target_pairs={{0,2},{2,0},{1,3},{3,1},{4,6},{6,4},{5,7},{7,5},{8,10},{10,8},{9,1... | collective-permute-start | bytes 2359304 | tf_op jit(solution)/shard_map/ppermute | solution.py:44
  190.3 21.7 %collective-permute-start.25 = (bf16[128,2048]{1,0:T(8,128)(2,1)S(1)}, bf16[128,2048]{1,0:T(8,128)(2,1)S(1)}, u32[]{:S(2)}, u32[]{:S(2)}) collective-permute-start(bf16[128,2048]{1,0:T(8,128)(2,1)S(1)} %get-tuple-element.119.refs_0_), channel_id=1, source_target_pairs={{0,8},{8,0},{1,9},{9,1},{2,10},{10,2},{3,11},{11,3},{4,12},{12,4},... | collective-permute-start | bytes 1572872 | tf_op jit(solution)/shard_map/ppermute | solution.py:44
  190.7 22.3 %collective-permute-start.21 = (bf16[256,1536]{1,0:T(8,128)(2,1)}, bf16[256,1536]{1,0:T(8,128)(2,1)S(1)}, u32[]{:S(2)}, u32[]{:S(2)}) collective-permute-start(bf16[256,1536]{1,0:T(8,128)(2,1)} %collective-permute-done.11), channel_id=1, source_target_pairs={{0,2},{2,0},{1,3},{3,1},{4,6},{6,4},{5,7},{7,5},{8,10},{10,8},{9,1... | collective-permute-start | bytes 2359304 | tf_op jit(solution)/shard_map/ppermute | solution.py:44
  191.2 37.7 %collective-permute-start.22 = (bf16[256,1536]{1,0:T(8,128)(2,1)S(1)}, bf16[256,1536]{1,0:T(8,128)(2,1)S(1)}, u32[]{:S(2)}, u32[]{:S(2)}) collective-permute-start(bf16[256,1536]{1,0:T(8,128)(2,1)S(1)} %collective-permute-done.18), channel_id=1, source_target_pairs={{0,2},{2,0},{1,3},{3,1},{4,6},{6,4},{5,7},{7,5},{8,10},{10,8},{9,1... | collective-permute-start | bytes 2359304 | tf_op jit(solution)/shard_map/ppermute | solution.py:44
  192.7 36.2 %collective-permute-start.23 = (bf16[512,768]{1,0:T(8,128)(2,1)}, bf16[512,768]{1,0:T(8,128)(2,1)S(1)}, u32[]{:S(2)}, u32[]{:S(2)}) collective-permute-start(bf16[512,768]{1,0:T(8,128)(2,1)} %bitcast.7), channel_id=1, source_target_pairs={{0,16},{16,0},{1,17},{17,1},{2,18},{18,2},{3,19},{19,3},{4,20},{20... | collective-permute-start | bytes 2359304 | tf_op jit(solution)/shard_map/ppermute | solution.py:44
  196.2 32.8 %collective-permute-start.24 = (bf16[128,2048]{1,0:T(8,128)(2,1)S(1)}, bf16[128,2048]{1,0:T(8,128)(2,1)S(1)}, u32[]{:S(2)}, u32[]{:S(2)}) collective-permute-start(bf16[128,2048]{1,0:T(8,128)(2,1)S(1)} %get-tuple-element.119.refs_0_), channel_id=1, source_target_pairs={{0,4},{4,0},{1,5},{5,1},{2,6},{6,2},{3,7},{7,3},{8,12},{12,8},{9,1... | collective-permute-start | bytes 1572872 | tf_op jit(solution)/shard_map/ppermute | solution.py:44
  266.8 24.6 %collective-permute-start.34 = (bf16[512,2048]{1,0:T(8,128)(2,1)S(1)}, bf16[512,2048]{1,0:T(8,128)(2,1)S(1)}, u32[]{:S(2)}, u32[]{:S(2)}) collective-permute-start(bf16[512,2048]{1,0:T(8,128)(2,1)S(1)} %convolution_convert_fusion.4), channel_id=1, source_target_pairs={{0,1},{1,0},{2,3},{3,2},{4,5},{5,4},{6,7},{7,6},{8,9},{9,8},{10,11... | collective-permute-start | bytes 6291464 | tf_op jit(solution)/shard_map/ppermute | solution.py:44
  266.8 20.4 %collective-permute-start.35 = (bf16[512,768]{1,0:T(8,128)(2,1)S(1)}, bf16[512,768]{1,0:T(8,128)(2,1)S(1)}, u32[]{:S(2)}, u32[]{:S(2)}) collective-permute-start(bf16[512,768]{1,0:T(8,128)(2,1)S(1)} %convolution_convert_fusion.7), channel_id=1, source_target_pairs={{0,2},{2,0},{1,3},{3,1},{4,6},{6,4},{5,7},{7,5},{8,10},{10,8},{9,1... | collective-permute-start | bytes 2359304 | tf_op jit(solution)/shard_map/ppermute | solution.py:44
  271.9 55.3 %collective-permute-start.41 = (bf16[512,1536]{1,0:T(8,128)(2,1)}, bf16[512,1536]{1,0:T(8,128)(2,1)}, u32[]{:S(2)}, u32[]{:S(2)}) collective-permute-start(bf16[512,1536]{1,0:T(8,128)(2,1)} %convolution_convert_fusion.3), channel_id=1, source_target_pairs={{0,2},{2,0},{1,3},{3,1},{4,6},{6,4},{5,7},{7,5},{8,10},{10,8},{9,1... | collective-permute-start | bytes 4718600 | tf_op jit(solution)/shard_map/ppermute | solution.py:44
  288.4 29.3 %collective-permute-start.38 = (bf16[256,768]{1,0:T(8,128)(2,1)S(1)}, bf16[256,768]{1,0:T(8,128)(2,1)S(1)}, u32[]{:S(2)}, u32[]{:S(2)}) collective-permute-start(bf16[256,768]{1,0:T(8,128)(2,1)S(1)} %get-tuple-element.191), channel_id=1, source_target_pairs={{0,16},{16,0},{1,17},{17,1},{2,18},{18,2},{3,19},{19,3},{4,20},{20... | collective-permute-start | bytes 1179656 | tf_op jit(solution)/shard_map/ppermute | solution.py:44
  290.3 34.6 %collective-permute-start.39 = (bf16[256,768]{1,0:T(8,128)(2,1)S(1)}, bf16[256,768]{1,0:T(8,128)(2,1)}, u32[]{:S(2)}, u32[]{:S(2)}) collective-permute-start(bf16[256,768]{1,0:T(8,128)(2,1)S(1)} %get-tuple-element.190), channel_id=1, source_target_pairs={{0,16},{16,0},{1,17},{17,1},{2,18},{18,2},{3,19},{19,3},{4,20},{20... | collective-permute-start | bytes 1179656 | tf_op jit(solution)/shard_map/ppermute | solution.py:44
  297.6 27.3 %collective-permute-start.37 = (bf16[128,2048]{1,0:T(8,128)(2,1)S(1)}, bf16[128,2048]{1,0:T(8,128)(2,1)S(1)}, u32[]{:S(2)}, u32[]{:S(2)}) collective-permute-start(bf16[128,2048]{1,0:T(8,128)(2,1)S(1)} %get-tuple-element.180), channel_id=1, source_target_pairs={{0,4},{4,0},{1,5},{5,1},{2,6},{6,2},{3,7},{7,3},{8,12},{12,8},{9,1... | collective-permute-start | bytes 1572872 | tf_op jit(solution)/shard_map/ppermute | solution.py:44
  303.0 77.3 %collective-permute-start.30 = (bf16[512,2048]{1,0:T(8,128)(2,1)}, bf16[512,2048]{1,0:T(8,128)(2,1)}, u32[]{:S(2)}, u32[]{:S(2)}) collective-permute-start(bf16[512,2048]{1,0:T(8,128)(2,1)} %convolution_convert_fusion.5), channel_id=1, source_target_pairs={{0,1},{1,0},{2,3},{3,2},{4,5},{5,4},{6,7},{7,6},{8,9},{9,8},{10,11... | collective-permute-start | bytes 6291464 | tf_op jit(solution)/shard_map/ppermute | solution.py:44
  326.3 35.3 %collective-permute-start.42 = (bf16[512,768]{1,0:T(8,128)(2,1)S(1)}, bf16[512,768]{1,0:T(8,128)(2,1)S(1)}, u32[]{:S(2)}, u32[]{:S(2)}) collective-permute-start(bf16[512,768]{1,0:T(8,128)(2,1)S(1)} %convolution_convert_fusion.6), channel_id=1, source_target_pairs={{0,2},{2,0},{1,3},{3,1},{4,6},{6,4},{5,7},{7,5},{8,10},{10,8},{9,1... | collective-permute-start | bytes 2359304 | tf_op jit(solution)/shard_map/ppermute | solution.py:44
  340.2 21.1 %collective-permute-start.45 = (bf16[128,2048]{1,0:T(8,128)(2,1)}, bf16[128,2048]{1,0:T(8,128)(2,1)}, u32[]{:S(2)}, u32[]{:S(2)}) collective-permute-start(bf16[128,2048]{1,0:T(8,128)(2,1)} %get-tuple-element.127.refs_0_), channel_id=1, source_target_pairs={{0,8},{8,0},{1,9},{9,1},{2,10},{10,2},{3,11},{11,3},{4,12},{12,4},... | collective-permute-start | bytes 1572872 | tf_op jit(solution)/shard_map/ppermute | solution.py:44
  341.7 35.6 %collective-permute-start.43 = (bf16[256,1536]{1,0:T(8,128)(2,1)}, bf16[256,1536]{1,0:T(8,128)(2,1)}, u32[]{:S(2)}, u32[]{:S(2)}) collective-permute-start(bf16[256,1536]{1,0:T(8,128)(2,1)} %get-tuple-element.187), channel_id=1, source_target_pairs={{0,16},{16,0},{1,17},{17,1},{2,18},{18,2},{3,19},{19,3},{4,20},{20... | collective-permute-start | bytes 2359304 | tf_op jit(solution)/shard_map/ppermute | solution.py:44
  343.7 33.6 %collective-permute-start.44 = (bf16[128,2048]{1,0:T(8,128)(2,1)}, bf16[128,2048]{1,0:T(8,128)(2,1)}, u32[]{:S(2)}, u32[]{:S(2)}) collective-permute-start(bf16[128,2048]{1,0:T(8,128)(2,1)} %get-tuple-element.127.refs_0_), channel_id=1, source_target_pairs={{0,4},{4,0},{1,5},{5,1},{2,6},{6,2},{3,7},{7,3},{8,12},{12,8},{9,1... | collective-permute-start | bytes 1572872 | tf_op jit(solution)/shard_map/ppermute | solution.py:44
  364.7 38.7 %all-to-all-start.3 = ((bf16[4,128,768]{2,1,0:T(8,128)(2,1)}), bf16[4,128,768]{2,1,0:T(8,128)(2,1)S(1)}, u32[]{:S(2)}, u32[]{:S(2)}) async-start(bf16[4,128,768]{2,1,0:T(8,128)(2,1)} %bitcast.52), calls=%async_computation.3 | async-start | bytes 1572864 | tf_op jit(solution)/shard_map/all_to_all | solution.py:271
  380.2 30.4 %collective-permute-start.47 = (bf16[512,2048]{1,0:T(8,128)(2,1)}, bf16[512,2048]{1,0:T(8,128)(2,1)}, u32[]{:S(2)}, u32[]{:S(2)}) collective-permute-start(bf16[512,2048]{1,0:T(8,128)(2,1)} %join.14.refs_0_), channel_id=1, source_target_pairs={{0,1},{1,0},{2,3},{3,2},{4,5},{5,4},{6,7},{7,6},{8,9},{9,8},{10,11... | collective-permute-start | bytes 6291464 | tf_op jit(solution)/shard_map/ppermute | solution.py:44
  389.9 39.9 %collective-permute-start.54 = (bf16[512,1536]{1,0:T(8,128)(2,1)}, bf16[512,1536]{1,0:T(8,128)(2,1)}, u32[]{:S(2)}, u32[]{:S(2)}) collective-permute-start(bf16[512,1536]{1,0:T(8,128)(2,1)} %convolution_convert_fusion.1), channel_id=1, source_target_pairs={{0,2},{2,0},{1,3},{3,1},{4,6},{6,4},{5,7},{7,5},{8,10},{10,8},{9,1... | collective-permute-start | bytes 4718600 | tf_op jit(solution)/shard_map/ppermute | solution.py:44
  401.1 24.1 %collective-permute-start.33 = (bf16[128,2048]{1,0:T(8,128)(2,1)}, bf16[128,2048]{1,0:T(8,128)(2,1)}, u32[]{:S(2)}, u32[]{:S(2)}) collective-permute-start(bf16[128,2048]{1,0:T(8,128)(2,1)} %get-tuple-element.174), channel_id=1, source_target_pairs={{0,8},{8,0},{1,9},{9,1},{2,10},{10,2},{3,11},{11,3},{4,12},{12,4},... | collective-permute-start | bytes 1572872 | tf_op jit(solution)/shard_map/ppermute | solution.py:44
  402.7 36.4 %collective-permute-start.51 = (bf16[256,1536]{1,0:T(8,128)(2,1)}, bf16[256,1536]{1,0:T(8,128)(2,1)}, u32[]{:S(2)}, u32[]{:S(2)}) collective-permute-start(bf16[256,1536]{1,0:T(8,128)(2,1)} %get-tuple-element.186), channel_id=1, source_target_pairs={{0,16},{16,0},{1,17},{17,1},{2,18},{18,2},{3,19},{19,3},{4,20},{20... | collective-permute-start | bytes 2359304 | tf_op jit(solution)/shard_map/ppermute | solution.py:44
  429.8 30.3 %collective-permute-start.48 = (bf16[512,2048]{1,0:T(8,128)(2,1)}, bf16[512,2048]{1,0:T(8,128)(2,1)}, u32[]{:S(2)}, u32[]{:S(2)}) collective-permute-start(bf16[512,2048]{1,0:T(8,128)(2,1)} %convolution_convert_fusion.2), channel_id=1, source_target_pairs={{0,1},{1,0},{2,3},{3,2},{4,5},{5,4},{6,7},{7,6},{8,9},{9,8},{10,11... | collective-permute-start | bytes 6291464 | tf_op jit(solution)/shard_map/ppermute | solution.py:44
  443.9 37.2 %all-to-all-start.6 = ((bf16[4,128,1536]{2,1,0:T(8,128)(2,1)}), bf16[4,128,1536]{2,1,0:T(8,128)(2,1)S(1)}, u32[]{:S(2)}, u32[]{:S(2)}) async-start(bf16[4,128,1536]{2,1,0:T(8,128)(2,1)} %bitcast.51), calls=%async_computation.6 | async-start | bytes 3145728 | tf_op jit(solution)/shard_map/all_to_all | solution.py:271
  453.2 24.7 %collective-permute-start.56 = (bf16[512,256]{1,0:T(8,128)(2,1)S(1)}, bf16[512,256]{1,0:T(8,128)(2,1)S(1)}, u32[]{:S(2)}, u32[]{:S(2)}) collective-permute-start(bf16[512,256]{1,0:T(8,128)(2,1)S(1)} %convolution_convert_fusion.11), channel_id=1, source_target_pairs={{0,2},{2,0},{1,3},{3,1},{4,6},{6,4},{5,7},{7,5},{8,10},{10,8},{9,1... | collective-permute-start | bytes 786440 | tf_op jit(solution)/shard_map/ppermute | solution.py:44
  454.5 21.2 %collective-permute-start.52 = (bf16[512,512]{1,0:T(8,128)(2,1)S(1)}, bf16[512,512]{1,0:T(8,128)(2,1)S(1)}, u32[]{:S(2)}, u32[]{:S(2)}) collective-permute-start(bf16[512,512]{1,0:T(8,128)(2,1)S(1)} %convolution_convert_fusion.9), channel_id=1, source_target_pairs={{0,2},{2,0},{1,3},{3,1},{4,6},{6,4},{5,7},{7,5},{8,10},{10,8},{9,1... | collective-permute-start | bytes 1572872 | tf_op jit(solution)/shard_map/ppermute | solution.py:44
  457.7 32.0 %collective-permute-start.58 = (bf16[512,512]{1,0:T(8,128)(2,1)}, bf16[512,512]{1,0:T(8,128)(2,1)}, u32[]{:S(2)}, u32[]{:S(2)}) collective-permute-start(bf16[512,512]{1,0:T(8,128)(2,1)} %convolution_convert_fusion.8), channel_id=1, source_target_pairs={{0,2},{2,0},{1,3},{3,1},{4,6},{6,4},{5,7},{7,5},{8,10},{10,8},{9,1... | collective-permute-start | bytes 1572872 | tf_op jit(solution)/shard_map/ppermute | solution.py:44
  477.3 21.2 %collective-permute-start.59 = (bf16[512,512]{1,0:T(8,128)(2,1)}, bf16[512,512]{1,0:T(8,128)(2,1)}, u32[]{:S(2)}, u32[]{:S(2)}) collective-permute-start(bf16[512,512]{1,0:T(8,128)(2,1)} %fusion.8), channel_id=1, source_target_pairs={{0,16},{16,0},{1,17},{17,1},{2,18},{18,2},{3,19},{19,3},{4,20},{20... | collective-permute-start | bytes 1572872 | tf_op jit(solution)/shard_map/ppermute | solution.py:44
  479.1 36.7 %collective-permute-start.49 = (bf16[128,2048]{1,0:T(8,128)(2,1)}, bf16[128,2048]{1,0:T(8,128)(2,1)}, u32[]{:S(2)}, u32[]{:S(2)}) collective-permute-start(bf16[128,2048]{1,0:T(8,128)(2,1)} %get-tuple-element.179), channel_id=1, source_target_pairs={{0,4},{4,0},{1,5},{5,1},{2,6},{6,2},{3,7},{7,3},{8,12},{12,8},{9,1... | collective-permute-start | bytes 1572872 | tf_op jit(solution)/shard_map/ppermute | solution.py:44
  481.1 20.5 %all-to-all-start.5 = ((bf16[4,128,256]{2,1,0:T(8,128)(2,1)}), bf16[4,128,256]{2,1,0:T(8,128)(2,1)S(1)}, u32[]{:S(2)}, u32[]{:S(2)}) async-start(bf16[4,128,256]{2,1,0:T(8,128)(2,1)} %bitcast.54), calls=%async_computation.5 | async-start | bytes 524288 | tf_op jit(solution)/shard_map/all_to_all | solution.py:271
  487.6 28.1 %collective-permute-start.53 = (bf16[128,2048]{1,0:T(8,128)(2,1)}, bf16[128,2048]{1,0:T(8,128)(2,1)}, u32[]{:S(2)}, u32[]{:S(2)}) collective-permute-start(bf16[128,2048]{1,0:T(8,128)(2,1)} %get-tuple-element.170), channel_id=1, source_target_pairs={{0,8},{8,0},{1,9},{9,1},{2,10},{10,2},{3,11},{11,3},{4,12},{12,4},... | collective-permute-start | bytes 1572872 | tf_op jit(solution)/shard_map/ppermute | solution.py:44
  501.6 33.3 %all-to-all-start.4 = ((bf16[4,128,512]{2,1,0:T(8,128)(2,1)}), bf16[4,128,512]{2,1,0:T(8,128)(2,1)}, u32[]{:S(2)}, u32[]{:S(2)}) async-start(bf16[4,128,512]{2,1,0:T(8,128)(2,1)} %bitcast.53), calls=%async_computation.4 | async-start | bytes 1048576 | tf_op jit(solution)/shard_map/all_to_all | solution.py:271
  (104 other events, 1478.1 us)
